TPU v7x, 32 devices: a whole 2x2x4 slice. The times are simulated.
32 devices in a mesh: dp: 16 (over z, x, core), fsdp: 2 (over y).
Axes of the slice: x: 2, y: 2, z: 4, core: 2. Of those that a mesh axis runs over, the one named last changes fastest.
Arguments:
- tokens: bfloat16 [32, 512, 1024], P(('dp', 'fsdp')), may hold values from -6 to 6
- memory: bfloat16 [32, 512, 1024], P(('dp', 'fsdp')), may hold values from -6 to 6
- compressed: bfloat16 [32, 512, 1024], P(('dp', 'fsdp')), may hold values from -6 to 6
- cotangent: bfloat16 [32, 512, 1024], P(('dp', 'fsdp')), may hold values from -6 to 6
- seg_len: int32 [32], P(('dp', 'fsdp')), may hold values from 128 to 512, as said below
- mem_fill: int32 [32], P(('dp', 'fsdp')), may hold values from 0 to 512
- cmem_fill: int32 [32], P(('dp', 'fsdp')), may hold values from 0 to 512
- w_qkv: bfloat16 [3, 1024, 1024], P(None, 'fsdp'), may hold values from -0.1875 to 0.1875
- w_rel: bfloat16 [1024, 1024], P('fsdp'), may hold values from -0.1875 to 0.1875
- w_out: bfloat16 [1024, 1024], P('fsdp'), may hold values from -0.75 to 0.75
- w_up: bfloat16 [1024, 4096], P('fsdp'), may hold values from -0.1875 to 0.1875
- w_down: bfloat16 [4096, 1024], P('fsdp'), may hold values from -0.09375 to 0.09375
- w_comp: bfloat16 [3, 1024, 1024], P(None, 'fsdp'), may hold values from -0.109375 to 0.109375
- norm_gain1: float32 [1024], replicated, may hold values from 0.5 to 1.5
- norm_gain2: float32 [1024], replicated, may hold values from 0.5 to 1.5
- bias_content: float32 [1024], replicated, may hold values from -3 to 3
- bias_position: float32 [1024], replicated, may hold values from -3 to 3
- bias_up: float32 [4096], replicated, may hold values from -3 to 3
Outputs:
- output: bfloat16 [32, 512, 1024], P(('dp', 'fsdp'))
- grad_tokens: bfloat16 [32, 512, 1024], P(('dp', 'fsdp'))
- new_memory: bfloat16 [32, 512, 1024], P(('dp', 'fsdp'))
- new_compressed: bfloat16 [32, 512, 1024], P(('dp', 'fsdp'))
- grad_qkv: float32 [3, 1024, 1024], P(None, 'fsdp', 'dp')
- grad_rel: float32 [1024, 1024], P('fsdp', 'dp')
- grad_out: float32 [1024, 1024], P('fsdp', 'dp')
- grad_up: float32 [1024, 4096], P('fsdp', 'dp')
- grad_down: float32 [4096, 1024], P('fsdp', 'dp')
- grad_comp: float32 [3, 1024, 1024], P(None, 'fsdp', 'dp')
- grad_gain1: float32 [1024], P(('dp', 'fsdp'))
- grad_gain2: float32 [1024], P(('dp', 'fsdp'))
- grad_content: float32 [1024], P(('dp', 'fsdp'))
- grad_position: float32 [1024], P(('dp', 'fsdp'))
- grad_bias_up: float32 [4096], P(('dp', 'fsdp'))
Inputs may be any that keep to these rules, and one draw needn't show every extreme that they name: Each stream's segment length is 128, 256 or 512; rows from seg_len on are padding.
All inputs are finite; a program needn't handle non-finite values.
Results may differ from a plain program's by a relative error of at most 0.019.
Values may be sent and summed in bfloat16 or wider, within the bound.
No kernel may reach another device: no remote copies, remote signals or barrier semaphores. Data moves between devices by JAX's collectives and lax.ppermute only.
A program may use at most 320 MiB of HBM per device.

v0:
```python
import math

import jax
import jax.numpy as jnp
from jax import lax
from jax.sharding import PartitionSpec as P

H = 8


def layer_norm(row_block, norm_gain):
    row_mean = jnp.mean(row_block, axis=-1, keepdims=True)
    centred = row_block - row_mean
    spread = jnp.mean(centred * centred, axis=-1, keepdims=True)
    return centred * lax.rsqrt(spread + 1e-05) * norm_gain


def sinusoid(table_rows, table_width):
    distance = (table_rows - 1 - jnp.arange(table_rows)).astype(jnp.float32)
    frequency = jnp.exp(
        jnp.arange(0, table_width, 2).astype(jnp.float32) * (-math.log(10000.0) / table_width)
    )
    angles = distance[:, None] * frequency[None, :]
    return jnp.concatenate([jnp.sin(angles), jnp.cos(angles)], axis=1)


def rel_shift(scores):
    head_count, query_count, key_count = scores.shape
    padded = jnp.pad(scores, ((0, 0), (0, 0), (1, 0)))
    padded = padded.reshape(head_count, key_count + 1, query_count)[:, 1:]
    return padded.reshape(head_count, query_count, key_count)


def key_mask(query_count, comp_slots, mem_slots, mem_live, comp_live):
    row_index = jnp.arange(query_count)[:, None]
    col_index = jnp.arange(comp_slots + mem_slots + query_count)[None, :]
    seg_start = comp_slots + mem_slots
    live_comp = (col_index < comp_slots) & (col_index >= comp_slots - comp_live)
    live_mem = (
        (col_index >= comp_slots) & (col_index < seg_start) & (col_index >= seg_start - mem_live)
    )
    live_seg = (col_index >= seg_start) & (col_index - seg_start <= row_index)
    return live_comp | live_mem | live_seg


def attention_probs(scores, key_live):
    masked = jnp.where(key_live, scores, -1e30)
    top_score = jnp.max(masked, axis=-1, keepdims=True)
    weights = jnp.exp(masked - top_score)
    total = jnp.sum(weights, axis=-1, keepdims=True)
    return (weights / total, top_score + jnp.log(total))


def softmax_back(probs, grad_probs):
    return probs * (grad_probs - jnp.sum(grad_probs * probs, axis=-1, keepdims=True))


def score_block(query_content, query_position, key_heads, position):
    content = jnp.einsum(
        "qhd,khd->hqk", query_content, key_heads, preferred_element_type=jnp.float32
    )
    relative = jnp.einsum(
        "qhd,khd->hqk", query_position, position, preferred_element_type=jnp.float32
    )
    return content + rel_shift(relative)


def body(
    tokens,
    memory,
    compressed,
    cotangent,
    seg_len,
    mem_fill,
    cmem_fill,
    w_qkv,
    w_rel,
    w_out,
    w_up,
    w_down,
    w_comp,
    norm_gain1,
    norm_gain2,
    bias_content,
    bias_position,
    bias_up,
):
    streams, seg_rows, model_width = tokens.shape
    mem_rows = memory.shape[1]
    comp_rows = compressed.shape[1]
    seg_start = comp_rows + mem_rows
    key_rows = seg_start + seg_rows
    head_size = model_width // H
    squeeze_rows = mem_rows // 3
    query_scale = head_size ** (-0.5)
    gathered = (
        lax.all_gather(w_qkv, "fsdp", axis=1, tiled=True),
        lax.all_gather(w_rel, "fsdp", axis=0, tiled=True),
        lax.all_gather(w_out, "fsdp", axis=0, tiled=True),
        lax.all_gather(w_up, "fsdp", axis=0, tiled=True),
        lax.all_gather(w_down, "fsdp", axis=0, tiled=True),
        lax.all_gather(w_comp, "fsdp", axis=1, tiled=True),
    )
    sinus_table = sinusoid(key_rows, model_width).astype(jnp.bfloat16)
    position = (
        jnp.dot(sinus_table, gathered[1], preferred_element_type=jnp.float32)
        .astype(jnp.bfloat16)
        .reshape(key_rows, H, head_size)
    )

    def forward_step(counter, stream_items):
        current, recent, distant, seg_length, mem_live, comp_live = stream_items
        qkv_full, rel_full, out_full, up_full, down_full, comp_full = gathered
        hidden = jnp.concatenate([distant, recent, current], axis=0).astype(jnp.float32)
        normed = layer_norm(hidden, norm_gain1).astype(jnp.bfloat16)
        queries = jnp.dot(normed[seg_start:], qkv_full[0], preferred_element_type=jnp.float32)
        key_heads = (
            jnp.dot(normed, qkv_full[1], preferred_element_type=jnp.float32)
            .astype(jnp.bfloat16)
            .reshape(key_rows, H, head_size)
        )
        value_heads = (
            jnp.dot(normed, qkv_full[2], preferred_element_type=jnp.float32)
            .astype(jnp.bfloat16)
            .reshape(key_rows, H, head_size)
        )
        query_content = (
            ((queries + bias_content) * query_scale)
            .astype(jnp.bfloat16)
            .reshape(seg_rows, H, head_size)
        )
        query_position = (
            ((queries + bias_position) * query_scale)
            .astype(jnp.bfloat16)
            .reshape(seg_rows, H, head_size)
        )
        key_live = key_mask(seg_rows, comp_rows, mem_rows, mem_live, comp_live)
        scores = score_block(query_content, query_position, key_heads, position)
        probs, log_total = attention_probs(scores, key_live)
        mixed_out = (
            jnp.einsum(
                "hqk,khd->qhd",
                probs.astype(jnp.bfloat16),
                value_heads,
                preferred_element_type=jnp.float32,
            )
            .reshape(seg_rows, model_width)
            .astype(jnp.bfloat16)
        )
        attended = current.astype(jnp.float32) + jnp.dot(
            mixed_out, out_full, preferred_element_type=jnp.float32
        )
        second = layer_norm(attended, norm_gain2).astype(jnp.bfloat16)
        ffn_inner = jnp.dot(second, up_full, preferred_element_type=jnp.float32) + bias_up
        output = attended + jnp.dot(
            jax.nn.gelu(ffn_inner).astype(jnp.bfloat16),
            down_full,
            preferred_element_type=jnp.float32,
        )
        groups = recent[: 3 * squeeze_rows].reshape(squeeze_rows, 3 * model_width)
        squeezed = jnp.dot(
            groups,
            comp_full.reshape(3 * model_width, model_width),
            preferred_element_type=jnp.float32,
        )
        new_mem = lax.dynamic_slice_in_dim(
            jnp.concatenate([recent, current], axis=0), seg_length, mem_rows, 0
        )
        new_comp = lax.dynamic_slice_in_dim(
            jnp.concatenate([distant, squeezed.astype(jnp.bfloat16)], axis=0),
            seg_length // 3,
            comp_rows,
            0,
        )
        probe_heads = (queries * query_scale).astype(jnp.bfloat16).reshape(seg_rows, H, head_size)
        residues = (
            normed,
            key_heads,
            value_heads,
            query_content,
            query_position,
            log_total,
            mixed_out,
            attended,
            ffn_inner,
            squeezed,
            probe_heads,
        )
        return (counter, (output.astype(jnp.bfloat16), new_mem, new_comp, residues))

    counter_start = jnp.zeros((), jnp.int32)
    _, (outputs, new_memory, new_compressed, residues) = lax.scan(
        forward_step, counter_start, (tokens, memory, compressed, seg_len, mem_fill, cmem_fill)
    )
    back_weights = (
        lax.all_gather(w_qkv, "fsdp", axis=1, tiled=True),
        lax.all_gather(w_rel, "fsdp", axis=0, tiled=True),
        lax.all_gather(w_out, "fsdp", axis=0, tiled=True),
        lax.all_gather(w_up, "fsdp", axis=0, tiled=True),
        lax.all_gather(w_down, "fsdp", axis=0, tiled=True),
        lax.all_gather(w_comp, "fsdp", axis=1, tiled=True),
    )

    def backward_step(totals, stream_items):
        current, recent, distant, cot_rows, seg_length, mem_live, comp_live, kept_rows = (
            stream_items
        )
        (
            normed,
            key_heads,
            value_heads,
            query_content,
            query_position,
            log_total,
            mixed_out,
            attended,
            ffn_inner,
            squeezed,
            probe_heads,
        ) = kept_rows
        qkv_full, rel_full, out_full, up_full, down_full, comp_full = back_weights
        row_live = jnp.arange(seg_rows) < seg_length
        grad_output = jnp.where(row_live[:, None], cot_rows, jnp.zeros_like(cot_rows))
        second = layer_norm(attended, norm_gain2).astype(jnp.bfloat16)
        activated, gelu_pull = jax.vjp(jax.nn.gelu, ffn_inner)
        activated = activated.astype(jnp.bfloat16)
        term_down = jnp.einsum(
            "qf,qd->fd", activated, grad_output, preferred_element_type=jnp.float32
        )
        grad_act = jnp.einsum(
            "qd,fd->qf", grad_output, down_full, preferred_element_type=jnp.float32
        )
        grad_inner = gelu_pull(grad_act)[0].astype(jnp.bfloat16)
        term_up = jnp.einsum("qd,qf->df", second, grad_inner, preferred_element_type=jnp.float32)
        term_bias_up = jnp.sum(grad_inner.astype(jnp.float32), axis=0)
        _, second_pull = jax.vjp(layer_norm, attended, norm_gain2)
        grad_second = jnp.einsum(
            "qf,df->qd", grad_inner, up_full, preferred_element_type=jnp.float32
        )
        grad_norm_rows, term_gain2 = second_pull(grad_second)
        grad_attended = grad_norm_rows + grad_output.astype(jnp.float32)
        grad_att = grad_attended.astype(jnp.bfloat16)
        term_out = jnp.einsum("qe,qd->ed", mixed_out, grad_att, preferred_element_type=jnp.float32)
        grad_mixed = (
            jnp.einsum("qd,ed->qe", grad_att, out_full, preferred_element_type=jnp.float32)
            .astype(jnp.bfloat16)
            .reshape(seg_rows, H, head_size)
        )
        key_live = key_mask(seg_rows, comp_rows, mem_rows, mem_live, comp_live)
        scores = score_block(query_content, query_position, key_heads, position)
        probs = jnp.exp(jnp.where(key_live, scores, -1e30) - log_total)
        grad_values = jnp.einsum(
            "hqk,qhd->khd",
            probs.astype(jnp.bfloat16),
            grad_mixed,
            preferred_element_type=jnp.float32,
        )
        grad_probs = jnp.einsum(
            "qhd,khd->hqk", grad_mixed, value_heads, preferred_element_type=jnp.float32
        )
        grad_scores = softmax_back(probs, grad_probs).astype(jnp.bfloat16)
        grad_qc = jnp.einsum(
            "hqk,khd->qhd", grad_scores, key_heads, preferred_element_type=jnp.float32
        )
        grad_keys = jnp.einsum(
            "hqk,qhd->khd", grad_scores, query_content, preferred_element_type=jnp.float32
        )
        _, shift_pull = jax.vjp(rel_shift, scores)
        grad_shifted = shift_pull(grad_scores.astype(jnp.float32))[0].astype(jnp.bfloat16)
        grad_qp = jnp.einsum(
            "hqk,khd->qhd", grad_shifted, position, preferred_element_type=jnp.float32
        )
        grad_pos = (
            jnp.einsum(
                "hqk,qhd->khd", grad_shifted, query_position, preferred_element_type=jnp.float32
            )
            .astype(jnp.bfloat16)
            .reshape(key_rows, model_width)
        )
        term_rel = jnp.einsum(
            "kd,ke->de", sinus_table, grad_pos, preferred_element_type=jnp.float32
        )
        term_content = (jnp.sum(grad_qc, axis=0) * query_scale).reshape(model_width)
        term_position = (jnp.sum(grad_qp, axis=0) * query_scale).reshape(model_width)
        grad_queries = (
            ((grad_qc + grad_qp) * query_scale).reshape(seg_rows, model_width).astype(jnp.bfloat16)
        )
        grad_keys_low = grad_keys.astype(jnp.bfloat16).reshape(key_rows, model_width)
        grad_values_low = grad_values.astype(jnp.bfloat16).reshape(key_rows, model_width)
        term_query = jnp.einsum(
            "qd,qe->de", normed[seg_start:], grad_queries, preferred_element_type=jnp.float32
        )
        term_key = jnp.einsum(
            "kd,ke->de", normed, grad_keys_low, preferred_element_type=jnp.float32
        )
        term_value = jnp.einsum(
            "kd,ke->de", normed, grad_values_low, preferred_element_type=jnp.float32
        )
        grad_normed = jnp.einsum(
            "ke,de->kd", grad_keys_low, qkv_full[1], preferred_element_type=jnp.float32
        )
        grad_normed = grad_normed + jnp.einsum(
            "ke,de->kd", grad_values_low, qkv_full[2], preferred_element_type=jnp.float32
        )
        grad_normed = grad_normed.at[seg_start:].add(
            jnp.einsum("qe,de->qd", grad_queries, qkv_full[0], preferred_element_type=jnp.float32)
        )
        hidden = jnp.concatenate([distant, recent, current], axis=0).astype(jnp.float32)
        _, first_pull = jax.vjp(layer_norm, hidden, norm_gain1)
        grad_hidden, term_gain1 = first_pull(grad_normed)
        grad_rows = (grad_attended + grad_hidden[seg_start:]).astype(jnp.bfloat16)
        comp_count = seg_length // 3
        old_keys = key_heads[comp_rows:seg_start]
        old_values = value_heads[comp_rows:seg_start]
        old_live = jnp.arange(mem_rows)[None, :] < 3 * comp_count
        old_probs, _ = attention_probs(
            jnp.einsum("qhd,khd->hqk", probe_heads, old_keys, preferred_element_type=jnp.float32),
            old_live,
        )
        old_out = jnp.einsum(
            "hqk,khd->qhd",
            old_probs.astype(jnp.bfloat16),
            old_values,
            preferred_element_type=jnp.float32,
        )

        def squeeze_norm(squeeze_block):
            return layer_norm(squeeze_block, norm_gain1)

        squeezed_norm, squeeze_pull = jax.vjp(squeeze_norm, squeezed)
        squeezed_low = squeezed_norm.astype(jnp.bfloat16)
        comp_keys = (
            jnp.dot(squeezed_low, qkv_full[1], preferred_element_type=jnp.float32)
            .astype(jnp.bfloat16)
            .reshape(squeeze_rows, H, head_size)
        )
        comp_values = (
            jnp.dot(squeezed_low, qkv_full[2], preferred_element_type=jnp.float32)
            .astype(jnp.bfloat16)
            .reshape(squeeze_rows, H, head_size)
        )
        squeeze_live = jnp.arange(squeeze_rows)[None, :] < comp_count
        comp_probs, _ = attention_probs(
            jnp.einsum("qhd,khd->hqk", probe_heads, comp_keys, preferred_element_type=jnp.float32),
            squeeze_live,
        )
        comp_probs_low = comp_probs.astype(jnp.bfloat16)
        comp_out = jnp.einsum(
            "hqk,khd->qhd", comp_probs_low, comp_values, preferred_element_type=jnp.float32
        )
        recon_gap = jnp.where(row_live[:, None, None], comp_out - old_out, 0.0)
        grad_comp_out = (recon_gap * (2.0 / seg_length.astype(jnp.float32))).astype(jnp.bfloat16)
        grad_comp_values = (
            jnp.einsum(
                "hqk,qhd->khd", comp_probs_low, grad_comp_out, preferred_element_type=jnp.float32
            )
            .astype(jnp.bfloat16)
            .reshape(squeeze_rows, model_width)
        )
        grad_comp_probs = jnp.einsum(
            "qhd,khd->hqk", grad_comp_out, comp_values, preferred_element_type=jnp.float32
        )
        grad_comp_scores = softmax_back(comp_probs, grad_comp_probs).astype(jnp.bfloat16)
        grad_comp_keys = (
            jnp.einsum(
                "hqk,qhd->khd", grad_comp_scores, probe_heads, preferred_element_type=jnp.float32
            )
            .astype(jnp.bfloat16)
            .reshape(squeeze_rows, model_width)
        )
        grad_squeeze_norm = jnp.einsum(
            "ge,de->gd", grad_comp_keys, qkv_full[1], preferred_element_type=jnp.float32
        )
        grad_squeeze_norm = grad_squeeze_norm + jnp.einsum(
            "ge,de->gd", grad_comp_values, qkv_full[2], preferred_element_type=jnp.float32
        )
        grad_squeezed = squeeze_pull(grad_squeeze_norm)[0].astype(jnp.bfloat16)
        groups = recent[: 3 * squeeze_rows].reshape(squeeze_rows, 3 * model_width)
        term_comp = jnp.einsum(
            "gt,gd->td", groups, grad_squeezed, preferred_element_type=jnp.float32
        ).reshape(3, model_width, model_width)
        term_qkv = jnp.stack([term_query, term_key, term_value], axis=0)
        terms = (
            term_qkv,
            term_rel,
            term_out,
            term_up,
            term_down,
            term_comp,
            term_gain1,
            term_gain2,
            term_content,
            term_position,
            term_bias_up,
        )
        return (jax.tree.map(jnp.add, totals, terms), grad_rows)

    zero_grads = tuple(
        (jnp.zeros(weight_full.shape, jnp.float32) for weight_full in back_weights)
    ) + (
        jnp.zeros(norm_gain1.shape, jnp.float32),
        jnp.zeros(norm_gain2.shape, jnp.float32),
        jnp.zeros(bias_content.shape, jnp.float32),
        jnp.zeros(bias_position.shape, jnp.float32),
        jnp.zeros(bias_up.shape, jnp.float32),
    )
    totals, grad_tokens = lax.scan(
        backward_step,
        zero_grads,
        (tokens, memory, compressed, cotangent, seg_len, mem_fill, cmem_fill, residues),
    )
    (
        sum_qkv,
        sum_rel,
        sum_out,
        sum_up,
        sum_down,
        sum_comp,
        sum_gain1,
        sum_gain2,
        sum_content,
        sum_position,
        sum_bias,
    ) = totals
    reduced = (
        lax.psum_scatter(sum_qkv, "dp", scatter_dimension=2, tiled=True),
        lax.psum_scatter(sum_rel, "dp", scatter_dimension=1, tiled=True),
        lax.psum_scatter(sum_out, "dp", scatter_dimension=1, tiled=True),
        lax.psum_scatter(sum_up, "dp", scatter_dimension=1, tiled=True),
        lax.psum_scatter(sum_down, "dp", scatter_dimension=1, tiled=True),
        lax.psum_scatter(sum_comp, "dp", scatter_dimension=2, tiled=True),
        lax.psum_scatter(sum_gain1, "dp", scatter_dimension=0, tiled=True),
        lax.psum_scatter(sum_gain2, "dp", scatter_dimension=0, tiled=True),
        lax.psum_scatter(sum_content, "dp", scatter_dimension=0, tiled=True),
        lax.psum_scatter(sum_position, "dp", scatter_dimension=0, tiled=True),
        lax.psum_scatter(sum_bias, "dp", scatter_dimension=0, tiled=True),
    )
    (
        part_qkv,
        part_rel,
        part_out,
        part_up,
        part_down,
        part_comp,
        part_gain1,
        part_gain2,
        part_content,
        part_position,
        part_bias,
    ) = reduced
    final = (
        lax.psum_scatter(
            part_qkv.astype(jnp.bfloat16), "fsdp", scatter_dimension=1, tiled=True
        ).astype(jnp.float32),
        lax.psum_scatter(
            part_rel.astype(jnp.bfloat16), "fsdp", scatter_dimension=0, tiled=True
        ).astype(jnp.float32),
        lax.psum_scatter(
            part_out.astype(jnp.bfloat16), "fsdp", scatter_dimension=0, tiled=True
        ).astype(jnp.float32),
        lax.psum_scatter(
            part_up.astype(jnp.bfloat16), "fsdp", scatter_dimension=0, tiled=True
        ).astype(jnp.float32),
        lax.psum_scatter(
            part_down.astype(jnp.bfloat16), "fsdp", scatter_dimension=0, tiled=True
        ).astype(jnp.float32),
        lax.psum_scatter(
            part_comp.astype(jnp.bfloat16), "fsdp", scatter_dimension=1, tiled=True
        ).astype(jnp.float32),
        lax.psum_scatter(
            part_gain1.astype(jnp.bfloat16), "fsdp", scatter_dimension=0, tiled=True
        ).astype(jnp.float32),
        lax.psum_scatter(
            part_gain2.astype(jnp.bfloat16), "fsdp", scatter_dimension=0, tiled=True
        ).astype(jnp.float32),
        lax.psum_scatter(
            part_content.astype(jnp.bfloat16), "fsdp", scatter_dimension=0, tiled=True
        ).astype(jnp.float32),
        lax.psum_scatter(
            part_position.astype(jnp.bfloat16), "fsdp", scatter_dimension=0, tiled=True
        ).astype(jnp.float32),
        lax.psum_scatter(
            part_bias.astype(jnp.bfloat16), "fsdp", scatter_dimension=0, tiled=True
        ).astype(jnp.float32),
    )
    return (outputs, grad_tokens, new_memory, new_compressed) + tuple(final)


def solution(mesh):
    return jax.shard_map(
        body,
        mesh=mesh,
        in_specs=(
            P(("dp", "fsdp"), None, None),
            P(("dp", "fsdp"), None, None),
            P(("dp", "fsdp"), None, None),
            P(("dp", "fsdp"), None, None),
            P(("dp", "fsdp")),
            P(("dp", "fsdp")),
            P(("dp", "fsdp")),
            P(None, "fsdp", None),
            P("fsdp", None),
            P("fsdp", None),
            P("fsdp", None),
            P("fsdp", None),
            P(None, "fsdp", None),
            P(),
            P(),
            P(),
            P(),
            P(),
        ),
        out_specs=(
            P(("dp", "fsdp"), None, None),
            P(("dp", "fsdp"), None, None),
            P(("dp", "fsdp"), None, None),
            P(("dp", "fsdp"), None, None),
            P(None, "fsdp", "dp"),
            P("fsdp", "dp"),
            P("fsdp", "dp"),
            P("fsdp", "dp"),
            P("fsdp", "dp"),
            P(None, "fsdp", "dp"),
            P(("dp", "fsdp")),
            P(("dp", "fsdp")),
            P(("dp", "fsdp")),
            P(("dp", "fsdp")),
            P(("dp", "fsdp")),
        ),
        check_vma=False,
    )
```

profile of v0, /device:TPU:0, one launch (start us, length us, event | category | flops | bytes accessed | tf_op | source)
XLA Modules:
  0.0 1747.8 jit_solution(8559379127509621143)
XLA Ops:
  22.8 13.0 fusion.41
  37.3 8.1 all-gather.9.cloned.1.call-done
  45.4 6.0 convolution_convert_fusion.1
  51.5 75.9 %all-gather.7.cloned.1.call-done = bf16[3,1024,1024]{2,1,0:T(8,128)(2,1)} async-done(((bf16[3,512,1024]{2,1,0:T(8,128)(2,1)}), bf16[3,1024,1024]{2,1,0:T(8,128)(2,1)}) %all-gather.7.cloned.1.call-update) | async-done | bytes 6291472 | tf_op jit(solution)/shard_map/all_gather | solution.py:97
  134.7 11.6 fusion.124
  146.4 21.1 %pad.21 = f32[8,512,1537]{2,1,0:T(8,128)} pad(f32[8,512,1536]{2,1,0:T(8,128)} %fusion.124, f32[]{:T(128)} %constant.215.clone.1), padding=0_0x0_0x1_0 | pad | bytes 50348036 | tf_op jit(solution)/shard_map/while/body/eval_jaxpr/jit(_pad)/pad | solution.py:29
  167.5 31.5 %reshape.388 = f32[8,1537,512]{2,1,0:T(8,128)} reshape(f32[8,512,1537]{2,1,0:T(8,128)} %pad.21) | data formatting | bytes 50364416 | tf_op jit(solution)/shard_map/while/body/eval_jaxpr/reshape | solution.py:30
  199.0 18.0 %slice.104 = f32[8,1536,512]{2,1,0:T(8,128)} slice(f32[8,1537,512]{2,1,0:T(8,128)} %reshape.388), slice={[0:8], [1:1537], [0:512]} | slice | bytes 50331648 | tf_op jit(solution)/shard_map/while/body/eval_jaxpr/slice | solution.py:30
  217.0 29.6 %reshape.389 = f32[8,512,1536]{2,1,0:T(8,128)} reshape(f32[8,1536,512]{2,1,0:T(8,128)} %slice.104) | data formatting | bytes 50331648 | tf_op jit(solution)/shard_map/while/body/eval_jaxpr/reshape | solution.py:31
  247.9 6.0 convolution_convert_fusion.2
  254.0 17.7 %fusion.117 = (f32[8,512]{1,0:T(8,128)S(1)}, f32[8,512,1536]{2,1,0:T(8,128)}) fusion(f32[8,512,1536]{2,1,0:T(8,128)} %reshape.389, bf16[512,8,128]{0,2,1:T(8,128)(2,1)} %bitcast.219, bf16[1536,8,128]{0,2,1:T(8,128)(2,1)S(1)} %bitcast.217, pred[512,1536]{1,0:T(8,128)(4,1)} %fusion.44), kind=kOutput, calls=%fused_computation.215 | convolution fusion | flops 1629483008 | bytes 55328768 | tf_op jit(solution)/shard_map/while/body/eval_jaxpr/qhd,khd->hqk/dot_general | solution.py:59
  271.7 13.3 fusion.2
  285.0 5.6 convolution_convert_fusion.3
  292.2 11.6 fusion.56
  307.6 10.7 fusion.113
  318.3 54.7 %all-gather.15.cloned.1.call-done = bf16[4096,1024]{1,0:T(8,128)(2,1)} async-done(((bf16[2048,1024]{1,0:T(8,128)(2,1)}), bf16[4096,1024]{1,0:T(8,128)(2,1)}) %all-gather.15.cloned.1.call-update) | async-done | bytes 8388624 | tf_op jit(solution)/shard_map/all_gather | solution.py:101
  373.0 14.0 convert_reduce_fusion
  387.0 5.4 multiply_reduce_fusion.2
  399.7 17.0 multiply_reduce_fusion
  416.7 21.7 %multiply_convert_fusion = bf16[8,512,1536]{2,1,0:T(8,128)(2,1)} fusion(f32[8,512,1536]{2,1,0:T(8,128)} %get-tuple-element.342, f32[8,512,1536]{2,1,0:T(8,128)} %get-tuple-element.337, f32[8,512]{1,0:T(8,128)S(1)} %get-tuple-element.341, f32[8,512]{1,0:T(8,128)S(1)} %log_add_fusion), kind=kLoop, calls=%fused_computation.2 | loop fusion | flops 25165824 | bytes 62947328 | tf_op jit(solution)/shard_map/while/body/eval_jaxpr/convert_element_type | solution.py:261
  438.4 19.5 %reshape.393 = bf16[8,1536,512]{2,1,0:T(8,128)(2,1)} reshape(bf16[8,512,1536]{2,1,0:T(8,128)(2,1)} %multiply_convert_fusion) | data formatting | bytes 25165824 | tf_op jit(solution)/shard_map/while/body/eval_jaxpr/transpose(jvp())/reshape | solution.py:31
  457.9 11.5 pad.22
  469.4 29.9 %reshape.394 = bf16[8,512,1537]{2,1,0:T(8,128)(2,1)} reshape(bf16[8,1537,512]{2,1,0:T(8,128)(2,1)} %pad.22) | data formatting | bytes 25182208 | tf_op jit(solution)/shard_map/while/body/eval_jaxpr/transpose(jvp())/reshape | solution.py:30
  499.4 9.1 fusion.38
  519.4 11.1 fusion.112
  537.2 14.1 fusion.110
  578.0 6.5 convolution_bitcast_fusion
  584.5 12.8 copy.134
  597.3 19.0 %copy.135 = f32[3,1024,1024]{1,0,2:T(4,128)} copy(f32[3,1024,1024]{2,1,0:T(8,128)} %bitcast.208) | data formatting | bytes 25165824 | tf_op jit(solution)/shard_map/while/body/eval_jaxpr/reshape | solution.py:381
  616.2 10.5 fusion.125
  626.8 12.6 bitcast_reduce_fusion
  643.7 6.7 convolution_convert_fusion
  650.4 12.8 fusion.35
  663.2 6.4 convolution_bitcast_fusion.1
  673.2 7.0 pad_maximum_fusion
  680.2 19.4 %copy.120 = f32[3,1024,1024]{1,0,2:T(4,128)} copy(f32[3,1024,1024]{2,1,0:T(8,128)} %pad_maximum_fusion) | data formatting | bytes 25165824 | tf_op jit(solution)/shard_map/while/body/eval_jaxpr/stack | solution.py:382
  713.6 5.6 fusion.27
  720.5 792.2 %all-reduce.17 = (bf16[3,1024,1024]{1,0,2:T(4,128)(2,1)}, bf16[3,1024,1024]{1,0,2:T(4,128)(2,1)}, bf16[1024]{0:T(1024)(128)(2,1)}, bf16[1024]{0:T(1024)(128)(2,1...) all-reduce(f32[3,1024,1024]{1,0,2:T(4,128)} %copy.120, ...), channel_id=2, replica_groups=mesh['dp'=16,'fsdp'=2] {'dp'}, use_global_device_ids=true, to_apply=%region_11.12.clone | all-reduce | flops 6299648 | bytes 37797888
  1514.7 27.5 %copy.147 = bf16[3,1024,64]{0,2,1:T(8,128)(2,1)} copy(bf16[3,1024,64]{1,0,2:T(4,128)(2,1)} %dynamic-slice_convert_fusion.1) | data formatting | bytes 786432
  1542.2 25.6 %reshape.403 = bf16[1024,192]{1,0:T(8,128)(2,1)} reshape(bf16[1024,64,3]{2,1,0:T(8,128)(2,1)} %bitcast.193) | data formatting | bytes 786432
  1569.8 27.5 %copy.149 = bf16[3,1024,64]{0,2,1:T(8,128)(2,1)} copy(bf16[3,1024,64]{1,0,2:T(4,128)(2,1)} %dynamic-slice_convert_fusion) | data formatting | bytes 786432
  1597.3 25.6 %reshape.405 = bf16[1024,192]{1,0:T(8,128)(2,1)} reshape(bf16[1024,64,3]{2,1,0:T(8,128)(2,1)} %bitcast.194) | data formatting | bytes 786432
  1635.7 13.0 fusion.61
  1648.7 8.4 fusion.115
  1674.8 19.9 %reshape.404 = bf16[512,64,3]{2,1,0:T(8,128)(2,1)} reshape(bf16[512,192]{1,0:T(8,128)(2,1)} %reduce-scatter.31.cloned.1.call-done) | data formatting | bytes 393216
  1694.8 9.0 copy.148
  1704.5 19.9 %reshape.406 = bf16[512,64,3]{2,1,0:T(8,128)(2,1)} reshape(bf16[512,192]{1,0:T(8,128)(2,1)} %reduce-scatter.33.cloned.1.call-done) | data formatting | bytes 393216
  1724.5 9.0 copy.150
  (275 shorter events, 143.0 us)
Async XLA Ops:
  7.2 38.2 %all-gather.9.cloned.1.call-start = ((), (), s32[]{:S(2)}) async-start(), calls=%async_computation.11 | async-start | bytes 3145728 | tf_op jit(solution)/shard_map/all_gather | solution.py:98
  7.9 119.5 %all-gather.7.cloned.1.call-start = ((), (), s32[]{:S(2)}) async-start(), calls=%async_computation.10 | async-start | bytes 9437184 | tf_op jit(solution)/shard_map/all_gather | solution.py:97
  8.7 295.2 %all-gather.11.cloned.1.call-start = ((), (), s32[]{:S(2)}) async-start(), calls=%async_computation.12 | async-start | bytes 3145728 | tf_op jit(solution)/shard_map/all_gather | solution.py:99
  9.4 298.2 %all-gather.13.cloned.1.call-start = ((), (), s32[]{:S(2)}) async-start(), calls=%async_computation.13 | async-start | bytes 12582912 | tf_op jit(solution)/shard_map/all_gather | solution.py:100
  10.0 363.0 %all-gather.15.cloned.1.call-start = ((), (), s32[]{:S(2)}) async-start(), calls=%async_computation.14 | async-start | bytes 12582912 | tf_op jit(solution)/shard_map/all_gather | solution.py:101
  10.6 8.0 copy-start.43
  10.6 540.9 %all-gather.17.cloned.1.call-start = ((), (), s32[]{:S(2)}) async-start(), calls=%async_computation.15 | async-start | bytes 9437184 | tf_op jit(solution)/shard_map/all_gather | solution.py:102
  11.2 1611.8 %reduce-scatter.15.cloned.1.call-start = ((), (), s32[]{:S(2)}) async-start(), calls=%async_computation.16 | async-start | bytes 4456448 | tf_op jit(solution)/shard_map/reduce_scatter | solution.py:427
  12.4 10.3 copy-start.37
  16.0 19.7 %copy-start.39 = (f32[1536]{0:T(1024)}, f32[1536]{0:T(1024)S(1)}, u32[]{:S(2)}) copy-start(f32[1536]{0:T(1024)S(1)} %fusion.103) | copy-start | bytes 18436
  45.4 82.0 %copy-start.56 = (f32[1024]{0:T(1024)S(1)}, f32[1024]{0:T(1024)}, u32[]{:S(2)}) copy-start(f32[1024]{0:T(1024)} %param.36) | copy-start | bytes 12292
  45.4 82.0 %copy-start.57 = (f32[1024]{0:T(1024)S(1)}, f32[1024]{0:T(1024)}, u32[]{:S(2)}) copy-start(f32[1024]{0:T(1024)} %param.35) | copy-start | bytes 12292
  51.5 83.3 %copy-start.16 = (bf16[1536,1024]{0,1:T(8,128)(2,1)}, bf16[1536,1024]{0,1:T(8,128)(2,1)S(1)}, u32[]{:S(2)}) copy-start(bf16[1536,1024]{0,1:T(8,128)(2,1)S(1)} %convolution_convert_fusion.1) | copy-start | bytes 9437188
  217.0 29.6 %copy-start.32 = (bf16[512,1024]{1,0:T(8,128)(2,1)S(1)}, bf16[512,1024]{1,0:T(8,128)(2,1)}, u32[]{:S(2)}) copy-start(bf16[512,1024]{1,0:T(8,128)(2,1)} %get-tuple-element.332) | copy-start | bytes 3145732
  254.0 17.7 %copy-start.11 = (bf16[1536,1024]{0,1:T(8,128)(2,1)}, bf16[1536,1024]{0,1:T(8,128)(2,1)S(1)}, u32[]{:S(2)}) copy-start(bf16[1536,1024]{0,1:T(8,128)(2,1)S(1)} %convolution_convert_fusion.2) | copy-start | bytes 9437188
  271.6 13.3 copy-start.24
  284.9 131.8 %copy-start.35 = (f32[8,512]{1,0:T(8,128)}, f32[8,512]{1,0:T(8,128)S(1)}, u32[]{:S(2)}) copy-start(f32[8,512]{1,0:T(8,128)S(1)} %log_add_fusion) | copy-start | bytes 49156
  292.2 11.6 copy-start.4
  307.2 212.2 %copy-start.9 = (f32[512,1024]{1,0:T(8,128)}, f32[512,1024]{1,0:T(8,128)S(1)}, u32[]{:S(2)}) copy-start(f32[512,1024]{1,0:T(8,128)S(1)} %get-tuple-element.339) | copy-start | bytes 6291460
  307.5 65.5 %copy-start.21 = (bf16[1,512,1024]{2,1,0:T(8,128)(2,1)S(1)}, bf16[1,512,1024]{2,1,0:T(8,128)(2,1)}, u32[]{:S(2)}) copy-start(bf16[1,512,1024]{2,1,0:T(8,128)(2,1)} %param.23) | copy-start | bytes 3145732
  307.5 65.5 %copy-start.51 = (pred[512]{0:T(512)(128)(4,1)S(1)}, pred[512]{0:T(512)(128)(4,1)}, u32[]{:S(2)}) copy-start(pred[512]{0:T(512)(128)(4,1)} %iota_compare_fusion.8) | copy-start | bytes 1540
  307.5 65.5 %copy-start.54 = (f32[4096]{0:T(1024)S(1)}, f32[4096]{0:T(1024)}, u32[]{:S(2)}) copy-start(f32[4096]{0:T(1024)} %param.37) | copy-start | bytes 49156
  373.0 14.0 copy-start.53
  399.7 17.0 copy-start.14
  469.4 29.9 %copy-start.17 = (bf16[512,1024]{0,1:T(8,128)(2,1)S(1)}, bf16[512,1024]{0,1:T(8,128)(2,1)}, u32[]{:S(2)}) copy-start(bf16[512,1024]{0,1:T(8,128)(2,1)} %copy.152) | copy-start | bytes 3145732
  499.3 9.1 copy-start.29
  499.4 9.1 copy-start.30
  513.7 1111.1 %reduce-scatter.19.cloned.1.call-start = ((), (), s32[]{:S(2)}) async-start(), calls=%async_computation.18 | async-start | bytes 4456448 | tf_op jit(solution)/shard_map/reduce_scatter | solution.py:428
  519.3 1113.9 %reduce-scatter.23.cloned.1.call-start = ((), (), s32[]{:S(2)}) async-start(), calls=%async_computation.20 | async-start | bytes 17825792 | tf_op jit(solution)/shard_map/reduce_scatter | solution.py:429
  530.5 6.7 copy-start.22
  530.5 1126.6 %reduce-scatter.27.cloned.1.call-start = ((), (), s32[]{:S(2)}) async-start(), calls=%async_computation.22 | async-start | bytes 17825792 | tf_op jit(solution)/shard_map/reduce_scatter | solution.py:430
  551.3 1123.5 %reduce-scatter.31.cloned.1.call-start = ((), (), s32[]{:S(2)}) async-start(), calls=%async_computation.24 | async-start | bytes 786432
  597.3 19.0 %copy-start.12 = (bf16[1536,1024]{0,1:T(8,128)(2,1)S(1)}, bf16[1536,1024]{0,1:T(8,128)(2,1)}, u32[]{:S(2)}) copy-start(bf16[1536,1024]{0,1:T(8,128)(2,1)} %copy-done.11) | copy-start | bytes 9437188
  626.8 13.6 copy-start.25
  643.7 6.7 copy-start.15
  643.7 6.7 copy-start.36
  663.2 6.5 copy-start.26
  713.6 6.9 copy-start.47
  1567.8 136.8 %reduce-scatter.33.cloned.1.call-start = ((), (), s32[]{:S(2)}) async-start(), calls=%async_computation.25 | async-start | bytes 786432
  1597.3 29.8 %copy-start.60 = (u32[32]{0:T(128)S(1)}, u32[32]{0:T(128)}, u32[]{:S(2)}) copy-start(u32[32]{0:T(128)} %constant.268) | copy-start | bytes 388
  1622.9 111.3 %reduce-scatter.17.cloned.1.call-start = ((), (), s32[]{:S(2)}) async-start(), calls=%async_computation.17 | async-start | bytes 196608 | tf_op jit(solution)/shard_map/reduce_scatter | solution.py:455
  1624.6 11.1 copy-start.55
  1624.7 111.1 %reduce-scatter.21.cloned.1.call-start = ((), (), s32[]{:S(2)}) async-start(), calls=%async_computation.19 | async-start | bytes 196608 | tf_op jit(solution)/shard_map/reduce_scatter | solution.py:458
  1626.4 110.9 %reduce-scatter.25.cloned.1.call-start = ((), (), s32[]{:S(2)}) async-start(), calls=%async_computation.21 | async-start | bytes 786432 | tf_op jit(solution)/shard_map/reduce_scatter | solution.py:461
  1635.4 13.3 copy-start.42
  1635.4 103.6 %reduce-scatter.29.cloned.1.call-start = ((), (), s32[]{:S(2)}) async-start(), calls=%async_computation.23 | async-start | bytes 786432 | tf_op jit(solution)/shard_map/reduce_scatter | solution.py:464
  1648.7 22.2 %copy-start.46 = (f32[512]{0:T(512)S(1)}, f32[512]{0:T(512)}, u32[]{:S(2)}) copy-start(f32[512]{0:T(512)} %copy-done.45) | copy-start | bytes 6148
  1648.7 22.2 %copy-start.52 = (pred[512]{0:T(512)(128)(4,1)S(1)}, pred[512]{0:T(512)(128)(4,1)}, u32[]{:S(2)}) copy-start(pred[512]{0:T(512)(128)(4,1)} %iota_compare_fusion.8) | copy-start | bytes 1540
  (33 other events, 98.5 us)
Sparse Core Ops, SparseCore 0:
  9.6 35.8 all-gather.8
  47.0 80.3 all-gather.6
  128.9 33.1 all-gather.10
  163.5 103.9 all-gather.12
  268.9 104.0 all-gather.14
  374.4 80.3 all-gather.16
  513.8 72.4 reduce-scatter.14
  590.6 71.4 reduce-scatter.18
  666.2 279.1 reduce-scatter.22
  949.4 280.5 reduce-scatter.26
  1567.9 25.1 reduce-scatter.30
  1623.0 25.1 reduce-scatter.32
  1651.0 10.2 reduce-scatter.16
  1663.4 10.2 reduce-scatter.20
  1676.3 14.5 reduce-scatter.24
  1693.1 14.5 reduce-scatter.28
where the time goes:
time: 1770 us; the launch traced here: 1750 us
  blocking collectives  797 us (45%)
  local copies, waits for them, and re-layouts  407 us (23%)
  matrix products  265 us (15%)
  waiting for transfers between devices  143 us (8%)
  other arithmetic  114 us (6%)
  between operations  20.1 us (1%)
    unnamed x2, blocking collectives  797 us
    unnamed x153, local copies, waits for them, and re-layouts  182 us
    all_gather x1, waiting for transfers between devices, body(): lax.all_gather(w_qkv, 'fsdp', axis=1, tiled=True)  75.9 us
    reshape x2, local copies, waits for them, and re-layouts, rel_shift(): padded = padded.reshape(head_count, key_count + 1, query_count)[:, 1:]  61.5 us
    all_gather x1, waiting for transfers between devices, body(): lax.all_gather(w_down, 'fsdp', axis=0, tiled=True)  54.7 us
    reshape x2, local copies, waits for them, and re-layouts, rel_shift(): return padded.reshape(head_count, query_count, key_count)  49.1 us
  transfers between devices with their start and end apart: 16, of which 3 were waited for; matrix products, arithmetic and copies ran while one was open for 44% of the time, Pallas kernels for 0%

commit v1 on v0

v1 whole, which is shorter than its diff:
```python
import functools
import math

import jax
import jax.numpy as jnp
from jax import lax
from jax.experimental import pallas as pl
from jax.experimental.pallas import tpu as pltpu
from jax.sharding import PartitionSpec as P

H = 8
BF = jnp.bfloat16
F32 = jnp.float32
VMEM = 60 * 1024 * 1024
GELU_C = math.sqrt(2.0 / math.pi)


def nn(a, b):
    return lax.dot_general(a, b, (((1,), (0,)), ((), ())), preferred_element_type=F32)


def nt(a, b):
    return lax.dot_general(a, b, (((1,), (1,)), ((), ())), preferred_element_type=F32)


def tn(a, b):
    return lax.dot_general(a, b, (((0,), (0,)), ((), ())), preferred_element_type=F32)


def call(kernel, name, grid, ins, outs, scratch, scal, args, flops):
    moved = sum(a.size * a.dtype.itemsize for a in args)
    moved += sum(math.prod(s.shape) * s.dtype.itemsize for s, _ in outs)
    return pl.pallas_call(
        kernel,
        name=name,
        out_shape=[s for s, _ in outs],
        grid_spec=pltpu.PrefetchScalarGridSpec(
            num_scalar_prefetch=1,
            grid=grid,
            in_specs=ins,
            out_specs=[b for _, b in outs],
            scratch_shapes=scratch,
        ),
        compiler_params=pltpu.CompilerParams(
            vmem_limit_bytes=VMEM, dimension_semantics=("arbitrary",) * len(grid)
        ),
        cost_estimate=pl.CostEstimate(flops=int(flops), bytes_accessed=int(moved), transcendentals=0),
    )(scal, *args)


def whole(shape):
    return pl.BlockSpec(shape, lambda i, s: (0,) * len(shape))


def out(shape, dtype, block, index):
    return (jax.ShapeDtypeStruct(shape, dtype), pl.BlockSpec(block, index))


def norm_rows(rows):
    centred = rows - jnp.mean(rows, axis=-1, keepdims=True)
    spread = jnp.mean(centred * centred, axis=-1, keepdims=True)
    scale = lax.rsqrt(spread + 1e-05)
    return centred * scale, scale


def norm_back(grad, gain, unit, scale):
    g = grad * gain
    inner = jnp.mean(g * unit, axis=-1, keepdims=True)
    return scale * (g - jnp.mean(g, axis=-1, keepdims=True) - unit * inner)


def place(dst, s_ref, own, mine, theirs, lead=()):
    half, quarter = own.shape[-2], mine.shape[-2]
    y, core = s_ref[0], s_ref[1]
    base = (1 - y) * half
    dst[lead + (pl.ds(pl.multiple_of(y * half, quarter), half),)] = own[...]
    dst[lead + (pl.ds(pl.multiple_of(base + core * quarter, quarter), quarter),)] = mine[...]
    dst[lead + (pl.ds(pl.multiple_of(base + (1 - core) * quarter, quarter), quarter),)] = theirs[...]


def qkv_kernel(s_ref, x_ref, o_ref, m_ref, t_ref, bc_ref, bp_ref, k_ref, v_ref, qc_ref, qp_ref,
               pr_ref, w_ref, *, first_query, scale):
    i = pl.program_id(0)

    @pl.when(i == 0)
    def _():
        for n in range(3):
            place(w_ref, s_ref, o_ref.at[n], m_ref.at[n], t_ref.at[n], (n,))

    x = x_ref[...]
    k_ref[...] = nn(x, w_ref[1]).astype(BF)
    v_ref[...] = nn(x, w_ref[2]).astype(BF)

    @pl.when(i >= first_query)
    def _():
        q = nn(x, w_ref[0])
        qc_ref[...] = ((q + bc_ref[...]) * scale).astype(BF)
        qp_ref[...] = ((q + bp_ref[...]) * scale).astype(BF)
        pr_ref[...] = (q * scale).astype(BF)


def project_qkv(scal, normed, parts, bias_content, bias_position, seg, scale):
    rows, width = normed.shape
    blk = 256
    first = (rows - seg) // blk
    keys = lambda: out((rows, width), BF, (blk, width), lambda i, s: (i, 0))
    quer = lambda: out((seg, width), BF, (blk, width), lambda i, s: (jnp.maximum(i - first, 0), 0))
    own, mine, theirs = parts
    return call(
        functools.partial(qkv_kernel, first_query=first, scale=scale), "project_qkv", (rows // blk,),
        [pl.BlockSpec((blk, width), lambda i, s: (i, 0)), whole(own.shape), whole(mine.shape),
         whole(theirs.shape), whole((1, width)), whole((1, width))],
        [keys(), keys(), quer(), quer(), quer(),
         out((3, width, width), BF, (3, width, width), lambda i, s: (0, 0, 0))],
        [], scal,
        (normed, own, mine, theirs, bias_content.reshape(1, -1), bias_position.reshape(1, -1)),
        2 * (2 * rows + seg) * width * width)


def position_kernel(s_ref, x_ref, o_ref, m_ref, t_ref, p_ref, w_ref):
    @pl.when(pl.program_id(0) == 0)
    def _():
        place(w_ref, s_ref, o_ref, m_ref, t_ref)

    p_ref[...] = nn(x_ref[...], w_ref[...]).astype(BF)


def project_position(scal, table, parts):
    rows, width = table.shape
    blk = 256
    own, mine, theirs = parts
    return call(
        position_kernel, "project_position", (rows // blk,),
        [pl.BlockSpec((blk, width), lambda i, s: (i, 0)), whole(own.shape), whole(mine.shape),
         whole(theirs.shape)],
        [out((rows, width), BF, (blk, width), lambda i, s: (i, 0))],
        [pltpu.VMEM((width, width), BF)], scal, (table, own, mine, theirs),
        2 * rows * width * width)[0]


RB = 256


def attention_kernel(s_ref, qc_ref, qp_ref, k_ref, v_ref, pos_ref, p_ref, mix_ref, *, comp, mem):
    seg, keys = qc_ref.shape[0], k_ref.shape[0]
    start = comp + mem
    mem_live, comp_live = s_ref[3], s_ref[4]
    flip = (lax.broadcasted_iota(jnp.int32, (RB, RB), 0)
            + lax.broadcasted_iota(jnp.int32, (RB, RB), 1) == RB - 1).astype(BF)
    for r in range(seg // RB):
        width = start + RB * (r + 1)
        rows = slice(r * RB, (r + 1) * RB)
        content = nt(qc_ref[rows], k_ref[:width])
        rel = nt(qp_ref[rows], pos_ref[keys - width:])
        rel = pltpu.roll(rel, width - RB + 1, 1, stride=1, stride_axis=0)
        col = lax.broadcasted_iota(jnp.int32, (RB, width), 1)
        row = lax.broadcasted_iota(jnp.int32, (RB, width), 0) + r * RB
        live = ((col >= comp - comp_live) & (col < comp)) | (
            (col >= start - mem_live) & (col - start <= row))
        masked = jnp.where(live, content + rel, -1e30)
        top = jnp.max(masked, axis=-1, keepdims=True)
        weights = jnp.exp(masked - top)
        probs = (weights / jnp.sum(weights, axis=-1, keepdims=True)).astype(BF)
        mix_ref[rows] = nn(probs, v_ref[:width]).astype(BF)
        p_ref[0, rows, :width] = nn(flip, probs).astype(BF)


def attention(scal, qc, qp, k, v, pos, comp, mem):
    seg, width = qc.shape
    keys = k.shape[0]
    dh = width // H
    q_spec = pl.BlockSpec((seg, dh), lambda h, s: (0, h))
    k_spec = pl.BlockSpec((keys, dh), lambda h, s: (0, h))
    return call(
        functools.partial(attention_kernel, comp=comp, mem=mem), "attention", (H,),
        [q_spec, q_spec, k_spec, k_spec, k_spec],
        [out((H, seg, keys), BF, (1, seg, keys), lambda h, s: (h, 0, 0)),
         out((seg, width), BF, (seg, dh), lambda h, s: (0, h))],
        [], scal, (qc, qp, k, v, pos), 16 * seg * keys * width)


def attention_back_kernel(s_ref, p_ref, gm_ref, qc_ref, qp_ref, k_ref, v_ref, pos_ref, gq_ref,
                          gk_ref, gv_ref, gp_ref, gc_ref, gb_ref, gs_ref, sh_ref, pr_ref, rev_ref,
                          *, start, scale):
    seg, keys = qc_ref.shape[0], k_ref.shape[0]
    flip = (lax.broadcasted_iota(jnp.int32, (RB, RB), 0)
            + lax.broadcasted_iota(jnp.int32, (RB, RB), 1) == RB - 1).astype(BF)
    sum_c = jnp.zeros((1, gc_ref.shape[1]), F32)
    sum_p = jnp.zeros((1, gc_ref.shape[1]), F32)
    for r in range(seg // RB):
        width = start + RB * (r + 1)
        rows = slice(r * RB, (r + 1) * RB)
        for n, ref in enumerate((gm_ref, qc_ref, qp_ref)):
            rev_ref[n, rows] = nn(flip, ref[rows]).astype(BF)
        low = p_ref[0, rows, :width]
        probs = low.astype(F32)
        weighted = probs * nt(rev_ref[0, rows], v_ref[:width])
        scores = (weighted - probs * jnp.sum(weighted, axis=-1, keepdims=True))
        low_scores = scores.astype(BF)
        moved = pltpu.roll(scores, 0, 1, stride=1, stride_axis=0).astype(BF)
        gs_ref[rows, :width] = low_scores
        sh_ref[rows, keys - width:] = moved
        pr_ref[rows, :width] = low
        if width < keys:
            gs_ref[rows, width:] = jnp.zeros((RB, keys - width), BF)
            pr_ref[rows, width:] = jnp.zeros((RB, keys - width), BF)
            sh_ref[rows, : keys - width] = jnp.zeros((RB, keys - width), BF)
        grad_c = nn(low_scores, k_ref[:width])
        grad_p = nn(moved, pos_ref[keys - width:])
        sum_c += jnp.sum(grad_c, axis=0, keepdims=True)
        sum_p += jnp.sum(grad_p, axis=0, keepdims=True)
        gq_ref[rows] = nn(flip, ((grad_c + grad_p) * scale).astype(BF)).astype(BF)
    gc_ref[...] = sum_c * scale
    gb_ref[...] = sum_p * scale
    gv_ref[...] = tn(rev_ref[0], pr_ref[...]).astype(BF)
    gk_ref[...] = tn(rev_ref[1], gs_ref[...]).astype(BF)
    gp_ref[...] = tn(rev_ref[2], sh_ref[...]).astype(BF)


def attention_back(scal, probs, gm, qc, qp, k, v, pos, start, scale):
    seg, width = qc.shape
    keys = k.shape[0]
    dh = width // H
    q_spec = pl.BlockSpec((seg, dh), lambda h, s: (0, h))
    k_spec = pl.BlockSpec((keys, dh), lambda h, s: (0, h))
    turned = lambda: out((width, keys), BF, (dh, keys), lambda h, s: (h, 0))
    sums = lambda: out((1, width), F32, (1, dh), lambda h, s: (0, h))
    big = pltpu.VMEM((seg, keys), BF)
    return call(
        functools.partial(attention_back_kernel, start=start, scale=scale), "attention_back", (H,),
        [pl.BlockSpec((1, seg, keys), lambda h, s: (h, 0, 0)), q_spec, q_spec, q_spec, k_spec,
         k_spec, k_spec],
        [out((seg, width), BF, (seg, dh), lambda h, s: (0, h)), turned(), turned(), turned(),
         sums(), sums()],
        [big, big, big, pltpu.VMEM((3, seg, dh), BF)], scal, (probs, gm, qc, qp, k, v, pos),
        24 * seg * keys * width)


def mixed_kernel(s_ref, tok_ref, mix_ref, o_ref, m_ref, t_ref, g_ref, att_ref, sec_ref, w_ref):
    @pl.when(pl.program_id(0) == 0)
    def _():
        place(w_ref, s_ref, o_ref, m_ref, t_ref)

    attended = tok_ref[...].astype(F32) + nn(mix_ref[...], w_ref[...])
    att_ref[...] = attended
    sec_ref[...] = (norm_rows(attended)[0] * g_ref[...]).astype(BF)


def mix_out(scal, tokens, mixed, parts, gain):
    seg, width = tokens.shape
    blk = 256
    own, mine, theirs = parts
    row = pl.BlockSpec((blk, width), lambda i, s: (i, 0))
    return call(
        mixed_kernel, "mix_out", (seg // blk,),
        [row, row, whole(own.shape), whole(mine.shape), whole(theirs.shape), whole((1, width))],
        [out((seg, width), F32, (blk, width), lambda i, s: (i, 0)),
         out((seg, width), BF, (blk, width), lambda i, s: (i, 0)),
         out((width, width), BF, (width, width), lambda i, s: (0, 0))],
        [], scal, (tokens, mixed, own, mine, theirs, gain), 2 * seg * width * width)


def part_shape(rows, cols, n_dp, extra=()):
    return (2, n_dp // 2) + extra + (rows // n_dp, cols // 2)


def put(keep, send, buf, values, core, width):
    rows, cols = values.shape
    pairs, _, chunk, _ = buf.shape
    buf[...] = values.reshape(pairs, 2, chunk, cols)
    mine, theirs = buf[:, core], buf[:, 1 - core]
    for y in range(cols // width):
        keep[y] = mine[:, :, y * width:(y + 1) * width].astype(BF)
        send[y] = theirs[:, :, y * width:(y + 1) * width].astype(BF)


def ffn_kernel(s_ref, sec_ref, cot_ref, att_ref, uo_ref, um_ref, ut_ref, do_ref, dm_ref, dt_ref,
               b_ref, g_ref, out_ref, gatt_ref, uk_ref, us_ref, dk_ref, ds_ref, gb_ref, gg_ref,
               gout_ref, wu_ref, wd_ref, acc_ref, gsec_ref, ubuf, dbuf):
    i, n = pl.program_id(0), pl.num_programs(0)
    y, core = s_ref[0], s_ref[1]

    @pl.when(i == 0)
    def _():
        row = lax.broadcasted_iota(jnp.int32, cot_ref.shape, 0)
        gout_ref[...] = jnp.where(row < s_ref[2], cot_ref[...], jnp.zeros((), BF))
        acc_ref[...] = att_ref[...]
        gsec_ref[...] = jnp.zeros_like(gsec_ref)

    place(wu_ref, s_ref, uo_ref, um_ref, ut_ref)
    half = i // (n // 2)
    side = (i % (n // 2)) // (n // 4)

    @pl.when(half == y)
    def _():
        wd_ref[...] = do_ref[...]

    @pl.when((half != y) & (side == core))
    def _():
        wd_ref[...] = dm_ref[...]

    @pl.when((half != y) & (side != core))
    def _():
        wd_ref[...] = dt_ref[...]

    second, gout = sec_ref[...], gout_ref[...]
    v = nn(second, wu_ref[...]) + b_ref[...]
    t = jnp.tanh(GELU_C * (v + 0.044715 * (v * v * v)))
    act = (0.5 * v * (1.0 + t)).astype(BF)
    slope = 0.5 * (1.0 + t) + 0.5 * v * (1.0 - t * t) * (GELU_C * (1.0 + 3 * 0.044715 * v * v))
    acc_ref[...] += nn(act, wd_ref[...])
    grad_inner = (nt(gout, wd_ref[...]) * slope).astype(BF)
    gb_ref[...] = jnp.sum(grad_inner.astype(F32), axis=0, keepdims=True)
    gsec_ref[...] += nt(grad_inner, wu_ref[...])
    put(dk_ref, ds_ref, dbuf, tn(gout, act), core, act.shape[1])
    put(uk_ref, us_ref, ubuf, tn(grad_inner, second), core, second.shape[1] // 2)

    @pl.when(i == n - 1)
    def _():
        out_ref[...] = acc_ref[...].astype(BF)
        unit, scale = norm_rows(att_ref[...])
        grad = gsec_ref[...]
        gg_ref[...] = jnp.sum(grad * unit, axis=0, keepdims=True)
        gatt_ref[...] = norm_back(grad, g_ref[...], unit, scale) + gout_ref[...].astype(F32)


def feed_forward(scal, second, cotangent, attended, up_parts, down_parts, bias_up, gain, n_dp):
    seg, width = second.shape
    inner = bias_up.shape[1]
    n = 8
    blk = inner // n
    uo, um, ut = up_parts
    do, dm, dt = down_parts
    uch, dch = inner // n_dp, width // n_dp
    pairs = blk // (2 * uch)
    col = lambda a: pl.BlockSpec((a.shape[0], blk), lambda i, s: (0, i))
    row = lambda m: pl.BlockSpec((blk, width), lambda i, s: (i % m, 0))
    up_shape, down_shape = part_shape(inner, width, n_dp), part_shape(width, inner, n_dp)
    up_out = lambda: out(up_shape, BF, (2, pairs, uch, width // 2), lambda i, s: (0, i, 0, 0))
    down_out = lambda: out(down_shape, BF, (1, n_dp // 2, dch, blk),
                           lambda i, s: (i // (n // 2), 0, 0, i % (n // 2)))
    full = (seg, width)
    return call(
        ffn_kernel, "feed_forward", (n,),
        [whole(full), whole(full), whole(full), col(uo), col(um), col(ut), row(n // 2),
         row(n // 4), row(n // 4), pl.BlockSpec((1, blk), lambda i, s: (0, i)), whole((1, width))],
        [out(full, BF, full, lambda i, s: (0, 0)), out(full, F32, full, lambda i, s: (0, 0)),
         up_out(), up_out(), down_out(), down_out(),
         out((1, inner), F32, (1, blk), lambda i, s: (0, i)),
         out((1, width), F32, (1, width), lambda i, s: (0, 0))],
        [pltpu.VMEM(full, BF), pltpu.VMEM((width, blk), BF), pltpu.VMEM((blk, width), BF),
         pltpu.VMEM(full, F32), pltpu.VMEM(full, F32), pltpu.VMEM((pairs, 2, uch, width), F32),
         pltpu.VMEM((n_dp // 2, 2, dch, blk), F32)],
        scal, (second, cotangent, attended, uo, um, ut, do, dm, dt, bias_up, gain),
        12 * seg * width * inner)


def mid_kernel(s_ref, ga_ref, mix_ref, w_ref, gm_ref, k_ref, x_ref, acc_ref, buf):
    i = pl.program_id(0)
    low = ga_ref[...].astype(BF)
    part = nt(low, w_ref[...])

    @pl.when(i == 0)
    def _():
        acc_ref[...] = part

    @pl.when(i > 0)
    def _():
        acc_ref[...] += part

    put(k_ref, x_ref, buf, tn(low, mix_ref[...]), s_ref[1], mix_ref.shape[1] // 2)

    @pl.when(i == pl.num_programs(0) - 1)
    def _():
        gm_ref[...] = acc_ref[...].astype(BF)


def mid(scal, grad_attended, mixed, w_out, n_dp):
    seg, width = mixed.shape
    blk = 256
    chunk = width // n_dp
    pairs = blk // (2 * chunk)
    shape = part_shape(width, width, n_dp)
    half = lambda: out(shape, BF, (2, pairs, chunk, width // 2), lambda i, s: (0, i, 0, 0))
    return call(
        mid_kernel, "grad_mixed", (width // blk,),
        [pl.BlockSpec((seg, blk), lambda i, s: (0, i)), whole((seg, width)),
         pl.BlockSpec((width, blk), lambda i, s: (0, i))],
        [out((seg, width), BF, (seg, width), lambda i, s: (0, 0)), half(), half()],
        [pltpu.VMEM((seg, width), F32), pltpu.VMEM((pairs, 2, chunk, width), F32)], scal,
        (grad_attended, mixed, w_out), 4 * seg * width * width)


def rel_kernel(s_ref, gp_ref, tab_ref, k_ref, x_ref, buf):
    put(k_ref, x_ref, buf, nn(gp_ref[...], tab_ref[...]), s_ref[1], tab_ref.shape[1] // 2)


def grad_rel(scal, gpos, table, n_dp):
    rows, width = table.shape
    blk = 256
    chunk = width // n_dp
    pairs = blk // (2 * chunk)
    shape = part_shape(width, width, n_dp)
    half = lambda: out(shape, BF, (2, pairs, chunk, width // 2), lambda i, s: (0, i, 0, 0))
    return call(
        rel_kernel, "grad_rel", (width // blk,),
        [pl.BlockSpec((blk, rows), lambda i, s: (i, 0)), whole((rows, width))],
        [half(), half()], [pltpu.VMEM((pairs, 2, chunk, width), F32)], scal, (gpos, table),
        2 * rows * width * width)


def grad_qkv_kernel(s_ref, gq_ref, gk_ref, gv_ref, x_ref, qk, qx, kk, kx, vk, vx, buf):
    core = s_ref[1]
    seg = gq_ref.shape[0]
    width = x_ref.shape[1] // 2
    put(kk, kx, buf, nn(gk_ref[...], x_ref[...]), core, width)
    put(vk, vx, buf, nn(gv_ref[...], x_ref[...]), core, width)
    put(qk, qx, buf, tn(gq_ref[...], x_ref[x_ref.shape[0] - seg:]), core, width)


def grad_qkv(scal, gq, gk, gv, normed, n_dp):
    rows, width = normed.shape
    seg = gq.shape[0]
    blk = 256
    chunk = width // n_dp
    pairs = blk // (2 * chunk)
    shape = part_shape(width, width, n_dp)
    half = lambda: out(shape, BF, (2, pairs, chunk, width // 2), lambda i, s: (0, i, 0, 0))
    turned = pl.BlockSpec((blk, rows), lambda i, s: (i, 0))
    return call(
        grad_qkv_kernel, "grad_qkv", (width // blk,),
        [pl.BlockSpec((seg, blk), lambda i, s: (0, i)), turned, turned, whole((rows, width))],
        [half() for _ in range(6)], [pltpu.VMEM((pairs, 2, chunk, width), F32)], scal,
        (gq, gk, gv, normed), 2 * (2 * rows + seg) * width * width)


def grad_tokens_kernel(s_ref, gq_ref, gk_ref, gv_ref, x_ref, tok_ref, ga_ref, w_ref, g_ref,
                       gt_ref, gg_ref, *, first):
    i = pl.program_id(0)
    grad = nt(gk_ref[...].T, w_ref[1]) + nt(gv_ref[...].T, w_ref[2])
    gain = g_ref[...]

    @pl.when(i == 0)
    def _():
        gg_ref[...] = jnp.zeros_like(gg_ref)

    @pl.when(i < first)
    def _():
        gg_ref[...] += jnp.sum(grad * x_ref[...].astype(F32), axis=0, keepdims=True) / gain

    @pl.when(i >= first)
    def _():
        total = grad + nt(gq_ref[...], w_ref[0])
        unit, scale = norm_rows(tok_ref[...].astype(F32))
        gg_ref[...] += jnp.sum(total * unit, axis=0, keepdims=True)
        gt_ref[...] = (ga_ref[...] + norm_back(total, gain, unit, scale)).astype(BF)


def grad_tokens(scal, gq, gk, gv, normed, tokens, grad_attended, w, gain):
    rows, width = normed.shape
    seg = tokens.shape[0]
    blk = 256
    first = (rows - seg) // blk
    turned = pl.BlockSpec((width, blk), lambda i, s: (0, i))
    late = pl.BlockSpec((blk, width), lambda i, s: (jnp.maximum(i - first, 0), 0))
    return call(
        functools.partial(grad_tokens_kernel, first=first), "grad_tokens", (rows // blk,),
        [late, turned, turned, pl.BlockSpec((blk, width), lambda i, s: (i, 0)), late, late,
         whole(w.shape), whole((1, width))],
        [out((seg, width), BF, (blk, width), lambda i, s: (jnp.maximum(i - first, 0), 0)),
         out((1, width), F32, (1, width), lambda i, s: (0, 0))],
        [], scal, (gq, gk, gv, normed, tokens, grad_attended, w, gain),
        2 * (2 * rows + seg) * width * width)


def squeeze_kernel(s_ref, gr_ref, o_ref, m_ref, t_ref, w_ref, g_ref, sq_ref, low_ref, k_ref, v_ref):
    y, core = s_ref[0], s_ref[1]
    half, quarter = o_ref.shape[1], m_ref.shape[1]
    base = (1 - y) * half
    total = jnp.zeros(sq_ref.shape, F32)
    for t in range(3):
        at = lambda off, size: gr_ref[t, :, pl.ds(pl.multiple_of(off, quarter), size)]
        total += nn(at(y * half, half), o_ref[t])
        total += nn(at(base + core * quarter, quarter), m_ref[t])
        total += nn(at(base + (1 - core) * quarter, quarter), t_ref[t])
    sq_ref[...] = total
    low_ref[...] = total.astype(BF)
    unit = (norm_rows(total)[0] * g_ref[...]).astype(BF)
    k_ref[...] = nn(unit, w_ref[1]).astype(BF)
    v_ref[...] = nn(unit, w_ref[2]).astype(BF)


def squeeze(scal, groups, parts, w, gain):
    _, rows, width = groups.shape
    own, mine, theirs = parts
    shape = (rows, width)
    here = lambda d: out(shape, d, shape, lambda i, s: (0, 0))
    return call(
        squeeze_kernel, "squeeze", (1,),
        [whole(groups.shape), whole(own.shape), whole(mine.shape), whole(theirs.shape),
         whole(w.shape), whole((1, width))],
        [here(F32), here(BF), here(BF), here(BF)], [], scal, (groups, own, mine, theirs, w, gain),
        10 * rows * width * width)


def masked_softmax(scores, live):
    masked = jnp.where(live, scores, -1e30)
    weights = jnp.exp(masked - jnp.max(masked, axis=-1, keepdims=True))
    return weights / jnp.sum(weights, axis=-1, keepdims=True)


def recon_kernel(s_ref, pr_ref, ok_ref, ov_ref, ck_ref, cv_ref, gk_ref, gv_ref):
    seg_len = s_ref[2]
    count = seg_len // 3
    probe = pr_ref[...]
    seg, mem, comp = probe.shape[0], ok_ref.shape[0], ck_ref.shape[0]
    old_live = lax.broadcasted_iota(jnp.int32, (seg, mem), 1) < 3 * count
    old = nn(masked_softmax(nt(probe, ok_ref[...]), old_live).astype(BF), ov_ref[...])
    live = lax.broadcasted_iota(jnp.int32, (seg, comp), 1) < count
    probs = masked_softmax(nt(probe, ck_ref[...]), live)
    low = probs.astype(BF)
    gap = nn(low, cv_ref[...]) - old
    row = lax.broadcasted_iota(jnp.int32, gap.shape, 0)
    grad_out = (jnp.where(row < seg_len, gap, 0.0) * (2.0 / seg_len.astype(F32))).astype(BF)
    gv_ref[...] = tn(low, grad_out).astype(BF)
    weighted = probs * nt(grad_out, cv_ref[...])
    scores = (weighted - probs * jnp.sum(weighted, axis=-1, keepdims=True)).astype(BF)
    gk_ref[...] = tn(scores, probe).astype(BF)


def reconstruct(scal, probe, k, v, ck, cv, mem):
    seg, width = probe.shape
    rows = ck.shape[0]
    dh = width // H
    at = lambda n, b: pl.BlockSpec((n, dh), lambda h, s: (b, h))
    grads = lambda: out((rows, width), BF, (rows, dh), lambda h, s: (0, h))
    return call(
        recon_kernel, "reconstruct", (H,),
        [at(seg, 0), at(mem, 1), at(mem, 1), at(rows, 0), at(rows, 0)], [grads(), grads()], [],
        scal, (probe, k, v, ck, cv), 4 * seg * width * mem + 12 * seg * width * rows)


def grad_comp_kernel(s_ref, sq_ref, gk_ref, gv_ref, w_ref, g_ref, gr_ref, k_ref, x_ref, low_ref, buf):
    @pl.when(pl.program_id(0) == 0)
    def _():
        grad = nt(gk_ref[...], w_ref[1]) + nt(gv_ref[...], w_ref[2])
        unit, scale = norm_rows(sq_ref[...])
        low_ref[...] = norm_back(grad, g_ref[...], unit, scale).astype(BF)

    part = tn(low_ref[...], gr_ref[0])
    put(k_ref.at[:, :, 0], x_ref.at[:, :, 0], buf, part, s_ref[1], part.shape[1] // 2)


def grad_comp(scal, squeezed, gk, gv, w, gain, groups, n_dp):
    taps, rows, width = groups.shape
    chunk = width // n_dp
    shape = part_shape(width, width, n_dp, (taps,))
    half = lambda: out(shape, BF, shape[:2] + (1,) + shape[3:], lambda i, s: (0, 0, i, 0, 0))
    here = whole((rows, width))
    return call(
        grad_comp_kernel, "grad_comp", (taps,),
        [here, here, here, whole(w.shape), whole((1, width)),
         pl.BlockSpec((1, rows, width), lambda i, s: (i, 0, 0))],
        [half(), half()],
        [pltpu.VMEM((rows, width), BF), pltpu.VMEM((n_dp // 2, 2, chunk, width), F32)], scal,
        (squeezed, gk, gv, w, gain, groups), 10 * rows * width * width)


class Links:
    def __init__(self):
        self.dp = lax.axis_index("dp")
        self.y = lax.axis_index("fsdp")
        self.n_dp = lax.axis_size("dp")
        self.bits = self.n_dp.bit_length() - 1

    def bit(self, axis):
        return self.y if axis == "y" else (self.dp >> axis) & 1

    def swap(self, value, axis):
        if axis == "y":
            return lax.ppermute(value, "fsdp", [(0, 1), (1, 0)])
        return lax.ppermute(value, "dp", [(i, i ^ (1 << axis)) for i in range(self.n_dp)])


def ordered(a, b, bit):
    shape = (a.shape[0], 2) + a.shape[1:]
    at = lax.broadcasted_iota(jnp.int32, shape, 1)
    return jnp.where(at == bit, a[:, None], b[:, None])


def gather(links, local, first, second):
    n, rows, cols = local.shape
    place_of = links.bit(0) * 4 + links.bit(second) * 2 + links.bit(first)
    piece = lax.dynamic_index_in_dim(local.reshape(n, 8, rows // 8, cols), place_of, 1, False)
    one = links.swap(piece, "y")
    two = ordered(one, links.swap(one, first), links.bit(first))
    two = two.reshape(n, rows // 4, cols)
    mine = ordered(two, links.swap(two, second), links.bit(second)).reshape(n, rows // 2, cols)
    return local, mine, links.swap(mine, 0)


def stage_kernel(s_ref, *refs, slots):
    n = len(slots)
    for c in range(n):
        keep, recv, held, send = refs[c], refs[n + c], refs[2 * n + c], refs[3 * n + c]
        bit = s_ref[slots[c]]
        total = lambda b: (keep[:, b].astype(F32) + recv[:, b].astype(F32)).astype(held.dtype)
        held[...] = total(bit)
        send[...] = total(1 - bit)


def stage(links, keeps, recvs, axes, places, steps):
    ins, outs = [], []
    args = [[], []]
    for keep, recv, where in zip(keeps, recvs, places):
        lead, tail = keep.shape[:-3], keep.shape[-3:]
        pre, post = math.prod(lead[:where]), math.prod(lead[where + 1:])
        view = (pre, 2, post * tail[0]) + tail[1:]
        rows = view[2]
        split = 1 if keep.dtype == F32 else steps
        bp = max(pre // split, 1)
        br = rows * bp * split // (pre * split) if split == 1 else rows * pre // (split * bp)
        br = min(max(br, 1), rows)
        nr = rows // br
        if split == 1:
            spec = lambda i, s: (0, 0, 0, 0, 0)
            held = lambda i, s: (0, 0, 0, 0)
            bp, br = pre, rows
        else:
            spec = functools.partial(lambda nr, i, s: (i // nr, 0, i % nr, 0, 0), nr)
            held = functools.partial(lambda nr, i, s: (i // nr, i % nr, 0, 0), nr)
        ins.append(pl.BlockSpec((bp, 2, br) + tail[1:], spec))
        shape = (pre, rows) + tail[1:]
        outs.append(out(shape, keep.dtype, (bp, br) + tail[1:], held))
        args[0].append(keep.reshape(view))
        args[1].append(recv.reshape(view))
    scal = jnp.stack([links.bit(a) for a in axes]).astype(jnp.int32)
    done = call(
        functools.partial(stage_kernel, slots=tuple(range(len(axes)))), "stage", (steps,),
        ins + ins, outs + outs, [], scal, args[0] + args[1], 0)
    n = len(keeps)
    shapes = [k.shape[:w] + k.shape[w + 1:] for k, w in zip(keeps, places)]
    held = [d.reshape(s) for d, s in zip(done[:n], shapes)]
    send = [d.reshape(s) for d, s in zip(done[n:], shapes)]
    return held, send


def final_kernel(s_ref, *refs):
    n = len(refs) // 3
    for c in range(n):
        total = refs[c][...].astype(F32) + refs[n + c][...].astype(F32)
        if total.shape[1] == 1:
            refs[2 * n + c][...] = total
        else:
            for t in range(total.shape[0]):
                refs[2 * n + c][t] = total[t].T


def final(keeps, recvs, scal):
    ins, outs = [], []
    for keep in keeps:
        taps, rows, cols = keep.shape
        ins.append(whole(keep.shape))
        shape = keep.shape if rows == 1 else (taps, cols, rows)
        outs.append(out(shape, F32, shape, lambda i, s: (0, 0, 0)))
    return call(final_kernel, "final", (1,), ins + ins, outs, [], scal, list(keeps) + list(recvs), 0)


def scatter(links, chains, orders, scal, steps):
    names = ["y"] + list(range(links.bits - 1, 0, -1))
    left = [list(names) for _ in chains]
    split = lambda a: a.reshape((2,) * len(names) + a.shape[2:])
    keeps = [split(k) for k, _ in chains]
    recvs = [links.swap(split(s), 0) for _, s in chains]
    for level in range(len(names)):
        axes = [o[level] for o in orders]
        places = [l.index(a) for l, a in zip(left, axes)]
        count = steps if level < 2 else 1
        keeps, sends = stage(links, keeps, recvs, axes, places, count)
        for l, a in zip(left, axes):
            l.remove(a)
        recvs = [links.swap(s, a) for s, a in zip(sends, axes)]
    return final(keeps, recvs, scal)


def turns(links):
    rest = list(range(3, links.bits))
    return [[1, "y", 2] + rest, ["y", 2, 1] + rest, [2, 1, "y"] + rest]


def sinusoid(table_rows, table_width):
    distance = (table_rows - 1 - jnp.arange(table_rows)).astype(F32)
    frequency = jnp.exp(
        jnp.arange(0, table_width, 2).astype(F32) * (-math.log(10000.0) / table_width)
    )
    angles = distance[:, None] * frequency[None, :]
    return jnp.concatenate([jnp.sin(angles), jnp.cos(angles)], axis=1)


def body(tokens, memory, compressed, cotangent, seg_len, mem_fill, cmem_fill, w_qkv, w_rel, w_out,
         w_up, w_down, w_comp, norm_gain1, norm_gain2, bias_content, bias_position, bias_up):
    streams = tokens.shape[0]
    assert streams == 1
    links = Links()
    n_dp = links.n_dp
    seg, width = tokens.shape[1:]
    mem, comp = memory.shape[1], compressed.shape[1]
    start = comp + mem
    keys = start + seg
    squeezed_rows = mem // 3
    scale = (width // H) ** (-0.5)
    current, recent, distant = tokens[0], memory[0], compressed[0]
    seg_length = seg_len[0]
    core = links.bit(0)
    scal = jnp.stack([links.y, core, seg_length, mem_fill[0], cmem_fill[0]]).astype(jnp.int32)
    gain1, gain2 = norm_gain1.reshape(1, -1), norm_gain2.reshape(1, -1)

    qkv_parts = gather(links, w_qkv, 2, 1)
    rel_parts = [p[0] for p in gather(links, w_rel[None], 1, 2)]
    comp_parts = gather(links, w_comp, 1, 2)
    out_parts = [p[0] for p in gather(links, w_out[None], 2, 1)]
    up_parts = [p[0] for p in gather(links, w_up[None], 2, 1)]
    down_parts = [p[0] for p in gather(links, w_down[None], 1, 2)]

    hidden = jnp.concatenate([distant, recent, current], axis=0).astype(F32)
    normed = (norm_rows(hidden)[0] * norm_gain1).astype(BF)
    table = sinusoid(keys, width).astype(BF)
    pad = -squeezed_rows % 64
    groups = jnp.stack([
        jnp.pad(recent[t:3 * squeezed_rows:3], ((0, pad), (0, 0))) for t in range(3)])

    k, v, qc, qp, probe, w_full = project_qkv(
        scal, normed, qkv_parts, bias_content, bias_position, seg, scale)
    pos = project_position(scal, table, rel_parts)
    probs, mixed = attention(scal, qc, qp, k, v, pos, comp, mem)

    squeezed, squeezed_low, ck, cv = squeeze(scal, groups, comp_parts, w_full, gain1)
    gck, gcv = reconstruct(scal, probe, k, v, ck, cv, mem)
    comp_chain = grad_comp(scal, squeezed, gck, gcv, w_full, gain1, groups, n_dp)

    attended, second, w_out_full = mix_out(scal, current, mixed, out_parts, gain2)
    (output, grad_attended, up_keep, up_send, down_keep, down_send, sum_bias, sum_gain2
     ) = feed_forward(scal, second, cotangent[0], attended, up_parts, down_parts,
                      bias_up.reshape(1, -1), gain2, n_dp)
    grad_mix, out_keep, out_send = mid(scal, grad_attended, mixed, w_out_full, n_dp)
    gq, gk, gv, gpos, sum_content, sum_position = attention_back(
        scal, probs, grad_mix, qc, qp, k, v, pos, start, scale)
    qkv_chains = grad_qkv(scal, gq, gk, gv, normed, n_dp)
    rel_chain = grad_rel(scal, gpos, table, n_dp)
    grad_rows, sum_gain1 = grad_tokens(
        scal, gq, gk, gv, normed, current, grad_attended, w_full, gain1)

    turn = turns(links)
    tap = lambda a: a[:, :, None]
    (grad_comp_t,) = scatter(links, [comp_chain], [turn[2]], scal, 4)
    grad_up_t, grad_down_t, grad_out_t = scatter(
        links, [(tap(up_keep), tap(up_send)), (tap(down_keep), tap(down_send)),
                (tap(out_keep), tap(out_send))],
        [turn[0], turn[1], turn[2]], scal, 4)
    small = jnp.concatenate(
        [s.reshape(n_dp, 2, -1) for s in
         (sum_gain1, sum_gain2, sum_content, sum_position, sum_bias)], axis=-1)
    small = small.reshape(n_dp // 2, 2, 2, 1, 1, -1).transpose(1, 2, 0, 3, 4, 5)
    small_keep = lax.dynamic_index_in_dim(small, core, 0, False)
    small_send = lax.dynamic_index_in_dim(small, 1 - core, 0, False)
    qk, qx, kk, kx, vk, vx = [tap(a) for a in qkv_chains]
    grad_q_t, grad_k_t, grad_v_t, grad_rel_t, vec = scatter(
        links, [(qk, qx), (kk, kx), (vk, vx), tuple(tap(a) for a in rel_chain),
                (small_keep, small_send)],
        [turn[0], turn[1], turn[2], turn[0], turn[1]], scal, 2)
    each = width // (2 * n_dp)
    vec = vec.reshape(-1)
    grad_gain1, grad_gain2, grad_content, grad_position = [
        vec[n * each:(n + 1) * each] for n in range(4)]

    new_memory = lax.dynamic_slice_in_dim(
        jnp.concatenate([recent, current], axis=0), seg_length, mem, 0)
    new_compressed = lax.dynamic_slice_in_dim(
        jnp.concatenate([distant, squeezed_low[:squeezed_rows]], axis=0), seg_length // 3, comp, 0)
    return (output[None], grad_rows[None], new_memory[None], new_compressed[None],
            jnp.concatenate([grad_q_t, grad_k_t, grad_v_t], axis=0), grad_rel_t[0], grad_out_t[0],
            grad_up_t[0], grad_down_t[0], grad_comp_t, grad_gain1, grad_gain2, grad_content,
            grad_position, vec[4 * each:])


def solution(mesh):
    rows = P(("dp", "fsdp"), None, None)
    one = P(("dp", "fsdp"))
    return jax.shard_map(
        body,
        mesh=mesh,
        in_specs=(rows, rows, rows, rows, one, one, one, P(None, "fsdp", None), P("fsdp", None),
                  P("fsdp", None), P("fsdp", None), P("fsdp", None), P(None, "fsdp", None), P(),
                  P(), P(), P(), P()),
        out_specs=(rows, rows, rows, rows, P(None, "fsdp", "dp"), P("fsdp", "dp"),
                   P("fsdp", "dp"), P("fsdp", "dp"), P("fsdp", "dp"), P(None, "fsdp", "dp"), one,
                   one, one, one, one),
        check_vma=False,
    )
```

time: 1770 us -> 599 us (0.34)
  blocking collectives: 797 us -> 0 us
  local copies, waits for them, and re-layouts: 407 us -> 38.5 us
  Pallas kernels: 0 us -> 275 us
  matrix products: 265 us -> 0 us
  starting transfers between devices: 1.53 us -> 65.6 us
  other arithmetic: 114 us -> 50.5 us
    unnamed x2 -> x0, blocking collectives: 797 us -> none
    pallas_call x0 -> x28, Pallas kernels: none -> 275 us  [call(): pl.pallas_call(kernel, name=name, out_shape=[s for s, _ in outs], grid_sp...]
    dot_general x42 -> x0, matrix products: 265 us -> none  [the longest x1 17.7 us: score_block(): jnp.einsum('qhd,khd->hqk', query_content, key_heads, preferred_element_ty...]
    unnamed x153 -> x103, local copies, waits for them, and re-layouts: 182 us -> 15.2 us
    ppermute x0 -> x69, waiting for transfers between devices: none -> 155 us  [the longest x54 137 us: swap(): lax.ppermute(value, 'dp', [(i, i ^ 1 << axis) for i in range(self.n_dp)])]
    all_gather x6 -> x0, waiting for transfers between devices: 139 us -> none  [the longest x1 75.9 us: body(): lax.all_gather(w_qkv, 'fsdp', axis=1, tiled=True)]
    reshape x11 -> x0, local copies, waits for them, and re-layouts: 135 us -> none  [the longest x2 61.5 us: rel_shift(): padded = padded.reshape(head_count, key_count + 1, query_count)[:, 1:]]
    ppermute x0 -> x69, starting transfers between devices: none -> 65.6 us  [the longest x54 49.6 us: swap(): lax.ppermute(value, 'dp', [(i, i ^ 1 << axis) for i in range(self.n_dp)])]
  transfers between devices with their start and end apart: 16 -> 69, of which waited for: 3 -> 20; matrix products, arithmetic and copies ran while one was open for 44% -> 13% of each run, Pallas kernels for 0% -> 46%
where the time goes in v1:
time: 599 us; the launch traced here: 588 us
  Pallas kernels  275 us (46%)
  waiting for transfers between devices  155 us (26%)
  starting transfers between devices  65.6 us (11%)
  other arithmetic  50.5 us (8%)
  local copies, waits for them, and re-layouts  38.5 us (6%)
    pallas_call x28, Pallas kernels, call(): pl.pallas_call(kernel, name=name, out_shape=[s for s, _ in outs], grid_sp...  275 us
    ppermute x54, waiting for transfers between devices, swap(): lax.ppermute(value, 'dp', [(i, i ^ 1 << axis) for i in range(self.n_dp)])  137 us
    ppermute x54, starting transfers between devices, swap(): lax.ppermute(value, 'dp', [(i, i ^ 1 << axis) for i in range(self.n_dp)])  49.6 us
    ppermute x15, waiting for transfers between devices, swap(): return lax.ppermute(value, 'fsdp', [(0, 1), (1, 0)])  18.4 us
    select_n x20, other arithmetic, ordered(): return jnp.where(at == bit, a[:, None], b[:, None])  17.8 us
    ppermute x15, starting transfers between devices, swap(): return lax.ppermute(value, 'fsdp', [(0, 1), (1, 0)])  16 us
    unnamed x103, local copies, waits for them, and re-layouts  15.2 us
  transfers between devices with their start and end apart: 69, of which 20 were waited for; matrix products, arithmetic and copies ran while one was open for 13% of the time, Pallas kernels for 46%

profile of v1, /device:TPU:0, one launch (start us, length us, event | category | flops | bytes accessed | tf_op | source)
XLA Modules:
  0.0 588.5 jit_solution(9111282715271598445)
XLA Ops:
  2.6 3.0 collective-permute-start
  15.2 3.0 fusion.2
  18.2 4.1 fusion.4.x_ref
  22.3 11.9 %fusion.5 = (bf16[1536,512]{1,0:T(8,128)(2,1)S(1)}, bf16[1536,512]{1,0:T(8,128)(2,1)S(1)}) fusion(f32[512]{0:T(512)S(1)} %multiply_exponential_fusion, f32[1536]{0:T(1024)S(1)} %subtract_convert_fusion), kind=kLoop, calls=%fused_computation.9 | loop fusion | flops 2359296 | bytes 3153920 | tf_op jit(solution)/shard_map/convert
  49.6 6.8 %collective-permute-done.9 = bf16[1,64,1024]{2,1,0:T(8,128)(2,1)S(1)} collective-permute-done((bf16[1,64,1024]{2,1,0:T(8,128)(2,1)S(1)}, bf16[1,64,1024]{2,1,0:T(8,128)(2,1)S(1)}, u32[]{:S(2)}, u32[]{:S(2)}) %collective-permute-start.9) | collective-permute-done | bytes 131104 | tf_op jit(solution)/shard_map/ppermute | solution.py:582
  63.9 7.5 %collective-permute-done.1 = bf16[3,64,1024]{2,1,0:T(8,128)(2,1)S(1)} collective-permute-done((bf16[3,64,1024]{2,1,0:T(8,128)(2,1)}, bf16[3,64,1024]{2,1,0:T(8,128)(2,1)S(1)}, u32[]{:S(2)}, u32[]{:S(2)}) %collective-permute-start.1) | collective-permute-done | bytes 393248 | tf_op jit(solution)/shard_map/ppermute | solution.py:582
  75.9 16.1 %collective-permute-done.10 = bf16[1,128,1024]{2,1,0:T(8,128)(2,1)S(1)} collective-permute-done((bf16[1,128,1024]{2,1,0:T(8,128)(2,1)S(1)}, bf16[1,128,1024]{2,1,0:T(8,128)(2,1)S(1)}, u32[]{:S(2)}, u32[]{:S(2)}) %collective-permute-start.10) | collective-permute-done | bytes 262176 | tf_op jit(solution)/shard_map/ppermute | solution.py:582
  93.9 6.4 %collective-permute-done.21 = bf16[3,64,1024]{2,1,0:T(8,128)(2,1)S(1)} collective-permute-done((bf16[3,64,1024]{2,1,0:T(8,128)(2,1)}, bf16[3,64,1024]{2,1,0:T(8,128)(2,1)S(1)}, u32[]{:S(2)}, u32[]{:S(2)}) %collective-permute-start.21) | collective-permute-done | bytes 393248 | tf_op jit(solution)/shard_map/ppermute | solution.py:582
  102.8 8.9 %collective-permute-done.17 = bf16[1,256,1024]{2,1,0:T(8,128)(2,1)S(1)} collective-permute-done((bf16[1,256,1024]{2,1,0:T(8,128)(2,1)S(1)}, bf16[1,256,1024]{2,1,0:T(8,128)(2,1)S(1)}, u32[]{:S(2)}, u32[]{:S(2)}) %collective-permute-start.17) | collective-permute-done | bytes 524320 | tf_op jit(solution)/shard_map/ppermute | solution.py:582
  113.8 11.4 %collective-permute-done.2 = bf16[3,128,1024]{2,1,0:T(8,128)(2,1)S(1)} collective-permute-done((bf16[3,128,1024]{2,1,0:T(8,128)(2,1)S(1)}, bf16[3,128,1024]{2,1,0:T(8,128)(2,1)S(1)}, u32[]{:S(2)}, u32[]{:S(2)}) %collective-permute-start.2) | collective-permute-done | bytes 786464 | tf_op jit(solution)/shard_map/ppermute | solution.py:582
  130.4 16.9 %collective-permute-done.18 = bf16[1,512,1024]{2,1,0:T(8,128)(2,1)S(1)} collective-permute-done((bf16[1,512,1024]{2,1,0:T(8,128)(2,1)S(1)}, bf16[1,512,1024]{2,1,0:T(8,128)(2,1)S(1)}, u32[]{:S(2)}, u32[]{:S(2)}) %collective-permute-start.18) | collective-permute-done | bytes 1048608 | tf_op jit(solution)/shard_map/ppermute | solution.py:582
  150.8 8.7 %project_position.1.pos_ref = bf16[1536,1024]{1,0:T(8,128)(2,1)} custom-call(s32[5]{0:T(128)} %stack.38.s_ref, bf16[1536,1024]{1,0:T(8,128)(2,1)} %pad_maximum_fusion.1.x_ref.tab_ref, bf16[512,1024]{1,0:T(8,128)(2,1)} %o_ref.5, bf16[256,1024]{1,0:T(8,128)(2,1)} %bitcast_select_fusion.15.m_ref, bf16[256,1024]{1,0:T(8,128)(2,1)} %bitcast.451), custom_call_target="tpu_custom_call" | custom-call | flops 3221225472 | bytes 8388608 | tf_op jit(solution)/shard_map/project_position/pallas_call | solution.py:33
  159.6 2.7 bitcast_select_fusion.4.m_ref
  165.9 17.6 %project_qkv.1 = (bf16[1536,1024]{1,0:T(8,128)(2,1)}, bf16[1536,1024]{1,0:T(8,128)(2,1)}, bf16[512,1024]{1,0:T(8,128)(2,1)}, bf16[512,1024]{1,0:T(8,128)(2,1)}, ...) custom-call(s32[5]{0:T(128)} %stack.38.s_ref, bf16[1536,1024]{1,0:T(8,128)(2,1)} %fusion.4.x_ref, ...), custom_call_target="tpu_custom_call" | custom-call | flops 7516192768 | bytes 25174016 | tf_op jit(solution)/shard_map/project_qkv/pallas_call | solution.py:33
  183.5 25.8 %attention.1 = (bf16[8,512,1536]{2,1,0:T(8,128)(2,1)}, bf16[512,1024]{1,0:T(8,128)(2,1)}) custom-call(s32[5]{0:T(128)} %stack.38.s_ref, bf16[512,1024]{1,0:T(8,128)(2,1)} %get-tuple-element.141.qc_ref, bf16[512,1024]{1,0:T(8,128)(2,1)} %get-tuple-element.142.qp_ref, bf16[1536,1024]{1,0:T(8,128)(2,1)} %get-tuple-element.143.k_ref.ok_ref, ...), custom_call_target="tpu_custom_call" | custom-call | flops 12884901888 | bytes 25165824 | tf_op jit(solution)/shard_map/attention/pallas_call | solution.py:33
  209.3 5.8 mix_out.1
  215.1 42.0 %feed_forward.1 = (bf16[512,1024]{1,0:T(8,128)(2,1)}, f32[512,1024]{1,0:T(8,128)}, bf16[2,8,256,512]{3,2,1,0:T(8,128)(2,1)}, bf16[2,8,256,512]{3,2,1,0:T(8,128)(...) custom-call(s32[5]{0:T(128)} %stack.38.s_ref, ...), custom_call_target="tpu_custom_call" | custom-call | flops 25769803776 | bytes 40935424 | tf_op jit(solution)/shard_map/feed_forward/pallas_call | solution.py:33
  261.8 9.0 %squeeze.84 = (f32[192,1024]{1,0:T(8,128)}, bf16[192,1024]{1,0:T(8,128)(2,1)}, bf16[192,1024]{1,0:T(8,128)(2,1)}, bf16[192,1024]{1,0:T(8,128)(2,1)}) custom-call(s32[5]{0:T(128)} %stack.38.s_ref, bf16[3,192,1024]{2,1,0:T(8,128)(2,1)} %pad_maximum_fusion.2.gr_ref, bf16[3,512,1024]{2,1,0:T(8,128)(2,1)} %o_ref.7, ...), custom_call_target="tpu_custom_call" | custom-call | flops 2013265920 | bytes 15732736 | tf_op jit(solution)/shard_map/squeeze/pallas_call | solution.py:33
  270.7 15.0 %reconstruct.1 = (bf16[192,1024]{1,0:T(8,128)(2,1)}, bf16[192,1024]{1,0:T(8,128)(2,1)}) custom-call(s32[5]{0:T(128)} %stack.38.s_ref, bf16[512,1024]{1,0:T(8,128)(2,1)} %get-tuple-element.251.pr_ref, bf16[1536,1024]{1,0:T(8,128)(2,1)} %get-tuple-element.143.k_ref.ok_ref, bf16[1536,1024]{1,0:T(8,128)(2,1)} %get-tuple-element.144.v_ref.ov_ref, ...), custom_call_target="tpu_custom_call" | custom-call | flops 2281701376 | bytes 8912896 | tf_op jit(solution)/shard_map/reconstruct/pallas_call | solution.py:33
  285.7 10.2 %grad_comp.1 = (bf16[2,8,3,64,512]{4,3,2,1,0:T(8,128)(2,1)}, bf16[2,8,3,64,512]{4,3,2,1,0:T(8,128)(2,1)}) custom-call(s32[5]{0:T(128)} %stack.38.s_ref, f32[192,1024]{1,0:T(8,128)} %get-tuple-element.250.sq_ref, bf16[192,1024]{1,0:T(8,128)(2,1)} %get-tuple-element.254.gk_ref, bf16[192,1024]{1,0:T(8,128)(2,1)} %get-tuple-element.255.gv_ref, ...), custom_call_target="tpu_custom_call" | custom-call | flops 2013265920 | bytes 15339520 | tf_op jit(solution)/shard_map/grad_comp/pallas_call | solution.py:33
  296.1 8.5 %grad_mixed.1 = (bf16[512,1024]{1,0:T(8,128)(2,1)}, bf16[2,8,64,512]{3,2,1,0:T(8,128)(2,1)}, bf16[2,8,64,512]{3,2,1,0:T(8,128)(2,1)}) custom-call(s32[5]{0:T(128)} %stack.38.s_ref, f32[512,1024]{1,0:T(8,128)} %get-tuple-element.150.ga_ref, bf16[512,1024]{1,0:T(8,128)(2,1)} %get-tuple-element.145.mix_ref, bf16[1024,1024]{1,0:T(8,128)(2,1)} %get-tuple-element.151.w_ref), custom_call_target="tpu_custom_call" | custom-call | flops 2147483648 | bytes 8388608 | tf_op jit(solution)/shard_map/grad_mixed/pallas_call | solution.py:33
  304.9 28.8 %attention_back.1 = (bf16[512,1024]{1,0:T(8,128)(2,1)}, bf16[1024,1536]{1,0:T(8,128)(2,1)}, bf16[1024,1536]{1,0:T(8,128)(2,1)}, bf16[1024,1536]{1,0:T(8,128)(2,1...) custom-call(s32[5]{0:T(128)} %stack.38.s_ref, bf16[8,512,1536]{2,1,0:T(8,128)(2,1)} %get-tuple-element.149.p_ref, ...), custom_call_target="tpu_custom_call" | custom-call | flops 19327352832 | bytes 35659776 | tf_op jit(solution)/shard_map/attention_back/pallas_call | solution.py:33
  333.6 13.3 %grad_qkv.1 = (bf16[2,8,64,512]{3,2,1,0:T(8,128)(2,1)}, bf16[2,8,64,512]{3,2,1,0:T(8,128)(2,1)}, bf16[2,8,64,512]{3,2,1,0:T(8,128)(2,1)}, bf16[2,8,64,512]{3,2,1...) custom-call(s32[5]{0:T(128)} %stack.38.s_ref, ...), custom_call_target="tpu_custom_call" | custom-call | flops 7516192768 | bytes 16777216 | tf_op jit(solution)/shard_map/grad_qkv/pallas_call | solution.py:33
  347.7 11.0 %stage.16 = (bf16[8,1,256,512]{3,2,1,0:T(8,128)(2,1)}, bf16[1,8,64,2048]{3,2,1,0:T(8,128)(2,1)}, bf16[4,2,64,512]{3,2,1,0:T(8,128)(2,1)}, bf16[8,1,256,512]{3,2,...) custom-call(s32[3]{0:T(128)} %pad_add_fusion.2.s_ref, ...), custom_call_target="tpu_custom_call" | custom-call | bytes 28311552 | tf_op jit(solution)/shard_map/stage/pallas_call | solution.py:33
  361.1 16.9 %grad_tokens.1 = (bf16[512,1024]{1,0:T(8,128)(2,1)}, f32[1,1024]{1,0:T(1,128)}) custom-call(s32[5]{0:T(128)} %stack.38.s_ref, bf16[512,1024]{1,0:T(8,128)(2,1)} %get-tuple-element.153.gq_ref, bf16[1024,1536]{1,0:T(8,128)(2,1)} %get-tuple-element.154.gk_ref, bf16[1024,1536]{1,0:T(8,128)(2,1)} %get-tuple-element.155.gv_ref, bf16[1536,1024]{1,0:T(8,128)(2,1)} %fusion.4.x_ref, ...), custom_call_target="tpu_custom_call" | custom-call | flops 7516192768 | bytes 20979712 | tf_op jit(solution)/shard_map/grad_tokens/pallas_call | solution.py:33
  385.0 8.1 %grad_rel.1 = (bf16[2,8,64,512]{3,2,1,0:T(8,128)(2,1)}, bf16[2,8,64,512]{3,2,1,0:T(8,128)(2,1)}) custom-call(s32[5]{0:T(128)} %stack.38.s_ref, bf16[1024,1536]{1,0:T(8,128)(2,1)} %get-tuple-element.162.gp_ref, bf16[1536,1024]{1,0:T(8,128)(2,1)} %pad_maximum_fusion.1.x_ref.tab_ref), custom_call_target="tpu_custom_call" | custom-call | flops 3221225472 | bytes 8388608 | tf_op jit(solution)/shard_map/grad_rel/pallas_call | solution.py:33
  393.3 5.0 stage.20
  401.9 5.8 stage.12
  408.4 3.4 collective-permute-done.33
  412.2 34.3 %collective-permute-done.54 = bf16[2,2,2,1,64,512]{5,4,2,1,0,3:T(8,128)(2,1)} collective-permute-done((bf16[2,2,2,1,64,512]{5,4,2,1,0,3:T(8,128)(2,1)}, bf16[2,2,2,1,64,512]{5,4,2,1,0,3:T(8,128)(2,1)}, u32[]{:S(2)}, u32[]{:S(2)}) %collective-permute-start.54) | collective-permute-done | bytes 524320 | tf_op jit(solution)/shard_map/ppermute | solution.py:582
  449.7 6.9 %stage.17 = (bf16[1,4,256,512]{3,2,1,0:T(8,128)(2,1)}, bf16[2,2,64,2048]{3,2,1,0:T(8,128)(2,1)}, bf16[4,1,64,512]{3,2,1,0:T(8,128)(2,1)}, bf16[1,4,256,512]{3,2,...) custom-call(s32[3]{0:T(128)} %pad_add_fusion.1.s_ref, ...), custom_call_target="tpu_custom_call" | custom-call | bytes 14155776 | tf_op jit(solution)/shard_map/stage/pallas_call | solution.py:33
  463.9 4.1 stage.13
  468.3 4.2 stage.21
  474.4 9.9 %collective-permute-done.38.refs_9_ = f32[2,2,1,1,256]{4,3,2,1,0:T(1,128)S(1)} collective-permute-done((f32[2,2,1,1,256]{4,3,2,1,0:T(1,128)S(1)}, f32[2,2,1,1,256]{4,3,2,1,0:T(1,128)S(1)}, u32[]{:S(2)}, u32[]{:S(2)}) %collective-permute-start.38) | collective-permute-done | bytes 4128 | tf_op jit(solution)/shard_map/ppermute | solution.py:582
  486.4 5.6 collective-permute-done.34.refs_5_
  494.1 4.7 collective-permute-done.37.refs_8_
  498.8 3.3 stage.14
  502.1 3.8 collective-permute-done.43
  505.9 2.8 collective-permute-start.39
  509.8 4.9 stage.18
  519.0 2.8 stage.15
  521.8 2.6 collective-permute-start.48
  542.8 2.8 final.3
  551.8 3.5 stage.19
  562.5 7.5 %collective-permute-done.68.refs_1_ = bf16[3,64,512]{2,1,0:T(8,128)(2,1)S(1)} collective-permute-done((bf16[3,64,512]{2,1,0:T(8,128)(2,1)}, bf16[3,64,512]{2,1,0:T(8,128)(2,1)S(1)}, u32[]{:S(2)}, u32[]{:S(2)}) %collective-permute-start.68) | collective-permute-done | bytes 196640 | tf_op jit(solution)/shard_map/ppermute | solution.py:582
  570.6 2.9 final.5
  575.6 4.1 collective-permute-done.63.refs_5_
  580.6 3.4 final.4
  (321 shorter events, 136.8 us)
Async XLA Ops:
  2.6 55.4 %collective-permute-start = (bf16[3,64,1024]{2,1,0:T(8,128)(2,1)}, bf16[3,64,1024]{2,1,0:T(8,128)(2,1)}, u32[]{:S(2)}, u32[]{:S(2)}) collective-permute-start(bf16[3,64,1024]{2,1,0:T(8,128)(2,1)} %dynamic-slice_bitcast_fusion.3), channel_id=1, source_target_pairs={{0,1},{1,0},{2,3},{3,2},{4,5},{5,4},{6,7},{7,6},{8,9},{9,8},{10,11... | collective-permute-start | bytes 1179656 | tf_op jit(solution)/shard_map/ppermute | solution.py:581
  7.4 54.4 %collective-permute-start.20 = (bf16[3,64,1024]{2,1,0:T(8,128)(2,1)}, bf16[3,64,1024]{2,1,0:T(8,128)(2,1)}, u32[]{:S(2)}, u32[]{:S(2)}) collective-permute-start(bf16[3,64,1024]{2,1,0:T(8,128)(2,1)} %dynamic-slice_bitcast_fusion.2), channel_id=1, source_target_pairs={{0,1},{1,0},{2,3},{3,2},{4,5},{5,4},{6,7},{7,6},{8,9},{9,8},{10,11... | collective-permute-start | bytes 1179656 | tf_op jit(solution)/shard_map/ppermute | solution.py:581
  8.3 28.1 %collective-permute-start.4 = (bf16[1,64,1024]{2,1,0:T(8,128)(2,1)S(1)}, bf16[1,64,1024]{2,1,0:T(8,128)(2,1)S(1)}, u32[]{:S(2)}, u32[]{:S(2)}) collective-permute-start(bf16[1,64,1024]{2,1,0:T(8,128)(2,1)S(1)} %dynamic-slice_bitcast_fusion.5), channel_id=1, source_target_pairs={{0,1},{1,0},{2,3},{3,2},{4,5},{5,4},{6,7},{7,6},{8,9},{9,8},{10,11... | collective-permute-start | bytes 393224 | tf_op jit(solution)/shard_map/ppermute | solution.py:581
  11.3 36.0 %collective-permute-start.8 = (bf16[1,64,1024]{2,1,0:T(8,128)(2,1)S(1)}, bf16[1,64,1024]{2,1,0:T(8,128)(2,1)S(1)}, u32[]{:S(2)}, u32[]{:S(2)}) collective-permute-start(bf16[1,64,1024]{2,1,0:T(8,128)(2,1)S(1)} %dynamic-slice_bitcast_fusion.4), channel_id=1, source_target_pairs={{0,1},{1,0},{2,3},{3,2},{4,5},{5,4},{6,7},{7,6},{8,9},{9,8},{10,11... | collective-permute-start | bytes 393224 | tf_op jit(solution)/shard_map/ppermute | solution.py:581
  12.4 27.9 %collective-permute-start.12 = (bf16[1,64,4096]{2,1,0:T(8,128)(2,1)S(1)}, bf16[1,64,4096]{2,1,0:T(8,128)(2,1)}, u32[]{:S(2)}, u32[]{:S(2)}) collective-permute-start(bf16[1,64,4096]{2,1,0:T(8,128)(2,1)S(1)} %dynamic-slice_bitcast_fusion.1), channel_id=1, source_target_pairs={{0,1},{1,0},{2,3},{3,2},{4,5},{5,4},{6,7},{7,6},{8,9},{9,8},{10,11... | collective-permute-start | bytes 1572872 | tf_op jit(solution)/shard_map/ppermute | solution.py:581
  40.3 18.3 %collective-permute-start.13 = (bf16[1,64,4096]{2,1,0:T(8,128)(2,1)}, bf16[1,64,4096]{2,1,0:T(8,128)(2,1)S(1)}, u32[]{:S(2)}, u32[]{:S(2)}) collective-permute-start(bf16[1,64,4096]{2,1,0:T(8,128)(2,1)} %collective-permute-done.12), channel_id=1, source_target_pairs={{0,8},{2,10},{4,12},{6,14},{8,0},{10,2},{12,4},{14,6},{16,24},{18,... | collective-permute-start | bytes 1572872 | tf_op jit(solution)/shard_map/ppermute | solution.py:582
  47.3 15.2 %collective-permute-start.16 = (bf16[1,256,1024]{2,1,0:T(8,128)(2,1)S(1)}, bf16[1,256,1024]{2,1,0:T(8,128)(2,1)S(1)}, u32[]{:S(2)}, u32[]{:S(2)}) collective-permute-start(bf16[1,256,1024]{2,1,0:T(8,128)(2,1)S(1)} %dynamic-slice_bitcast_fusion), channel_id=1, source_target_pairs={{0,1},{1,0},{2,3},{3,2},{4,5},{5,4},{6,7},{7,6},{8,9},{9,8},{10,11... | collective-permute-start | bytes 1572872 | tf_op jit(solution)/shard_map/ppermute | solution.py:581
  56.4 17.2 %collective-permute-start.6 = (bf16[1,128,1024]{2,1,0:T(8,128)(2,1)S(1)}, bf16[1,128,1024]{2,1,0:T(8,128)(2,1)S(1)}, u32[]{:S(2)}, u32[]{:S(2)}) collective-permute-start(bf16[1,128,1024]{2,1,0:T(8,128)(2,1)S(1)} %bitcast_select_fusion.18), channel_id=1, source_target_pairs={{0,8},{2,10},{4,12},{6,14},{8,0},{10,2},{12,4},{14,6},{16,24},{18,... | collective-permute-start | bytes 786440 | tf_op jit(solution)/shard_map/ppermute | solution.py:582
  60.2 67.6 %collective-permute-start.14 = (bf16[1,128,4096]{2,1,0:T(8,128)(2,1)S(1)}, bf16[1,128,4096]{2,1,0:T(8,128)(2,1)S(1)}, u32[]{:S(2)}, u32[]{:S(2)}) collective-permute-start(bf16[1,128,4096]{2,1,0:T(8,128)(2,1)S(1)} %bitcast_select_fusion.8), channel_id=1, source_target_pairs={{0,4},{2,6},{4,0},{6,2},{8,12},{10,14},{12,8},{14,10},{16,20},{18,... | collective-permute-start | bytes 3145736 | tf_op jit(solution)/shard_map/ppermute | solution.py:582
  61.8 30.2 %collective-permute-start.10 = (bf16[1,128,1024]{2,1,0:T(8,128)(2,1)S(1)}, bf16[1,128,1024]{2,1,0:T(8,128)(2,1)S(1)}, u32[]{:S(2)}, u32[]{:S(2)}) collective-permute-start(bf16[1,128,1024]{2,1,0:T(8,128)(2,1)S(1)} %bitcast_select_fusion.16), channel_id=1, source_target_pairs={{0,4},{2,6},{4,0},{6,2},{8,12},{10,14},{12,8},{14,10},{16,20},{18,... | collective-permute-start | bytes 786440 | tf_op jit(solution)/shard_map/ppermute | solution.py:582
  62.5 37.9 %collective-permute-start.21 = (bf16[3,64,1024]{2,1,0:T(8,128)(2,1)}, bf16[3,64,1024]{2,1,0:T(8,128)(2,1)S(1)}, u32[]{:S(2)}, u32[]{:S(2)}) collective-permute-start(bf16[3,64,1024]{2,1,0:T(8,128)(2,1)} %collective-permute-done.20), channel_id=1, source_target_pairs={{0,4},{2,6},{4,0},{6,2},{8,12},{10,14},{12,8},{14,10},{16,20},{18,... | collective-permute-start | bytes 1179656 | tf_op jit(solution)/shard_map/ppermute | solution.py:582
  71.4 40.2 %collective-permute-start.17 = (bf16[1,256,1024]{2,1,0:T(8,128)(2,1)S(1)}, bf16[1,256,1024]{2,1,0:T(8,128)(2,1)S(1)}, u32[]{:S(2)}, u32[]{:S(2)}) collective-permute-start(bf16[1,256,1024]{2,1,0:T(8,128)(2,1)S(1)} %collective-permute-done.16), channel_id=1, source_target_pairs={{0,4},{2,6},{4,0},{6,2},{8,12},{10,14},{12,8},{14,10},{16,20},{18,... | collective-permute-start | bytes 1572872 | tf_op jit(solution)/shard_map/ppermute | solution.py:582
  73.7 51.6 %collective-permute-start.2 = (bf16[3,128,1024]{2,1,0:T(8,128)(2,1)S(1)}, bf16[3,128,1024]{2,1,0:T(8,128)(2,1)S(1)}, u32[]{:S(2)}, u32[]{:S(2)}) collective-permute-start(bf16[3,128,1024]{2,1,0:T(8,128)(2,1)S(1)} %bitcast_select_fusion.11), channel_id=1, source_target_pairs={{0,4},{2,6},{4,0},{6,2},{8,12},{10,14},{12,8},{14,10},{16,20},{18,... | collective-permute-start | bytes 2359304 | tf_op jit(solution)/shard_map/ppermute | solution.py:582
  92.0 57.9 %collective-permute-start.7 = (bf16[1,256,1024]{2,1,0:T(8,128)(2,1)S(1)}, bf16[1,256,1024]{2,1,0:T(8,128)(2,1)S(1)}, u32[]{:S(2)}, u32[]{:S(2)}) collective-permute-start(bf16[1,256,1024]{2,1,0:T(8,128)(2,1)S(1)} %bitcast_select_fusion.14), channel_id=1, source_target_pairs={{0,2},{2,0},{4,6},{6,4},{8,10},{10,8},{12,14},{14,12},{16,18},{18,... | collective-permute-start | bytes 1572872 | tf_op jit(solution)/shard_map/ppermute | solution.py:582
  100.4 108.9 %collective-permute-start.11 = (bf16[1,256,1024]{2,1,0:T(8,128)(2,1)}, bf16[1,256,1024]{2,1,0:T(8,128)(2,1)}, u32[]{:S(2)}, u32[]{:S(2)}) collective-permute-start(bf16[1,256,1024]{2,1,0:T(8,128)(2,1)} %bitcast_select_fusion.12), channel_id=1, source_target_pairs={{0,2},{2,0},{4,6},{6,4},{8,10},{10,8},{12,14},{14,12},{16,18},{18,... | collective-permute-start | bytes 1572872 | tf_op jit(solution)/shard_map/ppermute | solution.py:582
  111.6 48.0 %collective-permute-start.22 = (bf16[3,128,1024]{2,1,0:T(8,128)(2,1)S(1)}, bf16[3,128,1024]{2,1,0:T(8,128)(2,1)}, u32[]{:S(2)}, u32[]{:S(2)}) collective-permute-start(bf16[3,128,1024]{2,1,0:T(8,128)(2,1)S(1)} %bitcast_select_fusion.10), channel_id=1, source_target_pairs={{0,8},{2,10},{4,12},{6,14},{8,0},{10,2},{12,4},{14,6},{16,24},{18,... | collective-permute-start | bytes 2359304 | tf_op jit(solution)/shard_map/ppermute | solution.py:582
  125.2 22.0 %collective-permute-start.18 = (bf16[1,512,1024]{2,1,0:T(8,128)(2,1)S(1)}, bf16[1,512,1024]{2,1,0:T(8,128)(2,1)S(1)}, u32[]{:S(2)}, u32[]{:S(2)}) collective-permute-start(bf16[1,512,1024]{2,1,0:T(8,128)(2,1)S(1)} %bitcast_select_fusion.6), channel_id=1, source_target_pairs={{0,8},{2,10},{4,12},{6,14},{8,0},{10,2},{12,4},{14,6},{16,24},{18,... | collective-permute-start | bytes 3145736 | tf_op jit(solution)/shard_map/ppermute | solution.py:582
  127.8 38.1 %collective-permute-start.3 = (bf16[3,256,1024]{2,1,0:T(8,128)(2,1)}, bf16[3,256,1024]{2,1,0:T(8,128)(2,1)}, u32[]{:S(2)}, u32[]{:S(2)}) collective-permute-start(bf16[3,256,1024]{2,1,0:T(8,128)(2,1)} %bitcast_select_fusion.5.m_ref), channel_id=1, source_target_pairs={{0,2},{2,0},{4,6},{6,4},{8,10},{10,8},{12,14},{14,12},{16,18},{18,... | collective-permute-start | bytes 4718600 | tf_op jit(solution)/shard_map/ppermute | solution.py:582
  147.3 67.8 %collective-permute-start.15 = (bf16[1,256,4096]{2,1,0:T(8,128)(2,1)}, bf16[1,256,4096]{2,1,0:T(8,128)(2,1)}, u32[]{:S(2)}, u32[]{:S(2)}) collective-permute-start(bf16[1,256,4096]{2,1,0:T(8,128)(2,1)} %bitcast_select_fusion.2), channel_id=1, source_target_pairs={{0,2},{2,0},{4,6},{6,4},{8,10},{10,8},{12,14},{14,12},{16,18},{18,... | collective-permute-start | bytes 6291464 | tf_op jit(solution)/shard_map/ppermute | solution.py:582
  150.7 64.4 %collective-permute-start.19 = (bf16[1,1024,1024]{2,1,0:T(8,128)(2,1)}, bf16[1,1024,1024]{2,1,0:T(8,128)(2,1)}, u32[]{:S(2)}, u32[]{:S(2)}) collective-permute-start(bf16[1,1024,1024]{2,1,0:T(8,128)(2,1)} %bitcast_select_fusion), channel_id=1, source_target_pairs={{0,2},{2,0},{4,6},{6,4},{8,10},{10,8},{12,14},{14,12},{16,18},{18,... | collective-permute-start | bytes 6291464 | tf_op jit(solution)/shard_map/ppermute | solution.py:582
  162.3 99.5 %collective-permute-start.23 = (bf16[3,256,1024]{2,1,0:T(8,128)(2,1)}, bf16[3,256,1024]{2,1,0:T(8,128)(2,1)}, u32[]{:S(2)}, u32[]{:S(2)}) collective-permute-start(bf16[3,256,1024]{2,1,0:T(8,128)(2,1)} %bitcast_select_fusion.4.m_ref), channel_id=1, source_target_pairs={{0,2},{2,0},{4,6},{6,4},{8,10},{10,8},{12,14},{14,12},{16,18},{18,... | collective-permute-start | bytes 4718600 | tf_op jit(solution)/shard_map/ppermute | solution.py:582
  257.1 90.6 %collective-permute-start.49 = (bf16[2,2,2,2,1,256,512]{6,5,3,2,1,0,4:T(8,128)(2,1)}, bf16[2,2,2,2,1,256,512]{6,5,3,2,1,0,4:T(8,128)(2,1)}, u32[]{:S(2)}, u32[]{:S(2)}) collective-permute-start(bf16[2,2,2,2,1,256,512]{6,5,3,2,1,0,4:T(8,128)(2,1)} %bitcast.433), channel_id=1, source_target_pairs={{0,2},{2,0},{4,6},{6,4},{8,10},{10,8},{12,14},{14,12},{16,18},{18,... | collective-permute-start | bytes 12582920 | tf_op jit(solution)/shard_map/ppermute | solution.py:582
  257.3 90.4 %collective-permute-start.50 = (bf16[2,2,2,2,1,64,2048]{6,5,3,2,1,0,4:T(8,128)(2,1)}, bf16[2,2,2,2,1,64,2048]{6,5,3,2,1,0,4:T(8,128)(2,1)}, u32[]{:S(2)}, u32[]{:S(2)}) collective-permute-start(bf16[2,2,2,2,1,64,2048]{6,5,3,2,1,0,4:T(8,128)(2,1)} %bitcast.432), channel_id=1, source_target_pairs={{0,2},{2,0},{4,6},{6,4},{8,10},{10,8},{12,14},{14,12},{16,18},{18,... | collective-permute-start | bytes 12582920 | tf_op jit(solution)/shard_map/ppermute | solution.py:582
  295.9 97.2 %collective-permute-start.64 = (bf16[2,2,2,2,3,64,512]{6,5,4,3,2,1,0:T(8,128)(2,1)}, bf16[2,2,2,2,3,64,512]{6,5,4,3,2,1,0:T(8,128)(2,1)}, u32[]{:S(2)}, u32[]{:S(2)}) collective-permute-start(bf16[2,2,2,2,3,64,512]{6,5,4,3,2,1,0:T(8,128)(2,1)} %bitcast.434), channel_id=1, source_target_pairs={{0,2},{2,0},{4,6},{6,4},{8,10},{10,8},{12,14},{14,12},{16,18},{18,... | collective-permute-start | bytes 9437192 | tf_op jit(solution)/shard_map/ppermute | solution.py:582
  304.5 43.2 %collective-permute-start.51 = (bf16[2,2,2,2,1,64,512]{6,5,3,2,1,0,4:T(8,128)(2,1)}, bf16[2,2,2,2,1,64,512]{6,5,3,2,1,0,4:T(8,128)(2,1)}, u32[]{:S(2)}, u32[]{:S(2)}) collective-permute-start(bf16[2,2,2,2,1,64,512]{6,5,3,2,1,0,4:T(8,128)(2,1)} %bitcast.444), channel_id=1, source_target_pairs={{0,2},{2,0},{4,6},{6,4},{8,10},{10,8},{12,14},{14,12},{16,18},{18,... | collective-permute-start | bytes 3145736 | tf_op jit(solution)/shard_map/ppermute | solution.py:582
  346.9 37.7 %collective-permute-start.25 = (bf16[2,2,2,2,1,64,512]{6,5,3,2,1,0,4:T(8,128)(2,1)}, bf16[2,2,2,2,1,64,512]{6,5,3,2,1,0,4:T(8,128)(2,1)S(1)}, u32[]{:S(2)}, u32[]{:S(2)}) collective-permute-start(bf16[2,2,2,2,1,64,512]{6,5,3,2,1,0,4:T(8,128)(2,1)} %bitcast.443), channel_id=1, source_target_pairs={{0,2},{2,0},{4,6},{6,4},{8,10},{10,8},{12,14},{14,12},{16,18},{18,... | collective-permute-start | bytes 3145736 | tf_op jit(solution)/shard_map/ppermute | solution.py:582
  358.7 88.4 %collective-permute-start.52 = (bf16[2,2,2,1,256,512]{5,4,2,1,0,3:T(8,128)(2,1)}, bf16[2,2,2,1,256,512]{5,4,2,1,0,3:T(8,128)(2,1)}, u32[]{:S(2)}, u32[]{:S(2)}) collective-permute-start(bf16[2,2,2,1,256,512]{5,4,2,1,0,3:T(8,128)(2,1)} %bitcast.436), channel_id=1, source_target_pairs={{0,4},{2,6},{4,0},{6,2},{8,12},{10,14},{12,8},{14,10},{16,20},{18,... | collective-permute-start | bytes 6291464 | tf_op jit(solution)/shard_map/ppermute | solution.py:582
  359.5 89.1 %collective-permute-start.53 = (bf16[2,2,2,1,64,2048]{5,4,2,1,0,3:T(8,128)(2,1)}, bf16[2,2,2,1,64,2048]{5,4,2,1,0,3:T(8,128)(2,1)}, u32[]{:S(2)}, u32[]{:S(2)}) collective-permute-start(bf16[2,2,2,1,64,2048]{5,4,2,1,0,3:T(8,128)(2,1)} %bitcast.435), channel_id=1, source_target_pairs={{0,1},{1,0},{2,3},{3,2},{4,5},{5,4},{6,7},{7,6},{8,9},{9,8},{10,11... | collective-permute-start | bytes 6291464 | tf_op jit(solution)/shard_map/ppermute | solution.py:581
  384.4 13.9 %collective-permute-start.26 = (bf16[2,2,2,2,1,64,512]{6,5,3,2,1,0,4:T(8,128)(2,1)}, bf16[2,2,2,2,1,64,512]{6,5,3,2,1,0,4:T(8,128)(2,1)}, u32[]{:S(2)}, u32[]{:S(2)}) collective-permute-start(bf16[2,2,2,2,1,64,512]{6,5,3,2,1,0,4:T(8,128)(2,1)} %bitcast.442), channel_id=1, source_target_pairs={{0,2},{2,0},{4,6},{6,4},{8,10},{10,8},{12,14},{14,12},{16,18},{18,... | collective-permute-start | bytes 3145736 | tf_op jit(solution)/shard_map/ppermute | solution.py:582
  384.6 15.3 %collective-permute-start.24 = (bf16[2,2,2,2,1,64,512]{6,5,3,2,1,0,4:T(8,128)(2,1)}, bf16[2,2,2,2,1,64,512]{6,5,3,2,1,0,4:T(8,128)(2,1)}, u32[]{:S(2)}, u32[]{:S(2)}) collective-permute-start(bf16[2,2,2,2,1,64,512]{6,5,3,2,1,0,4:T(8,128)(2,1)} %bitcast.441), channel_id=1, source_target_pairs={{0,2},{2,0},{4,6},{6,4},{8,10},{10,8},{12,14},{14,12},{16,18},{18,... | collective-permute-start | bytes 3145736 | tf_op jit(solution)/shard_map/ppermute | solution.py:582
  398.3 69.9 %collective-permute-start.65 = (bf16[2,2,2,3,64,512]{5,4,3,2,1,0:T(8,128)(2,1)}, bf16[2,2,2,3,64,512]{5,4,3,2,1,0:T(8,128)(2,1)}, u32[]{:S(2)}, u32[]{:S(2)}) collective-permute-start(bf16[2,2,2,3,64,512]{5,4,3,2,1,0:T(8,128)(2,1)} %bitcast.437), channel_id=1, source_target_pairs={{0,8},{2,10},{4,12},{6,14},{8,0},{10,2},{12,4},{14,6},{16,24},{18,... | collective-permute-start | bytes 4718600 | tf_op jit(solution)/shard_map/ppermute | solution.py:582
  399.9 46.6 %collective-permute-start.54 = (bf16[2,2,2,1,64,512]{5,4,2,1,0,3:T(8,128)(2,1)}, bf16[2,2,2,1,64,512]{5,4,2,1,0,3:T(8,128)(2,1)}, u32[]{:S(2)}, u32[]{:S(2)}) collective-permute-start(bf16[2,2,2,1,64,512]{5,4,2,1,0,3:T(8,128)(2,1)} %bitcast.176), channel_id=1, source_target_pairs={{0,8},{2,10},{4,12},{6,14},{8,0},{10,2},{12,4},{14,6},{16,24},{18,... | collective-permute-start | bytes 1572872 | tf_op jit(solution)/shard_map/ppermute | solution.py:582
  411.7 44.9 %collective-permute-start.29 = (bf16[2,2,2,1,64,512]{5,4,2,1,0,3:T(8,128)(2,1)}, bf16[2,2,2,1,64,512]{5,4,2,1,0,3:T(8,128)(2,1)S(1)}, u32[]{:S(2)}, u32[]{:S(2)}) collective-permute-start(bf16[2,2,2,1,64,512]{5,4,2,1,0,3:T(8,128)(2,1)} %bitcast.453), channel_id=1, source_target_pairs={{0,4},{2,6},{4,0},{6,2},{8,12},{10,14},{12,8},{14,10},{16,20},{18,... | collective-permute-start | bytes 1572872 | tf_op jit(solution)/shard_map/ppermute | solution.py:582
  446.5 14.8 %collective-permute-start.30 = (bf16[2,2,2,1,64,512]{5,4,2,1,0,3:T(8,128)(2,1)}, bf16[2,2,2,1,64,512]{5,4,2,1,0,3:T(8,128)(2,1)}, u32[]{:S(2)}, u32[]{:S(2)}) collective-permute-start(bf16[2,2,2,1,64,512]{5,4,2,1,0,3:T(8,128)(2,1)} %bitcast.452), channel_id=1, source_target_pairs={{0,1},{1,0},{2,3},{3,2},{4,5},{5,4},{6,7},{7,6},{8,9},{9,8},{10,11... | collective-permute-start | bytes 1572872 | tf_op jit(solution)/shard_map/ppermute | solution.py:581
  447.1 16.8 %collective-permute-start.31 = (bf16[2,2,2,1,64,512]{5,4,2,1,0,3:T(8,128)(2,1)}, bf16[2,2,2,1,64,512]{5,4,2,1,0,3:T(8,128)(2,1)}, u32[]{:S(2)}, u32[]{:S(2)}) collective-permute-start(bf16[2,2,2,1,64,512]{5,4,2,1,0,3:T(8,128)(2,1)} %bitcast.450), channel_id=1, source_target_pairs={{0,8},{2,10},{4,12},{6,14},{8,0},{10,2},{12,4},{14,6},{16,24},{18,... | collective-permute-start | bytes 1572872 | tf_op jit(solution)/shard_map/ppermute | solution.py:582
  448.6 15.3 %collective-permute-start.32 = (bf16[2,2,2,1,64,512]{5,4,2,1,0,3:T(8,128)(2,1)}, bf16[2,2,2,1,64,512]{5,4,2,1,0,3:T(8,128)(2,1)}, u32[]{:S(2)}, u32[]{:S(2)}) collective-permute-start(bf16[2,2,2,1,64,512]{5,4,2,1,0,3:T(8,128)(2,1)} %bitcast.449), channel_id=1, source_target_pairs={{0,4},{2,6},{4,0},{6,2},{8,12},{10,14},{12,8},{14,10},{16,20},{18,... | collective-permute-start | bytes 1572872 | tf_op jit(solution)/shard_map/ppermute | solution.py:582
  457.5 51.2 %collective-permute-start.55 = (bf16[2,2,1,256,512]{4,3,2,1,0:T(8,128)(2,1)}, bf16[2,2,1,256,512]{4,3,2,1,0:T(8,128)(2,1)S(1)}, u32[]{:S(2)}, u32[]{:S(2)}) collective-permute-start(bf16[2,2,1,256,512]{4,3,2,1,0:T(8,128)(2,1)} %bitcast.440), channel_id=1, source_target_pairs={{0,1},{1,0},{2,3},{3,2},{4,5},{5,4},{6,7},{7,6},{8,9},{9,8},{10,11... | collective-permute-start | bytes 3145736 | tf_op jit(solution)/shard_map/ppermute | solution.py:581
  461.3 47.5 %collective-permute-start.56 = (bf16[2,2,1,64,2048]{4,3,2,1,0:T(8,128)(2,1)}, bf16[2,2,1,64,2048]{4,3,2,1,0:T(8,128)(2,1)}, u32[]{:S(2)}, u32[]{:S(2)}) collective-permute-start(bf16[2,2,1,64,2048]{4,3,2,1,0:T(8,128)(2,1)} %bitcast.439), channel_id=1, source_target_pairs={{0,8},{2,10},{4,12},{6,14},{8,0},{10,2},{12,4},{14,6},{16,24},{18,... | collective-permute-start | bytes 3145736 | tf_op jit(solution)/shard_map/ppermute | solution.py:582
  468.0 16.8 %collective-permute-start.36 = (bf16[2,2,1,64,512]{4,3,1,0,2:T(8,128)(2,1)}, bf16[2,2,1,64,512]{4,3,1,0,2:T(8,128)(2,1)S(1)}, u32[]{:S(2)}, u32[]{:S(2)}) collective-permute-start(bf16[2,2,1,64,512]{4,3,1,0,2:T(8,128)(2,1)} %bitcast.460), channel_id=1, source_target_pairs={{0,4},{2,6},{4,0},{6,2},{8,12},{10,14},{12,8},{14,10},{16,20},{18,... | collective-permute-start | bytes 786440 | tf_op jit(solution)/shard_map/ppermute | solution.py:582
  472.5 52.3 %collective-permute-start.66 = (bf16[2,2,3,64,512]{4,3,2,1,0:T(8,128)(2,1)}, bf16[2,2,3,64,512]{4,3,2,1,0:T(8,128)(2,1)}, u32[]{:S(2)}, u32[]{:S(2)}) collective-permute-start(bf16[2,2,3,64,512]{4,3,2,1,0:T(8,128)(2,1)} %bitcast.446), channel_id=1, source_target_pairs={{0,4},{2,6},{4,0},{6,2},{8,12},{10,14},{12,8},{14,10},{16,20},{18,... | collective-permute-start | bytes 2359304 | tf_op jit(solution)/shard_map/ppermute | solution.py:582
  492.9 15.8 %collective-permute-start.57 = (bf16[2,2,1,64,512]{4,3,1,0,2:T(8,128)(2,1)}, bf16[2,2,1,64,512]{4,3,1,0,2:T(8,128)(2,1)S(1)}, u32[]{:S(2)}, u32[]{:S(2)}) collective-permute-start(bf16[2,2,1,64,512]{4,3,1,0,2:T(8,128)(2,1)} %bitcast.456), channel_id=1, source_target_pairs={{0,4},{2,6},{4,0},{6,2},{8,12},{10,14},{12,8},{14,10},{16,20},{18,... | collective-permute-start | bytes 786440 | tf_op jit(solution)/shard_map/ppermute | solution.py:582
  514.7 36.5 %collective-permute-start.58 = (bf16[2,1,256,512]{3,2,0,1:T(8,128)(2,1)}, bf16[2,1,256,512]{3,2,0,1:T(8,128)(2,1)}, u32[]{:S(2)}, u32[]{:S(2)}) collective-permute-start(bf16[2,1,256,512]{3,2,0,1:T(8,128)(2,1)} %bitcast.448), channel_id=1, source_target_pairs={{0,8},{2,10},{4,12},{6,14},{8,0},{10,2},{12,4},{14,6},{16,24},{18,... | collective-permute-start | bytes 1572872 | tf_op jit(solution)/shard_map/ppermute | solution.py:582
  516.5 34.7 %collective-permute-start.59 = (bf16[2,1,64,2048]{3,2,0,1:T(8,128)(2,1)}, bf16[2,1,64,2048]{3,2,0,1:T(8,128)(2,1)}, u32[]{:S(2)}, u32[]{:S(2)}) collective-permute-start(bf16[2,1,64,2048]{3,2,0,1:T(8,128)(2,1)} %bitcast.447), channel_id=1, source_target_pairs={{0,4},{2,6},{4,0},{6,2},{8,12},{10,14},{12,8},{14,10},{16,20},{18,... | collective-permute-start | bytes 1572872 | tf_op jit(solution)/shard_map/ppermute | solution.py:582
  529.7 17.8 %collective-permute-start.67 = (bf16[2,3,64,512]{3,2,1,0:T(8,128)(2,1)}, bf16[2,3,64,512]{3,2,1,0:T(8,128)(2,1)S(1)}, u32[]{:S(2)}, u32[]{:S(2)}) collective-permute-start(bf16[2,3,64,512]{3,2,1,0:T(8,128)(2,1)} %bitcast.455), channel_id=1, source_target_pairs={{0,1},{1,0},{2,3},{3,2},{4,5},{5,4},{6,7},{7,6},{8,9},{9,8},{10,11... | collective-permute-start | bytes 1179656 | tf_op jit(solution)/shard_map/ppermute | solution.py:581
  550.1 19.8 %collective-permute-start.68 = (bf16[3,64,512]{2,1,0:T(8,128)(2,1)}, bf16[3,64,512]{2,1,0:T(8,128)(2,1)S(1)}, u32[]{:S(2)}, u32[]{:S(2)}) collective-permute-start(bf16[3,64,512]{2,1,0:T(8,128)(2,1)} %bitcast.462), channel_id=1, source_target_pairs={{0,16},{2,18},{4,20},{6,22},{8,24},{10,26},{12,28},{14,30},{16,0},... | collective-permute-start | bytes 589832 | tf_op jit(solution)/shard_map/ppermute | solution.py:582
  555.3 24.5 %collective-permute-start.61 = (bf16[1,256,512]{2,1,0:T(8,128)(2,1)}, bf16[1,256,512]{2,1,0:T(8,128)(2,1)S(1)}, u32[]{:S(2)}, u32[]{:S(2)}) collective-permute-start(bf16[1,256,512]{2,1,0:T(8,128)(2,1)} %bitcast.461), channel_id=1, source_target_pairs={{0,16},{2,18},{4,20},{6,22},{8,24},{10,26},{12,28},{14,30},{16,0},... | collective-permute-start | bytes 786440 | tf_op jit(solution)/shard_map/ppermute | solution.py:582
  557.2 22.6 %collective-permute-start.62 = (bf16[1,64,2048]{2,1,0:T(8,128)(2,1)}, bf16[1,64,2048]{2,1,0:T(8,128)(2,1)S(1)}, u32[]{:S(2)}, u32[]{:S(2)}) collective-permute-start(bf16[1,64,2048]{2,1,0:T(8,128)(2,1)} %bitcast.459), channel_id=1, source_target_pairs={{0,16},{2,18},{4,20},{6,22},{8,24},{10,26},{12,28},{14,30},{16,0},... | collective-permute-start | bytes 786440 | tf_op jit(solution)/shard_map/ppermute | solution.py:582
  558.8 21.0 %collective-permute-start.63 = (bf16[1,64,512]{2,1,0:T(8,128)(2,1)}, bf16[1,64,512]{2,1,0:T(8,128)(2,1)S(1)}, u32[]{:S(2)}, u32[]{:S(2)}) collective-permute-start(bf16[1,64,512]{2,1,0:T(8,128)(2,1)} %bitcast.472), channel_id=1, source_target_pairs={{0,16},{2,18},{4,20},{6,22},{8,24},{10,26},{12,28},{14,30},{16,0},... | collective-permute-start | bytes 196616 | tf_op jit(solution)/shard_map/ppermute | solution.py:582
  (70 other events, 650.9 us)

commit v2 on v1

v2 whole, which is shorter than its diff:
```python
import functools
import math

import jax
import jax.numpy as jnp
from jax import lax
from jax.experimental import pallas as pl
from jax.experimental.pallas import tpu as pltpu
from jax.sharding import PartitionSpec as P

H = 8
BF = jnp.bfloat16
F32 = jnp.float32
VMEM = 60 * 1024 * 1024
GELU_C = math.sqrt(2.0 / math.pi)
COST = 1024
Y, CORE, SEG_LEN, MEM_LIVE, COMP_LIVE, PIECE_A, PIECE_B, BITS = range(8)


def nn(a, b):
    return lax.dot_general(a, b, (((1,), (0,)), ((), ())), preferred_element_type=F32)


def nt(a, b):
    return lax.dot_general(a, b, (((1,), (1,)), ((), ())), preferred_element_type=F32)


def tn(a, b):
    return lax.dot_general(a, b, (((0,), (0,)), ((), ())), preferred_element_type=F32)


class Steps:
    def __init__(self, scal):
        self.scal = scal
        self.token = None

    def __call__(self, kernel, name, grid, ins, outs, scratch, args, flops, aliases={}):
        before = [] if self.token is None else [self.token]
        n_in, n_out, extra = len(ins), len(outs), len(before)

        def ordered_kernel(s_ref, *refs):
            rest = refs[n_in + extra:]
            kernel(s_ref, *refs[:n_in], *rest[:n_out], *rest[n_out + 1:])

        anywhere = pl.BlockSpec(memory_space=pl.ANY)
        done = pl.pallas_call(
            ordered_kernel,
            name=name,
            out_shape=[s for s, _ in outs] + [jax.ShapeDtypeStruct((8, 128), F32)],
            grid_spec=pltpu.PrefetchScalarGridSpec(
                num_scalar_prefetch=1,
                grid=grid,
                in_specs=list(ins) + [anywhere] * extra,
                out_specs=[b for _, b in outs] + [anywhere],
                scratch_shapes=scratch,
            ),
            compiler_params=pltpu.CompilerParams(
                vmem_limit_bytes=VMEM, dimension_semantics=("arbitrary",) * len(grid)
            ),
            input_output_aliases=aliases,
            cost_estimate=pl.CostEstimate(flops=COST, bytes_accessed=COST, transcendentals=0),
        )(self.scal, *args, *before)
        *done, self.token = done
        return done


def follow(run, *values):
    anywhere = pl.BlockSpec(memory_space=pl.ANY)
    return run(
        lambda *refs: None, "follow", (1,), [anywhere] * len(values),
        [(jax.ShapeDtypeStruct(v.shape, v.dtype), anywhere) for v in values], [], values, 0,
        {n + 1: n for n in range(len(values))})


def whole(shape):
    return pl.BlockSpec(shape, lambda i, s: (0,) * len(shape))


def out(shape, dtype, block, index):
    return (jax.ShapeDtypeStruct(shape, dtype), pl.BlockSpec(block, index))


def fixed(shape, dtype):
    return out(shape, dtype, shape, lambda i, s: (0,) * len(shape))


def norm_rows(rows):
    centred = rows - jnp.mean(rows, axis=-1, keepdims=True)
    spread = jnp.mean(centred * centred, axis=-1, keepdims=True)
    scale = lax.rsqrt(spread + 1e-05)
    return centred * scale, scale


def norm_back(grad, gain, unit, scale):
    g = grad * gain
    inner = jnp.mean(g * unit, axis=-1, keepdims=True)
    return scale * (g - jnp.mean(g, axis=-1, keepdims=True) - unit * inner)


def place(dst, s_ref, own, mine, theirs, cols=slice(None)):
    half, quarter = own.shape[-2], mine.shape[-2]
    y, core = s_ref[Y], s_ref[CORE]
    base = (1 - y) * half
    at = lambda start, size: pl.ds(pl.multiple_of(start, quarter), size)
    dst[at(y * half, half), cols] = own[:, cols]
    dst[at(base + core * quarter, quarter), cols] = mine[...]
    dst[at(base + (1 - core) * quarter, quarter), cols] = theirs[...]


def pack_first_kernel(s_ref, rel, k, v, qa, qb, o_rel, o_a, o_b):
    width = rel.shape[-1]
    o_rel[...] = rel[...]
    o_a[0, :, :width] = k[0, 0]
    o_a[0, :, width:] = qa[0, 0]
    o_b[0, :, :width] = v[0, 0]
    o_b[0, :, width:] = qb[0, 0]


def pack_rest_kernel(s_ref, c0, c1, c2, ow, up, down, o_c, o_d, o_up, o_down):
    o_c[0] = c0[0, 0]
    o_c[1] = c1[0, 0]
    o_d[0] = c2[0, 0]
    o_d[1] = ow[0]
    o_up[...] = up[...]
    o_down[...] = down[...]


def eighths(a):
    lead = a.shape[:-2]
    return a.reshape(lead + (8, a.shape[-2] // 8, a.shape[-1]))


def part_of(a, where, n=0, cols=1, c=0):
    block = (1,) * (a.ndim - 2) + (a.shape[-2], a.shape[-1] // cols)
    if a.ndim == 3:
        return pl.BlockSpec(block, lambda i, s: (s[where], 0, c))
    return pl.BlockSpec(block, lambda i, s: (n, s[where], 0, c))


def pack_first(run, w_qkv, w_rel):
    qkv, rel = eighths(w_qkv), eighths(w_rel)
    part, width = rel.shape[1:]
    return run(
        pack_first_kernel, "pack_first", (1,),
        [part_of(rel, PIECE_A), part_of(qkv, PIECE_A, 1), part_of(qkv, PIECE_B, 2),
         part_of(qkv, PIECE_A, 0, 2, 0), part_of(qkv, PIECE_B, 0, 2, 1)],
        [fixed((1, part, width), BF), fixed((1, part, width * 3 // 2), BF),
         fixed((1, part, width * 3 // 2), BF)],
        [], (rel, qkv, qkv, qkv, qkv), 0)


def pack_rest(run, w_out, w_up, w_down, w_comp):
    comp, ow, up, down = eighths(w_comp), eighths(w_out), eighths(w_up), eighths(w_down)
    part, width = ow.shape[1:]
    return run(
        pack_rest_kernel, "pack_rest", (1,),
        [part_of(comp, PIECE_A, 0), part_of(comp, PIECE_A, 1), part_of(comp, PIECE_B, 2),
         part_of(ow, PIECE_B), part_of(up, PIECE_A), part_of(down, PIECE_B)],
        [fixed((2, part, width), BF), fixed((2, part, width), BF),
         fixed((1,) + up.shape[1:], BF), fixed((1,) + down.shape[1:], BF)],
        [], (comp, comp, comp, ow, up, down), 0)


def ordered(mine, theirs, bit):
    n, rows, cols = mine.shape
    at = lax.broadcasted_iota(jnp.int32, (n, 2, rows, cols), 1)
    return jnp.where(at == bit, mine[:, None], theirs[:, None]).reshape(n, 2 * rows, cols)


def normed_kernel(s_ref, d_ref, m_ref, t_ref, g_ref, x_ref):
    i = pl.program_id(0)
    for n, ref in enumerate((d_ref, m_ref, t_ref)):
        @pl.when(i // 2 == n)
        def _(ref=ref):
            x_ref[...] = (norm_rows(ref[...].astype(F32))[0] * g_ref[...]).astype(BF)


def norm_hidden(run, distant, recent, current, gain):
    mem, width = recent.shape
    blk = mem // 2
    part = lambda n: pl.BlockSpec((blk, width), lambda i, s: (jnp.clip(i - 2 * n, 0, 1), 0))
    return run(
        normed_kernel, "norm_hidden", (6,),
        [part(0), part(1), part(2), whole(gain.shape)],
        [out((3 * mem, width), BF, (blk, width), lambda i, s: (i, 0))],
        [], (distant, recent, current, gain), 0)[0]


def constants_kernel(s_ref, m_ref, sa_ref, ca_ref, sb_ref, cb_ref, tab_ref, gr_ref, wide_ref,
                     *, groups):
    i = pl.program_id(0)
    blk, width = tab_ref.shape
    half = width // 2
    fine = sb_ref.shape[0]
    for n in range(blk // fine):
        rows = slice(n * fine, (n + 1) * fine)
        a = i * (blk // fine) + n
        sa, ca = sa_ref[pl.ds(a, 1)], ca_ref[pl.ds(a, 1)]
        tab_ref[rows, :half] = (sa * cb_ref[...] + ca * sb_ref[...]).astype(BF)
        tab_ref[rows, half:] = (ca * cb_ref[...] - sa * sb_ref[...]).astype(BF)

    @pl.when(i == 0)
    def _():
        mem = m_ref.shape[0]
        lanes = wide_ref.shape[2]
        count = gr_ref.shape[1]
        live = lax.broadcasted_iota(jnp.int32, (count, 1), 0) < groups
        for n in range(width // lanes):
            cols = slice(n * lanes, (n + 1) * lanes)
            wide_ref[n, :mem] = m_ref[:, cols].astype(F32)
            wide_ref[n, mem:] = jnp.zeros((wide_ref.shape[1] - mem, lanes), F32)
            for t in range(3):
                rows = jnp.where(live, wide_ref[n, pl.ds(t, count, stride=3)], 0.0)
                gr_ref[t, :, cols] = rows.astype(BF)


def constants(run, recent, angles, groups):
    mem, width = recent.shape
    keys = 3 * mem
    blk = 512
    padded = groups + (-groups) % 64
    ins = (recent,) + angles
    return run(
        functools.partial(constants_kernel, groups=groups), "constants", (keys // blk,),
        [whole(a.shape) for a in ins],
        [out((keys, width), BF, (blk, width), lambda i, s: (i, 0)),
         fixed((3, padded, width), BF)],
        [pltpu.VMEM((width // 128, 3 * padded, 128), F32)], ins, 0)


def qkv_kernel(s_ref, x_ref, o_ref, am_ref, at_ref, bm_ref, bt_ref, bc_ref, bp_ref, kv_ref,
               qc_ref, qp_ref, pr_ref, w_ref, *, scale):
    i = pl.program_id(0)
    rows, width = x_ref.shape
    seg = qc_ref.shape[0]
    blk = 256
    lo, hi = slice(0, width // 2), slice(width // 2, width)
    own, dst = o_ref.at[0], w_ref.at[0]

    @pl.when(i == 0)
    def _():
        place(dst, s_ref, own, am_ref.at[0, :, :width], at_ref.at[0, :, :width])

    @pl.when(i == 1)
    def _():
        place(dst, s_ref, own, bm_ref.at[0, :, :width], bt_ref.at[0, :, :width])

    @pl.when(i == 2)
    def _():
        place(dst, s_ref, own, am_ref.at[0, :, width:], at_ref.at[0, :, width:], lo)
        place(dst, s_ref, own, bm_ref.at[0, :, width:], bt_ref.at[0, :, width:], hi)

    @pl.when(i < 2)
    def _():
        def some(n, _):
            at = pl.ds(pl.multiple_of(n * blk, blk), blk)
            kv_ref[0, at] = nn(x_ref[at], dst[...]).astype(BF)
            return 0

        lax.fori_loop(0, rows // blk, some, 0)

    @pl.when(i == 2)
    def _():
        for n in range(seg // blk):
            at = slice(n * blk, (n + 1) * blk)
            q = nn(x_ref[rows - seg + n * blk:rows - seg + (n + 1) * blk], dst[...])
            qc_ref[at] = ((q + bc_ref[...]) * scale).astype(BF)
            qp_ref[at] = ((q + bp_ref[...]) * scale).astype(BF)
            pr_ref[at] = (q * scale).astype(BF)


def project_qkv(run, normed, w_qkv, a_parts, b_parts, bias_content, bias_position, seg, scale):
    rows, width = normed.shape
    turn = lambda i, s: ((i + 1) % 3, 0, 0)
    parts = a_parts + b_parts
    return run(
        functools.partial(qkv_kernel, scale=scale), "project_qkv", (3,),
        [whole((rows, width)), pl.BlockSpec((1, width // 2, width), turn)]
        + [whole(p.shape) for p in parts] + [whole((1, width)), whole((1, width))],
        [out((2, rows, width), BF, (1, rows, width), lambda i, s: (jnp.minimum(i, 1), 0, 0)),
         fixed((seg, width), BF), fixed((seg, width), BF), fixed((seg, width), BF),
         out((3, width, width), BF, (1, width, width), turn)],
        [], (normed, w_qkv) + parts + (bias_content.reshape(1, -1), bias_position.reshape(1, -1)),
        2 * (2 * rows + seg) * width * width)


def position_kernel(s_ref, x_ref, o_ref, m_ref, t_ref, p_ref, w_ref):
    @pl.when(pl.program_id(0) == 0)
    def _():
        place(w_ref, s_ref, o_ref, m_ref.at[0], t_ref.at[0])

    p_ref[...] = nn(x_ref[...], w_ref[...]).astype(BF)


def project_position(run, table, own, parts):
    rows, width = table.shape
    blk = 512
    return run(
        position_kernel, "project_position", (rows // blk,),
        [pl.BlockSpec((blk, width), lambda i, s: (i, 0)), whole(own.shape)]
        + [whole(p.shape) for p in parts],
        [out((rows, width), BF, (blk, width), lambda i, s: (i, 0))],
        [pltpu.VMEM((width, width), BF)], (table, own) + parts,
        2 * rows * width * width)[0]


RB = 256


def flip_matrix():
    return (lax.broadcasted_iota(jnp.int32, (RB, RB), 0)
            + lax.broadcasted_iota(jnp.int32, (RB, RB), 1) == RB - 1).astype(BF)


def attention_kernel(s_ref, qc_ref, qp_ref, k_ref, v_ref, pos_ref, p_ref, mix_ref, bias_ref,
                     *, comp, mem):
    seg, keys = qc_ref.shape[0], k_ref.shape[1]
    start = comp + mem

    @pl.when(pl.program_id(0) == 0)
    def _():
        mem_live, comp_live = s_ref[MEM_LIVE], s_ref[COMP_LIVE]
        col = lax.broadcasted_iota(jnp.int32, bias_ref.shape, 1)
        row = lax.broadcasted_iota(jnp.int32, bias_ref.shape, 0)
        live = ((col >= comp - comp_live) & (col < comp)) | (
            (col >= start - mem_live) & (col - start <= row))
        bias_ref[...] = jnp.where(live, 0.0, -1e30)

    flip = flip_matrix()
    for r in range(seg // RB):
        width = start + RB * (r + 1)
        rows = slice(r * RB, (r + 1) * RB)
        content = nt(qc_ref[rows], k_ref[0, :width])
        rel = nt(qp_ref[rows], pos_ref[keys - width:])
        rel = pltpu.roll(rel, width - RB + 1, 1, stride=1, stride_axis=0)
        masked = content + rel + bias_ref[rows, :width]
        top = jnp.max(masked, axis=-1, keepdims=True)
        weights = jnp.exp(masked - top)
        probs = (weights * (1.0 / jnp.sum(weights, axis=-1, keepdims=True))).astype(BF)
        mix_ref[rows] = nn(probs, v_ref[0, :width]).astype(BF)
        p_ref[0, rows, :width] = nn(flip, probs).astype(BF)


def attention(run, qc, qp, kv, pos, comp, mem, half):
    seg, width = qc.shape
    keys = kv.shape[1]
    dh = width // H
    n = H // 2
    first = half * n
    q_spec = pl.BlockSpec((seg, dh), lambda h, s: (0, h + first))
    of = lambda m: pl.BlockSpec((1, keys, dh), lambda h, s: (m, 0, h + first))
    return run(
        functools.partial(attention_kernel, comp=comp, mem=mem), "attention", (n,),
        [q_spec, q_spec, of(0), of(1), pl.BlockSpec((keys, dh), lambda h, s: (0, h + first))],
        [out((n, seg, keys), BF, (1, seg, keys), lambda h, s: (h, 0, 0)),
         out((seg, width // 2), BF, (seg, dh), lambda h, s: (0, h))],
        [pltpu.VMEM((seg, keys), F32)], (qc, qp, kv, kv, pos), 16 * seg * keys * width)


def attention_back_kernel(s_ref, p_ref, gm_ref, qc_ref, qp_ref, k_ref, v_ref, pos_ref, gq_ref,
                          gk_ref, gv_ref, gp_ref, gc_ref, gb_ref, gs_ref, sh_ref, pr_ref, rev_ref,
                          *, start, scale):
    seg, keys = qc_ref.shape[0], k_ref.shape[1]
    flip = flip_matrix()
    sum_c = jnp.zeros((1, gc_ref.shape[1]), F32)
    sum_p = jnp.zeros((1, gc_ref.shape[1]), F32)
    for r in range(seg // RB):
        width = start + RB * (r + 1)
        rows = slice(r * RB, (r + 1) * RB)
        for n, ref in enumerate((gm_ref, qc_ref, qp_ref)):
            rev_ref[n, rows] = nn(flip, ref[rows]).astype(BF)
        low = p_ref[0, rows, :width]
        probs = low.astype(F32)
        weighted = probs * nt(rev_ref[0, rows], v_ref[0, :width])
        scores = (weighted - probs * jnp.sum(weighted, axis=-1, keepdims=True))
        low_scores = scores.astype(BF)
        moved = pltpu.roll(scores, 0, 1, stride=1, stride_axis=0).astype(BF)
        gs_ref[rows, :width] = low_scores
        sh_ref[rows, keys - width:] = moved
        pr_ref[rows, :width] = low
        if width < keys:
            gs_ref[rows, width:] = jnp.zeros((RB, keys - width), BF)
            pr_ref[rows, width:] = jnp.zeros((RB, keys - width), BF)
            sh_ref[rows, : keys - width] = jnp.zeros((RB, keys - width), BF)
        grad_c = nn(low_scores, k_ref[0, :width])
        grad_p = nn(moved, pos_ref[keys - width:])
        sum_c += jnp.sum(grad_c, axis=0, keepdims=True)
        sum_p += jnp.sum(grad_p, axis=0, keepdims=True)
        gq_ref[rows] = nn(flip, ((grad_c + grad_p) * scale).astype(BF)).astype(BF)
    gc_ref[...] = sum_c * scale
    gb_ref[...] = sum_p * scale
    gv_ref[...] = tn(rev_ref[0], pr_ref[...]).astype(BF)
    gk_ref[...] = tn(rev_ref[1], gs_ref[...]).astype(BF)
    gp_ref[...] = tn(rev_ref[2], sh_ref[...]).astype(BF)


def attention_back(run, probs, gm, qc, qp, kv, pos, start, scale, half):
    seg, width = qc.shape
    keys = kv.shape[1]
    dh = width // H
    n = H // 2
    first = half * n
    q_spec = pl.BlockSpec((seg, dh), lambda h, s: (0, h + first))
    of = lambda m: pl.BlockSpec((1, keys, dh), lambda h, s: (m, 0, h + first))
    turned = lambda: out((width // 2, keys), BF, (dh, keys), lambda h, s: (h, 0))
    sums = lambda: out((1, width // 2), F32, (1, dh), lambda h, s: (0, h))
    big = pltpu.VMEM((seg, keys), BF)
    return run(
        functools.partial(attention_back_kernel, start=start, scale=scale), "attention_back", (n,),
        [pl.BlockSpec((1, seg, keys), lambda h, s: (h, 0, 0)), q_spec, q_spec, q_spec,
         of(0), of(1), pl.BlockSpec((keys, dh), lambda h, s: (0, h + first))],
        [out((seg, width // 2), BF, (seg, dh), lambda h, s: (0, h)), turned(), turned(), turned(),
         sums(), sums()],
        [big, big, big, pltpu.VMEM((3, seg, dh), BF)], (probs[half], gm, qc, qp, kv, kv, pos),
        12 * seg * keys * width)


def mixed_kernel(s_ref, tok_ref, a_ref, b_ref, o_ref, m_ref, t_ref, g_ref, att_ref, sec_ref, w_ref):
    @pl.when(pl.program_id(0) == 0)
    def _():
        place(w_ref, s_ref, o_ref, m_ref.at[1], t_ref.at[1])

    mid = a_ref.shape[1]
    attended = (tok_ref[...].astype(F32) + nn(a_ref[...], w_ref[:mid])
                + nn(b_ref[...], w_ref[mid:]))
    att_ref[...] = attended
    sec_ref[...] = (norm_rows(attended)[0] * g_ref[...]).astype(BF)


def mix_out(run, tokens, mixed, own, parts, gain):
    seg, width = tokens.shape
    blk = 256
    row = pl.BlockSpec((blk, width), lambda i, s: (i, 0))
    side = pl.BlockSpec((blk, width // 2), lambda i, s: (i, 0))
    return run(
        mixed_kernel, "mix_out", (seg // blk,),
        [row, side, side, whole(own.shape)] + [whole(p.shape) for p in parts] + [whole((1, width))],
        [out((seg, width), F32, (blk, width), lambda i, s: (i, 0)),
         out((seg, width), BF, (blk, width), lambda i, s: (i, 0)),
         fixed((width, width), BF)],
        [], (tokens,) + mixed + (own,) + parts + (gain,), 2 * seg * width * width)


def part_shape(rows, cols, n_dp, taps, cut=1):
    return (2, n_dp // (2 * cut), taps, rows // n_dp, cols // 2)


def low_or_wide(chunk):
    return BF if chunk % 16 == 0 else F32


def by_core(buf, values, core):
    pairs, _, chunk, cols = buf.shape
    buf[...] = values.astype(buf.dtype).reshape(pairs, 2, chunk, cols)
    pick = lambda c: buf[:, c].reshape(pairs * chunk, cols)
    return jnp.concatenate([pick(core), pick(1 - core)], axis=0).astype(BF)


def put(keep, send, values):
    half = values.shape[0] // 2
    shape = keep.shape[:-1] + (values.shape[1],)
    keep[...] = values[:half].reshape(shape).astype(BF)
    send[...] = values[half:].reshape(shape).astype(BF)


def ffn_kernel(s_ref, sec_ref, cot_ref, att_ref, uo_ref, um_ref, ut_ref, do_ref, dm_ref, dt_ref,
               b_ref, g_ref, wo_ref, out_ref, gatt_ref, gm_ref, uk_ref, us_ref, dk_ref, ds_ref,
               gb_ref, gg_ref, gout_ref, turn_ref, wu_ref, wd_ref, acc_ref, gsec_ref, ubuf, dbuf):
    i, n = pl.program_id(0), pl.num_programs(0)
    y, core = s_ref[Y], s_ref[CORE]

    @pl.when(i == 0)
    def _():
        row = lax.broadcasted_iota(jnp.int32, cot_ref.shape, 0)
        live = jnp.where(row < s_ref[SEG_LEN], cot_ref[...], jnp.zeros((), BF))
        gout_ref[...] = live
        turn_ref[...] = by_core(dbuf, live.T, core)
        acc_ref[...] = att_ref[...]
        gsec_ref[...] = jnp.zeros_like(gsec_ref)

    place(wu_ref, s_ref, uo_ref, um_ref.at[0], ut_ref.at[0])
    half = i // (n // 2)
    side = (i % (n // 2)) // (n // 4)

    @pl.when(half == y)
    def _():
        wd_ref[...] = do_ref[...]

    @pl.when((half != y) & (side == core))
    def _():
        wd_ref[...] = dm_ref[0]

    @pl.when((half != y) & (side != core))
    def _():
        wd_ref[...] = dt_ref[0]

    second, gout = sec_ref[...], gout_ref[...]
    v = nn(second, wu_ref[...]) + b_ref[...]
    square = v * v
    gate = 0.5 + 0.5 * jnp.tanh(v * (GELU_C + (GELU_C * 0.044715) * square))
    act = (v * gate).astype(BF)
    slope = gate + (gate - gate * gate) * v * (2 * GELU_C + (6 * GELU_C * 0.044715) * square)
    acc_ref[...] += nn(act, wd_ref[...])
    grad_inner = nt(gout, wd_ref[...]) * slope
    low = grad_inner.astype(BF)
    gb_ref[...] = jnp.sum(low.astype(F32), axis=0, keepdims=True)
    gsec_ref[...] += nt(low, wu_ref[...])
    put(dk_ref.at[0, :, 0], ds_ref.at[0, :, 0], nn(turn_ref[...], act))
    part = nn(by_core(ubuf, low.T, core), second)
    width = part.shape[1] // 2
    for side in range(2):
        put(uk_ref.at[side, :, 0], us_ref.at[side, :, 0], part[:, side * width:(side + 1) * width])

    @pl.when(i == n - 1)
    def _():
        out_ref[...] = acc_ref[...].astype(BF)
        unit, scale = norm_rows(att_ref[...])
        grad = gsec_ref[...]
        gg_ref[...] = jnp.sum(grad * unit, axis=0, keepdims=True)
        gatt = norm_back(grad, g_ref[...], unit, scale) + gout_ref[...].astype(F32)
        gatt_ref[...] = gatt
        gm_ref[...] = nt(gatt.astype(BF), wo_ref[...]).astype(BF)


def feed_forward(run, second, cotangent, attended, w_up, up_parts, w_down, down_parts, bias_up,
                 gain, w_out, n_dp):
    seg, width = second.shape
    inner = bias_up.shape[1]
    n = 8
    blk = inner // n
    um, ut = up_parts
    dm, dt = down_parts
    uch, dch = inner // n_dp, width // n_dp
    pairs = blk // (2 * uch)
    col = lambda a: pl.BlockSpec((a.shape[0], blk), lambda i, s: (0, i))
    col3 = lambda a: pl.BlockSpec((1, a.shape[1], blk), lambda i, s: (0, 0, i))
    row3 = pl.BlockSpec((1, blk, width), lambda i, s: (0, i % (n // 4), 0))
    up_shape = part_shape(inner, width, n_dp, 1)
    down_shape = part_shape(width, inner, n_dp, n // 2)[:-1] + (blk,)
    up_out = lambda: out(up_shape, BF, (2, pairs, 1, uch, width // 2),
                         lambda i, s: (0, i, 0, 0, 0))
    down_out = lambda: out(down_shape, BF, (1, n_dp // 2, 1, dch, blk),
                           lambda i, s: (i // (n // 2), 0, i % (n // 2), 0, 0))
    full = (seg, width)
    return run(
        ffn_kernel, "feed_forward", (n,),
        [whole(full), whole(full), whole(full), col(w_up), col3(um), col3(ut),
         pl.BlockSpec((blk, width), lambda i, s: (i % (n // 2), 0)), row3, row3,
         pl.BlockSpec((1, blk), lambda i, s: (0, i)), whole((1, width)), whole((width, width))],
        [fixed(full, BF), fixed(full, F32), fixed(full, BF), up_out(), up_out(), down_out(),
         down_out(), out((1, inner), F32, (1, blk), lambda i, s: (0, i)), fixed((1, width), F32)],
        [pltpu.VMEM(full, BF), pltpu.VMEM((width, seg), BF), pltpu.VMEM((width, blk), BF),
         pltpu.VMEM((blk, width), BF), pltpu.VMEM(full, F32), pltpu.VMEM(full, F32),
         pltpu.VMEM((pairs, 2, uch, seg), low_or_wide(uch)),
         pltpu.VMEM((n_dp // 2, 2, dch, seg), low_or_wide(dch))],
        (second, cotangent, attended, w_up, um, ut, w_down, dm, dt, bias_up, gain, w_out),
        12 * seg * width * inner)


def grads_kernel(s_ref, gk_ref, gv_ref, gp_ref, gq_ref, ga_ref, x_ref, tab_ref, ma_ref, mb_ref, w_ref,
                 ak_ref, ax_ref, bk_ref, bx_ref, gg_ref, k_s, v_s, p_s, q_s, o_s, big, small):
    core = s_ref[CORE]
    rows = x_ref.shape[0]
    seg = gq_ref.shape[0]

    @pl.when(pl.program_id(0) == 0)
    def _():
        k_s[...] = by_core(big, gk_ref[...], core)
        v_s[...] = by_core(big, gv_ref[...], core)
        p_s[...] = by_core(big, gp_ref[...], core)
        q_s[...] = by_core(small, gq_ref[...].T, core)
        o_s[...] = by_core(small, ga_ref[...].astype(BF).T, core)

    x = x_ref[...]
    pairs, _, chunk, _ = small.shape
    n = pairs * chunk

    def both(a, b, tap, values):
        put(a.at[0, :, tap], b.at[0, :, tap], values)

    def gain(values, m):
        turned = w_ref[m].T.astype(F32)
        whole_ = turned.reshape(pairs, 2, chunk, turned.shape[1])
        even, odd = whole_[:, 0].reshape(n, -1), whole_[:, 1].reshape(n, -1)
        first = jnp.where(core == 0, even, odd)
        last = jnp.where(core == 0, odd, even)
        return (jnp.sum(values[:n] * first, axis=0, keepdims=True)
                + jnp.sum(values[n:] * last, axis=0, keepdims=True))

    part = nn(k_s[...], x)
    both(ak_ref, ax_ref, 0, part)
    total = gain(part, 1)
    part = nn(v_s[...], x)
    both(ak_ref, ax_ref, 1, part)
    total += gain(part, 2)
    part = nn(q_s[...], x[rows - seg:])
    both(bk_ref, bx_ref, 0, part)
    total += gain(part, 0)
    both(bk_ref, bx_ref, 1, nn(p_s[...], tab_ref[...]))
    gg_ref[...] = total
    i, n = pl.program_id(0), pl.num_programs(0)

    @pl.when(i < n // 2)
    def _():
        both(bk_ref, bx_ref, 2, nn(o_s[...], ma_ref[...]))

    @pl.when(i >= n // 2)
    def _():
        both(bk_ref, bx_ref, 2, nn(o_s[...], mb_ref[...]))


def projection_grads(run, turned, gq, gatt, normed, table, mixed, w, n_dp, half):
    rows, width = normed.shape
    seg = gq.shape[0]
    blk = 256
    chunk = width // n_dp
    mid = width // 2
    gk, gv, gpos = turned
    count = mid // blk
    col = lambda r: pl.BlockSpec((r, blk), lambda i, s: (0, i))
    shape = lambda taps: part_shape(width, width, n_dp, taps, 2)
    half_of = lambda taps: out(shape(taps), BF, (1,) + shape(taps)[1:4] + (blk,),
                               lambda i, s: (i // count, 0, 0, 0, i % count))
    side = pl.BlockSpec((seg, blk), lambda i, s: (0, i % count))
    kind = low_or_wide(chunk)
    pairs = mid // (2 * chunk)
    return run(
        grads_kernel, "projection_grads", (width // blk,),
        [whole(gk.shape), whole(gk.shape), whole(gk.shape), whole(gq.shape),
         pl.BlockSpec((seg, mid), lambda i, s: (0, half)), col(rows), col(rows), side, side,
         pl.BlockSpec((3, blk, mid), lambda i, s: (0, i, half))],
        [half_of(2), half_of(2), half_of(3), half_of(3),
         out((1, width), F32, (1, blk), lambda i, s: (0, i))],
        [pltpu.VMEM((mid, rows), BF)] * 3 + [pltpu.VMEM((mid, seg), BF)] * 2
        + [pltpu.VMEM((pairs, 2, chunk, rows), kind), pltpu.VMEM((pairs, 2, chunk, seg), kind)],
        (gk, gv, gpos, gq, gatt, normed, table) + mixed + (w,),
        (3 * rows + 2 * seg) * width * width)


def grad_tokens_kernel(s_ref, ka_ref, kb_ref, va_ref, vb_ref, qa_ref, qb_ref, tok_ref, ga_ref,
                       w_ref, g_ref, gt_ref, acc_ref):
    i = pl.program_id(0)
    mid = w_ref.shape[2] // 2
    left, right = w_ref[0, :, :mid], w_ref[0, :, mid:]

    @pl.when(i == 0)
    def _():
        acc_ref[...] = nn(left, ka_ref[...]) + nn(right, kb_ref[...])

    @pl.when(i == 1)
    def _():
        acc_ref[...] += nn(left, va_ref[...]) + nn(right, vb_ref[...])

    @pl.when(i == 2)
    def _():
        total = (acc_ref[...] + nt(left, qa_ref[...]) + nt(right, qb_ref[...])).T
        unit, scale = norm_rows(tok_ref[...].astype(F32))
        gt_ref[...] = (ga_ref[...] + norm_back(total, g_ref[...], unit, scale)).astype(BF)


def grad_tokens(run, gk, gv, gq, tokens, grad_attended, w, gain):
    seg, width = tokens.shape
    rows = gk[0].shape[1]
    late = pl.BlockSpec((width // 2, seg), lambda i, s: (0, rows // seg - 1))
    side = whole((seg, width // 2))
    return run(
        grad_tokens_kernel, "grad_tokens", (3,),
        [late] * 4 + [side] * 2 + [whole((seg, width)), whole((seg, width)),
         pl.BlockSpec((1, width, width), lambda i, s: ((i + 1) % 3, 0, 0)), whole((1, width))],
        [fixed((seg, width), BF)], [pltpu.VMEM((width, seg), F32)],
        tuple(gk) + tuple(gv) + tuple(gq) + (tokens, grad_attended, w, gain),
        6 * seg * width * width)[0]


def squeeze_kernel(s_ref, gr_ref, o_ref, am_ref, at_ref, bm_ref, bt_ref, w_ref, g_ref, sq_ref,
                   low_ref, k_ref, v_ref):
    y, core = s_ref[Y], s_ref[CORE]
    half, quarter = o_ref.shape[1], am_ref.shape[1]
    base = (1 - y) * half
    total = jnp.zeros(sq_ref.shape, F32)
    for t in range(3):
        m_ref, t_ref, n = (am_ref, at_ref, t) if t < 2 else (bm_ref, bt_ref, 0)
        at = lambda off, size: gr_ref[t, :, pl.ds(pl.multiple_of(off, quarter), size)]
        total += nn(at(y * half, half), o_ref[t])
        total += nn(at(base + core * quarter, quarter), m_ref[n])
        total += nn(at(base + (1 - core) * quarter, quarter), t_ref[n])
    sq_ref[...] = total
    low_ref[...] = total.astype(BF)
    unit = (norm_rows(total)[0] * g_ref[...]).astype(BF)
    k_ref[...] = nn(unit, w_ref[1]).astype(BF)
    v_ref[...] = nn(unit, w_ref[2]).astype(BF)


def squeeze(run, groups, own, a_parts, b_parts, w, gain):
    _, rows, width = groups.shape
    parts = a_parts + b_parts
    shape = (rows, width)
    return run(
        squeeze_kernel, "squeeze", (1,),
        [whole(groups.shape), whole(own.shape)] + [whole(p.shape) for p in parts]
        + [whole(w.shape), whole((1, width))],
        [fixed(shape, F32), fixed(shape, BF), fixed(shape, BF), fixed(shape, BF)], [],
        (groups, own) + parts + (w, gain), 10 * rows * width * width)


def masked_softmax(scores, live):
    masked = jnp.where(live, scores, -1e30)
    weights = jnp.exp(masked - jnp.max(masked, axis=-1, keepdims=True))
    return weights * (1.0 / jnp.sum(weights, axis=-1, keepdims=True))


def recon_kernel(s_ref, pr_ref, ok_ref, ov_ref, ck_ref, cv_ref, gk_ref, gv_ref):
    seg_len = s_ref[SEG_LEN]
    count = seg_len // 3
    probe = pr_ref[...]
    seg, mem, comp = probe.shape[0], ok_ref.shape[1], ck_ref.shape[0]
    old_live = lax.broadcasted_iota(jnp.int32, (1, mem), 1) < 3 * count
    old = nn(masked_softmax(nt(probe, ok_ref[0]), old_live).astype(BF), ov_ref[0])
    live = lax.broadcasted_iota(jnp.int32, (1, comp), 1) < count
    probs = masked_softmax(nt(probe, ck_ref[...]), live)
    low = probs.astype(BF)
    gap = nn(low, cv_ref[...]) - old
    row = lax.broadcasted_iota(jnp.int32, gap.shape, 0)
    grad_out = (jnp.where(row < seg_len, gap, 0.0) * (2.0 / seg_len.astype(F32))).astype(BF)
    gv_ref[...] = tn(low, grad_out).astype(BF)
    weighted = probs * nt(grad_out, cv_ref[...])
    scores = (weighted - probs * jnp.sum(weighted, axis=-1, keepdims=True)).astype(BF)
    gk_ref[...] = tn(scores, probe).astype(BF)


def reconstruct(run, probe, kv, ck, cv, mem):
    seg, width = probe.shape
    rows = ck.shape[0]
    dh = width // H
    at = lambda n, b: pl.BlockSpec((n, dh), lambda h, s: (b, h))
    old = lambda m: pl.BlockSpec((1, mem, dh), lambda h, s: (m, 1, h))
    grads = lambda: out((rows, width), BF, (rows, dh), lambda h, s: (0, h))
    return run(
        recon_kernel, "reconstruct", (H,),
        [at(seg, 0), old(0), old(1), at(rows, 0), at(rows, 0)], [grads(), grads()], [],
        (probe, kv, kv, ck, cv), 4 * seg * width * mem + 12 * seg * width * rows)


def grad_comp_kernel(s_ref, sq_ref, gk_ref, gv_ref, w_ref, g_ref, gr_ref, k_ref, x_ref, low_ref, buf):
    @pl.when(pl.program_id(0) == 0)
    def _():
        grad = nt(gk_ref[...], w_ref[1]) + nt(gv_ref[...], w_ref[2])
        unit, scale = norm_rows(sq_ref[...])
        low = norm_back(grad, g_ref[...], unit, scale).astype(BF)
        low_ref[...] = by_core(buf, low.astype(F32).T, s_ref[CORE])

    part = nn(low_ref[...], gr_ref[0])
    width = part.shape[1] // 2
    for y in range(2):
        put(k_ref.at[y, :, 0], x_ref.at[y, :, 0], part[:, y * width:(y + 1) * width])


def grad_comp(run, squeezed, gk, gv, w, gain, groups, n_dp):
    taps, rows, width = groups.shape
    chunk = width // n_dp
    shape = part_shape(width, width, n_dp, taps)
    half = lambda: out(shape, BF, shape[:2] + (1,) + shape[3:], lambda i, s: (0, 0, i, 0, 0))
    here = whole((rows, width))
    return run(
        grad_comp_kernel, "grad_comp", (taps,),
        [here, here, here, whole(w.shape), whole((1, width)),
         pl.BlockSpec((1, rows, width), lambda i, s: (i, 0, 0))],
        [half(), half()],
        [pltpu.VMEM((width, rows), BF), pltpu.VMEM((n_dp // 2, 2, chunk, rows), low_or_wide(chunk))],
        (squeezed, gk, gv, w, gain, groups), 10 * rows * width * width)


class Links:
    def __init__(self):
        self.dp = lax.axis_index("dp")
        self.y = lax.axis_index("fsdp")
        self.n_dp = lax.axis_size("dp")
        self.top = self.n_dp.bit_length() - 2

    def bit(self, axis):
        return self.y if axis == "y" else (self.dp >> axis) & 1

    def swap(self, value, axis):
        if axis == "y":
            return lax.ppermute(value, "fsdp", [(0, 1), (1, 0)])
        return lax.ppermute(value, "dp", [(i, i ^ (1 << axis)) for i in range(self.n_dp)])


class Chain:
    def __init__(self, links, keep, send, axes, order):
        self.links, self.axes, self.order = links, list(axes), list(order)
        lead = (2,) * len(self.axes)
        self.keep = keep.reshape(lead + keep.shape[2:])
        self.recv = links.swap(send.reshape(self.keep.shape), 0)

    def specs(self, steps):
        axis = self.order[0]
        where = self.axes.index(axis)
        lead, tail = self.keep.shape[:len(self.axes)], self.keep.shape[len(self.axes):]
        pre, post = math.prod(lead[:where]), math.prod(lead[where + 1:])
        rows = post * tail[0]
        view = (pre, 2, rows) + tail[1:]
        steps = math.gcd(steps, pre * post)
        bp = max(pre // steps, 1)
        nr = steps * bp // pre
        br = rows // nr
        last = steps - 1

        def read(i, s):
            i = jnp.minimum(i, last)
            return (i // nr, 0, i % nr, 0, 0)

        def write(i, s):
            i = jnp.minimum(i, last)
            return (i // nr, i % nr, 0, 0)

        args = [self.keep.reshape(view), self.recv.reshape(view)]
        ins = [pl.BlockSpec((bp, 2, br) + tail[1:], read)] * 2
        outs = [out((pre, rows) + tail[1:], BF, (bp, br) + tail[1:], write)] * 2
        slot = Y if axis == "y" else BITS + axis - 1

        def kernel(s_ref, keep, recv, held, send):
            @pl.when(pl.program_id(0) <= last)
            def _():
                bit = s_ref[slot]
                total = lambda b: (keep[:, b].astype(F32) + recv[:, b].astype(F32)).astype(BF)
                held[...] = total(bit)
                send[...] = total(1 - bit)

        def take(held, send):
            shape = lead[:where] + lead[where + 1:] + tail
            self.keep = held.reshape(shape)
            self.axes.pop(where)
            self.order.pop(0)
            self.recv = self.links.swap(send.reshape(shape), axis)

        return args, ins, outs, kernel, take


def chain_of(links, keep, recv, axes, order):
    chain = Chain.__new__(Chain)
    chain.links, chain.axes, chain.order = links, list(axes), list(order)
    chain.keep, chain.recv = keep, recv
    return chain


class Deal:
    def __init__(self, links, pairs, axes, orders, cuts):
        self.links, self.axes, self.orders, self.cuts = links, axes, orders, cuts
        self.keeps = [k for k, _ in pairs]
        self.sends = [x for _, x in pairs]
        self.rows, self.cols = self.keeps[0].shape[-2:]

    def start(self, sends):
        self.recvs = [self.links.swap(x, 0) for x in sends]

    def spans(self, c):
        lo, hi = self.cuts[c], self.cuts[c + 1]
        for n in range(2):
            a, b = max(lo - n * self.rows, 0), min(hi - n * self.rows, self.rows)
            if a < b:
                yield n, a, b

    def specs(self, steps):
        n = len(self.axes)
        lead = (2,) * n
        rows, cols = self.rows, self.cols
        firsts = [self.axes.index(o[0]) for o in self.orders]
        others = [a for a in range(n) if a not in firsts]
        split = max(steps >> len(others), 1)
        width = cols // split
        count = 2 ** len(others) * split

        def at(i):
            i = jnp.minimum(i, count - 1)
            places, rest = [0] * n, i // split
            for a in reversed(others):
                places[a] = rest % 2
                rest = rest // 2
            return places, i % split

        block = tuple(1 if a in others else 2 for a in range(n))

        def read(i, s):
            places, col = at(i)
            return (*places, 0, col)

        def write(first):
            def index(i, s):
                places, col = at(i)
                return (*places[:first], *places[first + 1:], 0, 0, col)
            return index

        args = [a.reshape(lead + (rows, cols)) for a in self.keeps + self.recvs]
        ins = [pl.BlockSpec(block + (rows, width), read)] * 4
        outs, slots = [], []
        for c, first in enumerate(firsts):
            size = self.cuts[c + 1] - self.cuts[c]
            shape = lead[1:] + (1, size, cols)
            less = block[:first] + block[first + 1:]
            outs += [out(shape, BF, less + (1, size, width), write(first))] * 2
            axis = self.axes[first]
            slots.append(Y if axis == "y" else BITS + axis - 1)

        def kernel(s_ref, *refs):
            held, sent = refs[4::2], refs[5::2]

            @pl.when(pl.program_id(0) < count)
            def _():
                for c, first in enumerate(firsts):
                    bit = s_ref[slots[c]]
                    row = 0
                    for m, a, b in self.spans(c):
                        keep, recv = refs[m], refs[2 + m]
                        for dst, side in ((held[c], bit), (sent[c], 1 - bit)):
                            pick = tuple(side if d == first else slice(None) for d in range(n))
                            pick += (slice(a, b), slice(None))
                            total = keep[pick].astype(F32) + recv[pick].astype(F32)
                            to = (slice(None),) * (n - 1) + (0, slice(row, row + b - a))
                            dst[to] = total.astype(BF)
                        row += b - a

        def take(*done):
            self.chains = []
            for c, order in enumerate(self.orders):
                axes = [a for a in self.axes if a != order[0]]
                recv = self.links.swap(done[2 * c + 1], order[0])
                self.chains.append(chain_of(self.links, done[2 * c], recv, axes, order[1:]))

        return args, ins, outs, kernel, take


class Dealt:
    def __init__(self, deal, blocks):
        self.deal, self.blocks = deal, blocks

    def specs(self, steps):
        deal = self.deal
        args = [a for c in deal.chains for a in (c.keep, c.recv)]
        rows, cols = deal.rows, deal.cols
        part = rows // self.blocks

        def kernel(s_ref, *refs):
            first, second = refs[-2:]

            @pl.when(pl.program_id(0) == 0)
            def _():
                halves = [[], []]
                for c in range(len(deal.chains)):
                    row = 0
                    for m, a, b in deal.spans(c):
                        pick = (0, slice(row, row + b - a))
                        halves[m].append(
                            refs[2 * c][pick].astype(F32) + refs[2 * c + 1][pick].astype(F32))
                        row += b - a
                one, two = [jnp.concatenate(h, axis=0) for h in halves]
                first[...] = one.T
                for n in range(self.blocks):
                    second[n * cols:(n + 1) * cols] = two[n * part:(n + 1) * part].T

        def take(*result):
            self.result = result

        outs = [fixed((cols, rows), F32), fixed((self.blocks * cols, part), F32)]
        return args, [whole(a.shape) for a in args], outs, kernel, take


class Join:
    def __init__(self, links, low, high):
        self.links, self.low, self.high = links, low, high

    def specs(self, steps):
        args = [self.low.keep, self.low.recv, self.high.keep, self.high.recv]
        shape = args[0].shape
        ins = [whole(shape)] * 4
        outs = [fixed(shape, BF)] * 2
        slot = BITS + self.links.top - 1

        def kernel(s_ref, lk, lr, hk, hr, held, send):
            @pl.when(pl.program_id(0) == 0)
            def _():
                low = (lk[...].astype(F32) + lr[...].astype(F32)).astype(BF)
                high = (hk[...].astype(F32) + hr[...].astype(F32)).astype(BF)
                upper = s_ref[slot] == 1
                held[...] = jnp.where(upper, high, low)
                send[...] = jnp.where(upper, low, high)

        def take(held, send):
            self.keep = held
            self.recv = self.links.swap(send, self.links.top)

        return args, ins, outs, kernel, take


class Small:
    def __init__(self, links, value):
        self.links, self.keep = links, value
        self.order = [0, "y"] + list(range(1, links.top + 1))
        self.send()

    def send(self):
        self.recv = self.links.swap(self.keep, self.order.pop(0)) if self.order else None

    def specs(self, steps):
        shape = self.keep.shape

        def kernel(s_ref, a, b, total):
            @pl.when(pl.program_id(0) == 0)
            def _():
                total[...] = a[...] + b[...]

        def take(total):
            self.keep = total
            self.send()

        return [self.keep, self.recv], [whole(shape)] * 2, [fixed(shape, F32)], kernel, take


class Last:
    def __init__(self, chain):
        self.chain = chain

    def specs(self, steps):
        keep, recv = self.chain.keep, self.chain.recv
        taps, rows, cols = keep.shape

        def kernel(s_ref, a, b, result):
            @pl.when(pl.program_id(0) == 0)
            def _():
                for t in range(taps):
                    result[t] = (a[t].astype(F32) + b[t].astype(F32)).T

        def take(result):
            self.result = result

        return ([keep, recv], [whole(keep.shape)] * 2, [fixed((taps, cols, rows), F32)], kernel, take)


class LastParts:
    def __init__(self, pair, rest):
        self.pair, self.rest = pair, rest

    def specs(self, steps):
        args = [self.pair.keep, self.pair.recv, self.rest.keep, self.rest.recv]
        _, rows, cols = args[0].shape

        def kernel(s_ref, a, b, c, d, qkv, rel, ow):
            @pl.when(pl.program_id(0) == 0)
            def _():
                total = lambda p, q, t: (p[t].astype(F32) + q[t].astype(F32)).T
                qkv[0] = total(c, d, 0)
                qkv[1] = total(a, b, 0)
                qkv[2] = total(a, b, 1)
                rel[...] = total(c, d, 1)
                ow[...] = total(c, d, 2)

        def take(*result):
            self.result = result

        outs = [fixed((3, cols, rows), F32), fixed((cols, rows), F32), fixed((cols, rows), F32)]
        return args, [whole(a.shape) for a in args], outs, kernel, take


class Carry:
    def __init__(self, *values):
        self.values = values

    def specs(self, steps):
        anywhere = pl.BlockSpec(memory_space=pl.ANY)
        outs = [(jax.ShapeDtypeStruct(v.shape, v.dtype), anywhere) for v in self.values]

        def take(*values):
            self.values = values

        return list(self.values), [anywhere] * len(outs), outs, lambda *refs: None, take


def advance(run, *items, steps=1):
    specs = [item.specs(steps) for item in items]
    n_in, n_out = [len(s[0]) for s in specs], [len(s[2]) for s in specs]
    aliases = {}
    for k, item in enumerate(items):
        if isinstance(item, Carry):
            aliases.update({1 + sum(n_in[:k]) + m: sum(n_out[:k]) + m for m in range(n_in[k])})

    def kernel(s_ref, *refs):
        a, b = 0, sum(n_in)
        for (_, _, _, part, _), i, o in zip(specs, n_in, n_out):
            part(s_ref, *refs[a:a + i], *refs[b:b + o])
            a, b = a + i, b + o

    done = list(run(
        kernel, "add", (steps,), [b for s in specs for b in s[1]], [o for s in specs for o in s[2]],
        [], [a for s in specs for a in s[0]], 0, aliases))
    for (_, _, outs, _, take) in specs:
        take(*done[:len(outs)])
        done = done[len(outs):]


def angle_parts(rows, width):
    fine = 32
    frequency = jnp.exp(
        jnp.arange(0, width, 2).astype(F32) * (-math.log(10000.0) / width))
    coarse = (fine * (rows // fine - 1 - jnp.arange(rows // fine))).astype(F32)
    near = (fine - 1 - jnp.arange(fine)).astype(F32)
    a, b = coarse[:, None] * frequency[None, :], near[:, None] * frequency[None, :]
    return (jnp.sin(a), jnp.cos(a), jnp.sin(b), jnp.cos(b))


def body(tokens, memory, compressed, cotangent, seg_len, mem_fill, cmem_fill, w_qkv, w_rel, w_out,
         w_up, w_down, w_comp, norm_gain1, norm_gain2, bias_content, bias_position, bias_up):
    streams = tokens.shape[0]
    assert streams == 1
    links = Links()
    n_dp, top = links.n_dp, links.top
    seg, width = tokens.shape[1:]
    mem, comp = memory.shape[1], compressed.shape[1]
    start = comp + mem
    keys = start + seg
    squeezed_rows = mem // 3
    scale = (width // H) ** (-0.5)
    current, recent, distant = tokens[0], memory[0], compressed[0]
    seg_length = seg_len[0]
    core, x, z = links.bit(0), links.bit(1), links.bit(2)
    run = Steps(jnp.stack(
        [links.y, core, seg_length, mem_fill[0], cmem_fill[0], core * 4 + x * 2 + z,
         core * 4 + z * 2 + x] + [links.bit(n) for n in range(1, top + 1)]).astype(jnp.int32))
    gain1, gain2 = norm_gain1.reshape(1, -1), norm_gain2.reshape(1, -1)

    swap = links.swap
    both = lambda value, axis: ordered(value, swap(value, axis), links.bit(axis))
    p_rel, p_a, p_b = pack_first(run, w_qkv, w_rel)
    rel, a, b = swap(p_rel, "y"), swap(p_a, "y"), swap(p_b, "y")
    normed = norm_hidden(run, distant, recent, current, gain1)
    c, d, up, down = [swap(p, "y") for p in pack_rest(run, w_out, w_up, w_down, w_comp)]
    table, groups = constants(run, recent, angle_parts(keys, width), squeezed_rows)
    rel = both(both(rel, 2), 1)
    a, b = both(a, 2), both(b, 1)
    a_far, b_far = swap(a, 1), swap(b, 2)
    pos = project_position(run, table, w_rel, (rel, swap(rel, 0)))
    a, a_far, b, b_far = follow(run, a, a_far, b, b_far)
    a, b = ordered(a, a_far, x), ordered(b, b_far, z)
    a_parts, b_parts = (a, swap(a, 0)), (b, swap(b, 0))
    c, d, up, down = follow(run, c, d, up, down)
    c_far, d_far, up_far, down_far = swap(c, 2), swap(d, 1), swap(up, 2), swap(down, 1)
    kv, qc, qp, probe, w_full = project_qkv(
        run, normed, w_qkv, a_parts, b_parts, bias_content, bias_position, seg, scale)
    c, c_far, d, d_far, up, up_far, down, down_far = follow(
        run, c, c_far, d, d_far, up, up_far, down, down_far)
    c, d, up, down = (ordered(c, c_far, z), ordered(d, d_far, x), ordered(up, up_far, z),
                      ordered(down, down_far, x))
    c_far, d_far, up_far, down_far = swap(c, 1), swap(d, 2), swap(up, 1), swap(down, 2)
    p0, m0 = attention(run, qc, qp, kv, pos, comp, mem, 0)
    p1, m1 = attention(run, qc, qp, kv, pos, comp, mem, 1)
    c, c_far, d, d_far = follow(run, c, c_far, d, d_far)
    c, d = ordered(c, c_far, x), ordered(d, d_far, z)
    c_parts, d_parts = (c, swap(c, 0)), (d, swap(d, 0))
    squeezed, squeezed_low, ck, cv = squeeze(run, groups, w_comp, c_parts, d_parts, w_full, gain1)
    far = list(range(3, top + 1))
    names, under = ["y"] + list(range(top, 0, -1)), ["y"] + list(range(top - 1, 0, -1))
    up, up_far, down, down_far = follow(run, up, up_far, down, down_far)
    up, down = ordered(up, up_far, x), ordered(down, down_far, z)
    up_parts, down_parts = (up, swap(up, 0)), (down, swap(down, 0))
    gck, gcv = reconstruct(run, probe, kv, ck, cv, mem)
    comp_chain = Chain(links, *grad_comp(run, squeezed, gck, gcv, w_full, gain1, groups, n_dp),
                       names, [2, 1, "y"] + far)

    attended, second, w_out_full = mix_out(run, current, (m0, m1), w_out, d_parts, gain2)
    advance(run, comp_chain, steps=2)
    (output, grad_attended, grad_mix, up_keep, up_send, down_keep, down_send, sum_bias, sum_gain2
     ) = feed_forward(run, second, cotangent[0], attended, w_up, up_parts, w_down, down_parts,
                      bias_up.reshape(1, -1), gain2, w_out_full, n_dp)
    rows, half = bias_up.shape[0] // n_dp, width // 2
    flat = lambda a: a.reshape(2, n_dp // 2, rows, half)
    third = max(2 * rows * 11 // 32 // 16 * 16, 8)
    deal = Deal(
        links, [(flat(up_keep), flat(up_send)), (flat(down_keep), flat(down_send))], names,
        [[1, "y", 2] + far, ["y", 2, 1] + far, [2, 1, "y"] + far],
        (0, third, 2 * third, 2 * rows))
    carry = Carry(*deal.sends)
    advance(run, comp_chain, carry)
    deal.start(carry.values)

    back = functools.partial(attention_back, run, (p0, p1), grad_mix, qc, qp, kv, pos, start, scale)
    grads = lambda turned, gq, half: projection_grads(
        run, turned, gq, grad_attended, normed, table, (m0, m1), w_full, n_dp, half)
    near = far[:-1]
    gq0, gk0, gv0, gpos0, content0, position0 = back(0)
    advance(run, deal, steps=4)
    *sent, gain_0 = grads((gk0, gv0, gpos0), gq0, 0)
    kv0, carry = sent[0], Carry(sent[1], sent[3])
    qro0 = sent[2]
    gq1, gk1, gv1, gpos1, content1, position1 = back(1)
    advance(run, *deal.chains, comp_chain, carry, steps=4)
    kv0 = Chain(links, kv0, carry.values[0], under, [2, "y", 1] + near)
    qro0 = Chain(links, qro0, carry.values[1], under, [1, 2, "y"] + near)
    *sent, gain_1 = grads((gk1, gv1, gpos1), gq1, 1)
    carry = Carry(sent[1], sent[3])
    advance(run, *deal.chains, comp_chain, kv0, qro0, carry, steps=2)
    kv1 = Chain(links, sent[0], carry.values[0], under, ["y", 2, 1] + near)
    qro1 = Chain(links, sent[2], carry.values[1], under, [1, "y", 2] + near)
    grad_rows = grad_tokens(run, (gk0, gk1), (gv0, gv1), (gq0, gq1), current, grad_attended,
                            w_full, gain1)
    row = lambda a, b: jnp.concatenate([a, b], axis=1)
    small = Small(links, jnp.concatenate(
        [(gain_0 + gain_1) / gain1, sum_gain2, row(content0, content1), row(position0, position1),
         sum_bias.reshape(-1, width)], axis=0))
    ready = [c for c in (*deal.chains, comp_chain, kv0, qro0) if c.order]
    advance(run, *ready, kv1, qro1, small, steps=2)
    new_memory = lax.dynamic_slice_in_dim(
        jnp.concatenate([recent, current], axis=0), seg_length, mem, 0)
    new_compressed = lax.dynamic_slice_in_dim(
        jnp.concatenate([distant, squeezed_low[:squeezed_rows]], axis=0), seg_length // 3, comp, 0)
    while kv1.order:
        ready = [c for c in (*deal.chains, comp_chain, kv0, qro0) if c.order]
        advance(run, *ready, kv1, qro1, small)
    last_comp = Last(comp_chain)
    dealt = Dealt(deal, bias_up.shape[0] // (2 * half))
    ends = [Join(links, kv0, kv1), Join(links, qro0, qro1)]
    advance(run, *ends, small, last_comp, dealt)
    tail = LastParts(*ends)
    advance(run, tail, small)
    while small.recv is not None:
        advance(run, small)
    grad_up, grad_down = dealt.result
    grad_qkv, grad_rel, grad_out = tail.result

    at = links.dp * 2 + links.y
    each, each_up = width // (2 * n_dp), bias_up.shape[0] // (2 * n_dp)
    vec = lax.dynamic_slice(small.keep[:4], (0, at * each), (4, each))
    vec_up = lax.dynamic_slice_in_dim(small.keep[4:].reshape(-1), at * each_up, each_up)
    return (output[None], grad_rows[None], new_memory[None], new_compressed[None],
            grad_qkv, grad_rel, grad_out,
            grad_up, grad_down, last_comp.result, vec[0], vec[1], vec[2], vec[3], vec_up)


def solution(mesh):
    rows = P(("dp", "fsdp"), None, None)
    one = P(("dp", "fsdp"))
    return jax.shard_map(
        body,
        mesh=mesh,
        in_specs=(rows, rows, rows, rows, one, one, one, P(None, "fsdp", None), P("fsdp", None),
                  P("fsdp", None), P("fsdp", None), P("fsdp", None), P(None, "fsdp", None), P(),
                  P(), P(), P(), P()),
        out_specs=(rows, rows, rows, rows, P(None, "fsdp", "dp"), P("fsdp", "dp"),
                   P("fsdp", "dp"), P("fsdp", "dp"), P("fsdp", "dp"), P(None, "fsdp", "dp"), one,
                   one, one, one, one),
        check_vma=False,
    )
```

time: 599 us -> 528 us (0.88)
  waiting for transfers between devices: 155 us -> 109 us
  other arithmetic: 50.5 us -> 14.1 us
  Pallas kernels: 275 us -> 289 us
    ppermute x54, waiting for transfers between devices: 137 us -> 73.2 us  [swap(): lax.ppermute(value, 'dp', [(i, i ^ 1 << axis) for i in range(self.n_dp)])]
    ppermute x15 -> x16, waiting for transfers between devices: 18.4 us -> 35.6 us  [swap(): return lax.ppermute(value, 'fsdp', [(0, 1), (1, 0)])]
    another operation x5 -> x0, other arithmetic: 14.9 us -> none
    pallas_call x28 -> x33, Pallas kernels: 275 us -> 289 us  [__call__(): pl.pallas_call(ordered_kernel, name=name, out_shape=[s for s, _ in outs]...]
    select_n x20 -> x15, other arithmetic: 17.8 us -> 7.07 us  [ordered(): jnp.where(at == bit, mine[:, None], theirs[:, None])]
    unnamed x103 -> x175, local copies, waits for them, and re-layouts: 15.2 us -> 25.9 us
    squeeze x6 -> x1, local copies, waits for them, and re-layouts: 7.67 us -> 0.53 us  [body(): vec[3]]
    ppermute x15 -> x16, starting transfers between devices: 16 us -> 18.8 us  [swap(): return lax.ppermute(value, 'fsdp', [(0, 1), (1, 0)])]
  transfers between devices with their start and end apart: 69 -> 70, of which waited for: 20 -> 23; matrix products, arithmetic and copies ran while one was open for 13% -> 5% of each run, Pallas kernels for 46% -> 41%
where the time goes in v2:
time: 528 us; the launch traced here: 519 us
  Pallas kernels  289 us (55%)
  waiting for transfers between devices  109 us (21%)
  starting transfers between devices  65.8 us (12%)
  local copies, waits for them, and re-layouts  36.7 us (7%)
  other arithmetic  14.1 us (3%)
    pallas_call x33, Pallas kernels, __call__(): pl.pallas_call(ordered_kernel, name=name, out_shape=[s for s, _ in outs]...  289 us
    ppermute x54, waiting for transfers between devices, swap(): lax.ppermute(value, 'dp', [(i, i ^ 1 << axis) for i in range(self.n_dp)])  73.2 us
    ppermute x54, starting transfers between devices, swap(): lax.ppermute(value, 'dp', [(i, i ^ 1 << axis) for i in range(self.n_dp)])  47 us
    ppermute x16, waiting for transfers between devices, swap(): return lax.ppermute(value, 'fsdp', [(0, 1), (1, 0)])  35.6 us
    unnamed x175, local copies, waits for them, and re-layouts  25.9 us
    ppermute x16, starting transfers between devices, swap(): return lax.ppermute(value, 'fsdp', [(0, 1), (1, 0)])  18.8 us
  transfers between devices with their start and end apart: 70, of which 23 were waited for; matrix products, arithmetic and copies ran while one was open for 5% of the time, Pallas kernels for 41%

profile of v2, /device:TPU:0, one launch (start us, length us, event | category | flops | bytes accessed | tf_op | source)
XLA Modules:
  0.0 518.9 jit_solution(15863355168183133066)
XLA Ops:
  3.3 2.5 pack_first.1
  5.8 3.0 collective-permute-start.6
  8.8 2.0 collective-permute-start.3
  10.8 7.0 %norm_hidden.1 = (bf16[1536,1024]{1,0:T(8,128)(2,1)}, f32[8,128]{1,0:T(8,128)}) custom-call(s32[10]{0:T(128)} %stack.31.s_ref, bf16[512,1024]{1,0:T(8,128)(2,1)} %bitcast.271, bf16[512,1024]{1,0:T(8,128)(2,1)} %bitcast.257, bf16[512,1024]{1,0:T(8,128)(2,1)} %bitcast.249, f32[1,1024]{1,0:T(1,128)} %bitcast.358, f32[8,128]{1,0:T(8,128)} %get-tuple-element.211.refs_4_), custom_call_target="tpu_custom_call" | custom-call | flops 1024 | bytes 1024 | tf_op jit(solution)/shard_map/norm_hidden/pallas_call | solution.py:46
  17.8 3.3 pack_rest.1
  34.9 5.8 %collective-permute-done.8 = bf16[1,128,1024]{2,1,0:T(8,128)(2,1)S(1)} collective-permute-done((bf16[1,128,1024]{2,1,0:T(8,128)(2,1)S(1)}, bf16[1,128,1024]{2,1,0:T(8,128)(2,1)S(1)}, u32[]{:S(2)}, u32[]{:S(2)}) %collective-permute-start.8) | collective-permute-done | bytes 262176 | tf_op jit(solution)/shard_map/ppermute | solution.py:786
  43.9 5.5 %constants.1 = (bf16[1536,1024]{1,0:T(8,128)(2,1)}, bf16[3,192,1024]{2,1,0:T(8,128)(2,1)}, f32[8,128]{1,0:T(8,128)}) custom-call(s32[10]{0:T(128)} %stack.31.s_ref, bf16[512,1024]{1,0:T(8,128)(2,1)} %bitcast.258, f32[48,512]{1,0:T(8,128)} %get-tuple-element.427.refs_1_, f32[48,512]{1,0:T(8,128)} %get-tuple-element.426.refs_2_, ...), custom_call_target="tpu_custom_call" | custom-call | flops 1024 | bytes 1024 | tf_op jit(solution)/shard_map/constants/pallas_call | solution.py:46
  50.3 7.7 %project_position.1 = (bf16[1536,1024]{1,0:T(8,128)(2,1)}, f32[8,128]{1,0:T(8,128)}) custom-call(s32[10]{0:T(128)} %stack.31.s_ref, bf16[1536,1024]{1,0:T(8,128)(2,1)} %get-tuple-element.217.refs_0_.refs_6_, bf16[512,1024]{1,0:T(8,128)(2,1)} %refs_1_.3, bf16[1,256,1024]{2,1,0:T(8,128)(2,1)} %copy-done.28, bf16[1,256,1024]{2,1,0:T(8,128)(2,1)} %copy-done.53, ...), custom_call_target="tpu_custom_call" | custom-call | flops 1024 | bytes 1024 | tf_op jit(solution)/shard_map/project_position/pallas_call | solution.py:46
  64.4 7.2 %collective-permute-done.13.refs_1_ = bf16[2,64,1024]{2,1,0:T(8,128)(2,1)S(1)} collective-permute-done((bf16[2,64,1024]{2,1,0:T(8,128)(2,1)S(1)}, bf16[2,64,1024]{2,1,0:T(8,128)(2,1)S(1)}, u32[]{:S(2)}, u32[]{:S(2)}) %collective-permute-start.13) | collective-permute-done | bytes 262176 | tf_op jit(solution)/shard_map/ppermute | solution.py:785
  77.5 17.8 %project_qkv.1 = (bf16[2,1536,1024]{2,1,0:T(8,128)(2,1)}, bf16[512,1024]{1,0:T(8,128)(2,1)}, bf16[512,1024]{1,0:T(8,128)(2,1)}, bf16[512,1024]{1,0:T(8,128)(2,1)...) custom-call(s32[10]{0:T(128)} %stack.31.s_ref, bf16[1536,1024]{1,0:T(8,128)(2,1)} %get-tuple-element.212.refs_0_.refs_5_, ...), custom_call_target="tpu_custom_call" | custom-call | flops 1024 | bytes 1024 | tf_op jit(solution)/shard_map/project_qkv/pallas_call | solution.py:46
  105.0 15.1 %attention.2 = (bf16[4,512,1536]{2,1,0:T(8,128)(2,1)}, bf16[512,512]{1,0:T(8,128)(2,1)}, f32[8,128]{1,0:T(8,128)}) custom-call(s32[10]{0:T(128)} %stack.31.s_ref, bf16[512,1024]{1,0:T(8,128)(2,1)} %get-tuple-element.231.refs_0_.refs_2_, bf16[512,1024]{1,0:T(8,128)(2,1)} %get-tuple-element.232.refs_1_.refs_3_, ...), custom_call_target="tpu_custom_call" | custom-call | flops 1024 | bytes 1024 | tf_op jit(solution)/shard_map/attention/pallas_call | solution.py:46
  120.1 14.9 %attention.3 = (bf16[4,512,1536]{2,1,0:T(8,128)(2,1)}, bf16[512,512]{1,0:T(8,128)(2,1)}, f32[8,128]{1,0:T(8,128)}) custom-call(s32[10]{0:T(128)} %stack.31.s_ref, bf16[512,1024]{1,0:T(8,128)(2,1)} %get-tuple-element.231.refs_0_.refs_2_, bf16[512,1024]{1,0:T(8,128)(2,1)} %get-tuple-element.232.refs_1_.refs_3_, ...), custom_call_target="tpu_custom_call" | custom-call | flops 1024 | bytes 1024 | tf_op jit(solution)/shard_map/attention/pallas_call | solution.py:46
  143.4 9.3 %squeeze.37 = (f32[192,1024]{1,0:T(8,128)}, bf16[192,1024]{1,0:T(8,128)(2,1)}, bf16[192,1024]{1,0:T(8,128)(2,1)}, bf16[192,1024]{1,0:T(8,128)(2,1)}, f32[8,128]{1,0:T(8,128)}) custom-call(s32[10]{0:T(128)} %stack.31.s_ref, bf16[3,192,1024]{2,1,0:T(8,128)(2,1)} %get-tuple-element.251.refs_0_.refs_5_, bf16[3,512,1024]{2,1,0:T(8,128)(2,1)} %refs_1_.5, ...), custom_call_target="tpu_custom_call" | custom-call | flops 1024 | bytes 1024 | tf_op jit(solution)/shard_map/squeeze/pallas_call | solution.py:46
  152.7 12.4 %collective-permute-done.24.refs_1_ = bf16[1,128,4096]{2,1,0:T(8,128)(2,1)} collective-permute-done((bf16[1,128,4096]{2,1,0:T(8,128)(2,1)S(1)}, bf16[1,128,4096]{2,1,0:T(8,128)(2,1)}, u32[]{:S(2)}, u32[]{:S(2)}) %collective-permute-start.24) | collective-permute-done | bytes 1048608 | tf_op jit(solution)/shard_map/ppermute | solution.py:786
  165.8 15.0 %reconstruct.1 = (bf16[192,1024]{1,0:T(8,128)(2,1)}, bf16[192,1024]{1,0:T(8,128)(2,1)}, f32[8,128]{1,0:T(8,128)}) custom-call(s32[10]{0:T(128)} %stack.31.s_ref, bf16[512,1024]{1,0:T(8,128)(2,1)} %get-tuple-element.257.refs_0_, bf16[2,1536,1024]{2,1,0:T(8,128)(2,1)} %get-tuple-element.233.refs_2_.refs_3_.refs_1_.refs_4_.refs_5_, ...), custom_call_target="tpu_custom_call" | custom-call | flops 1024 | bytes 1024 | tf_op jit(solution)/shard_map/reconstruct/pallas_call | solution.py:46
  180.7 10.6 %grad_comp.1 = (bf16[2,8,3,64,512]{4,3,2,1,0:T(8,128)(2,1)}, bf16[2,8,3,64,512]{4,3,2,1,0:T(8,128)(2,1)}, f32[8,128]{1,0:T(8,128)}) custom-call(s32[10]{0:T(128)} %stack.31.s_ref, f32[192,1024]{1,0:T(8,128)} %get-tuple-element.256.refs_0_, bf16[192,1024]{1,0:T(8,128)(2,1)} %get-tuple-element.266.refs_1_, bf16[192,1024]{1,0:T(8,128)(2,1)} %get-tuple-element.267.refs_2_, ...), custom_call_target="tpu_custom_call" | custom-call | flops 1024 | bytes 1024 | tf_op jit(solution)/shard_map/grad_comp/pallas_call | solution.py:46
  197.8 6.2 %mix_out.1 = (f32[512,1024]{1,0:T(8,128)}, bf16[512,1024]{1,0:T(8,128)(2,1)}, bf16[1024,1024]{1,0:T(8,128)(2,1)}, f32[8,128]{1,0:T(8,128)}) custom-call(s32[10]{0:T(128)} %stack.31.s_ref, bf16[512,1024]{1,0:T(8,128)(2,1)} %bitcast.250, bf16[512,512]{1,0:T(8,128)(2,1)} %get-tuple-element.241.refs_1_.refs_7_, ...), custom_call_target="tpu_custom_call" | custom-call | flops 1024 | bytes 1024 | tf_op jit(solution)/shard_map/mix_out/pallas_call | solution.py:46
  204.0 5.1 add.56
  209.5 42.5 %feed_forward.1 = (bf16[512,1024]{1,0:T(8,128)(2,1)}, f32[512,1024]{1,0:T(8,128)}, bf16[512,1024]{1,0:T(8,128)(2,1)}, bf16[2,8,1,256,512]{4,3,2,1,0:T(8,128)(2,1...) custom-call(s32[10]{0:T(128)} %stack.31.s_ref, ...), custom_call_target="tpu_custom_call" | custom-call | flops 1024 | bytes 1024 | tf_op jit(solution)/shard_map/feed_forward/pallas_call | solution.py:46
  253.1 4.0 add.57
  257.7 16.3 %attention_back.2 = (bf16[512,512]{1,0:T(8,128)(2,1)}, bf16[512,1536]{1,0:T(8,128)(2,1)}, bf16[512,1536]{1,0:T(8,128)(2,1)}, bf16[512,1536]{1,0:T(8,128)(2,1)}, ...) custom-call(s32[10]{0:T(128)} %stack.31.s_ref, bf16[4,512,1536]{2,1,0:T(8,128)(2,1)} %get-tuple-element.282.refs_0_, ...), custom_call_target="tpu_custom_call" | custom-call | flops 1024 | bytes 1024 | tf_op jit(solution)/shard_map/attention_back/pallas_call | solution.py:46
  274.0 10.5 %add.58 = (bf16[2,2,2,1,176,512]{5,4,3,2,1,0:T(8,128)(2,1)}, bf16[2,2,2,1,176,512]{5,4,3,2,1,0:T(8,128)(2,1)}, bf16[2,2,2,1,176,512]{5,4,3,2,1,0:T(8,128)(2,1)},...) custom-call(s32[10]{0:T(128)} %stack.31.s_ref, ...), custom_call_target="tpu_custom_call" | custom-call | flops 1024 | bytes 1024 | tf_op jit(solution)/shard_map/add/pallas_call | solution.py:46
  289.3 14.4 %projection_grads.2 = (bf16[2,4,2,64,512]{4,3,2,1,0:T(8,128)(2,1)}, bf16[2,4,2,64,512]{4,3,2,1,0:T(8,128)(2,1)}, bf16[2,4,3,64,512]{4,3,2,1,0:T(8,128)(2,1)}, bf...) custom-call(s32[10]{0:T(128)} %stack.31.s_ref, ...), custom_call_target="tpu_custom_call" | custom-call | flops 1024 | bytes 1024 | tf_op jit(solution)/shard_map/projection_grads/pallas_call | solution.py:46
  303.7 16.1 %attention_back.3 = (bf16[512,512]{1,0:T(8,128)(2,1)}, bf16[512,1536]{1,0:T(8,128)(2,1)}, bf16[512,1536]{1,0:T(8,128)(2,1)}, bf16[512,1536]{1,0:T(8,128)(2,1)}, ...) custom-call(s32[10]{0:T(128)} %stack.31.s_ref, bf16[4,512,1536]{2,1,0:T(8,128)(2,1)} %get-tuple-element.291.refs_0_, ...), custom_call_target="tpu_custom_call" | custom-call | flops 1024 | bytes 1024 | tf_op jit(solution)/shard_map/attention_back/pallas_call | solution.py:46
  319.8 15.2 %collective-permute-done.35 = bf16[2,2,3,64,512]{4,3,2,1,0:T(8,128)(2,1)S(1)} collective-permute-done((bf16[2,2,3,64,512]{4,3,2,1,0:T(8,128)(2,1)}, bf16[2,2,3,64,512]{4,3,2,1,0:T(8,128)(2,1)S(1)}, u32[]{:S(2)}, u32[]{:S(2)}) %collective-permute-start.35) | collective-permute-done | bytes 786464 | tf_op jit(solution)/shard_map/ppermute | solution.py:786
  336.9 7.3 %add.59 = (bf16[1,4,176,512]{3,2,1,0:T(8,128)(2,1)}, bf16[1,4,176,512]{3,2,1,0:T(8,128)(2,1)}, bf16[2,2,176,512]{3,2,1,0:T(8,128)(2,1)}, bf16[2,2,176,512]{3,2,1...) custom-call(s32[10]{0:T(128)} %stack.31.s_ref, ...), custom_call_target="tpu_custom_call", output_to_operand_aliasing={{8}: (9, {}), {9}: (10, {})} | custom-call | flops 1024 | bytes 1024 | tf_op jit(solution)/shard_map/add/pallas_call | solution.py:46
  348.1 8.5 %collective-permute-done.39 = bf16[2,3,64,512]{3,2,1,0:T(8,128)(2,1)} collective-permute-done((bf16[2,3,64,512]{3,2,1,0:T(8,128)(2,1)}, bf16[2,3,64,512]{3,2,1,0:T(8,128)(2,1)}, u32[]{:S(2)}, u32[]{:S(2)}) %collective-permute-start.39) | collective-permute-done | bytes 393248 | tf_op jit(solution)/shard_map/ppermute | solution.py:785
  357.1 14.6 %projection_grads.3 = (bf16[2,4,2,64,512]{4,3,2,1,0:T(8,128)(2,1)}, bf16[2,4,2,64,512]{4,3,2,1,0:T(8,128)(2,1)}, bf16[2,4,3,64,512]{4,3,2,1,0:T(8,128)(2,1)}, bf...) custom-call(s32[10]{0:T(128)} %stack.31.s_ref, ...), custom_call_target="tpu_custom_call" | custom-call | flops 1024 | bytes 1024 | tf_op jit(solution)/shard_map/projection_grads/pallas_call | solution.py:46
  374.8 6.8 %add.60 = (bf16[2,1,176,512]{3,2,1,0:T(8,128)(2,1)}, bf16[2,1,176,512]{3,2,1,0:T(8,128)(2,1)}, bf16[2,1,176,512]{3,2,1,0:T(8,128)(2,1)}, bf16[2,1,176,512]{3,2,1...) custom-call(s32[10]{0:T(128)} %stack.31.s_ref, ...), custom_call_target="tpu_custom_call", output_to_operand_aliasing={{12}: (13, {}), {13}: (14, {})} | custom-call | flops 1024 | bytes 1024 | tf_op jit(solution)/shard_map/add/pallas_call | solution.py:46
  388.3 5.5 %collective-permute-done.44 = bf16[2,1,160,512]{3,2,0,1:T(8,128)(2,1)} collective-permute-done((bf16[2,1,160,512]{3,2,0,1:T(8,128)(2,1)}, bf16[2,1,160,512]{3,2,0,1:T(8,128)(2,1)}, u32[]{:S(2)}, u32[]{:S(2)}) %collective-permute-start.44) | collective-permute-done | bytes 327712 | tf_op jit(solution)/shard_map/ppermute | solution.py:785
  395.3 3.0 collective-permute-done.42
  399.8 10.9 %grad_tokens.1 = (bf16[512,1024]{1,0:T(8,128)(2,1)}, f32[8,128]{1,0:T(8,128)}) custom-call(s32[10]{0:T(128)} %stack.31.s_ref, bf16[512,1536]{1,0:T(8,128)(2,1)} %get-tuple-element.290.refs_0_, bf16[512,1536]{1,0:T(8,128)(2,1)} %get-tuple-element.303.refs_0_.refs_1_, bf16[512,1536]{1,0:T(8,128)(2,1)} %get-tuple-element.292.refs_1_.refs_2_, ...), custom_call_target="tpu_custom_call" | custom-call | flops 1024 | bytes 1024 | tf_op jit(solution)/shard_map/grad_tokens/pallas_call | solution.py:46
  413.0 6.9 %add.61 = (bf16[1,1,176,512]{3,2,1,0:T(8,128)(2,1)}, bf16[1,1,176,512]{3,2,1,0:T(8,128)(2,1)}, bf16[1,1,176,512]{3,2,1,0:T(8,128)(2,1)}, bf16[1,1,176,512]{3,2,1...) custom-call(s32[10]{0:T(128)} %stack.31.s_ref, ...), custom_call_target="tpu_custom_call" | custom-call | flops 1024 | bytes 1024 | tf_op jit(solution)/shard_map/add/pallas_call | solution.py:46
  425.4 14.4 %collective-permute-done.54.refs_9_ = f32[8,1024]{1,0:T(8,128)S(1)} collective-permute-done((f32[8,1024]{1,0:T(8,128)}, f32[8,1024]{1,0:T(8,128)S(1)}, u32[]{:S(2)}, u32[]{:S(2)}) %collective-permute-start.54) | collective-permute-done | bytes 32800 | tf_op jit(solution)/shard_map/ppermute | solution.py:785
  441.1 4.4 add.62
  448.3 2.6 collective-permute-start.63
  452.7 2.3 collective-permute-done.58.refs_5_
  459.7 3.0 add.63
  462.7 7.5 %collective-permute-done.63.refs_11_ = bf16[3,64,512]{2,1,0:T(8,128)(2,1)} collective-permute-done((bf16[3,64,512]{2,1,0:T(8,128)(2,1)}, bf16[3,64,512]{2,1,0:T(8,128)(2,1)}, u32[]{:S(2)}, u32[]{:S(2)}) %collective-permute-start.63) | collective-permute-done | bytes 196640 | tf_op jit(solution)/shard_map/ppermute | solution.py:786
  470.3 9.1 %collective-permute-done.66.refs_17_ = bf16[1,160,512]{2,1,0:T(8,128)(2,1)} collective-permute-done((bf16[1,160,512]{2,1,0:T(8,128)(2,1)}, bf16[1,160,512]{2,1,0:T(8,128)(2,1)}, u32[]{:S(2)}, u32[]{:S(2)}) %collective-permute-start.66) | collective-permute-done | bytes 163872 | tf_op jit(solution)/shard_map/ppermute | solution.py:786
  481.4 3.1 collective-permute-done.55.refs_1_
  486.7 4.8 add.64
  491.7 2.9 collective-permute-start.67
  494.7 4.3 fusion.1
  498.9 2.4 copy.69
  502.4 4.6 collective-permute-done.69.refs_5_
  507.7 3.2 add.65
  510.9 2.1 copy.66
  (364 shorter events, 111.0 us)
Async XLA Ops:
  5.8 18.5 %collective-permute-start.6 = (bf16[1,64,1024]{2,1,0:T(8,128)(2,1)}, bf16[1,64,1024]{2,1,0:T(8,128)(2,1)S(1)}, u32[]{:S(2)}, u32[]{:S(2)}) collective-permute-start(bf16[1,64,1024]{2,1,0:T(8,128)(2,1)} %get-tuple-element.218), channel_id=1, source_target_pairs={{0,1},{1,0},{2,3},{3,2},{4,5},{5,4},{6,7},{7,6},{8,9},{9,8},{10,11... | collective-permute-start | bytes 393224 | tf_op jit(solution)/shard_map/ppermute | solution.py:785
  8.8 18.0 %collective-permute-start = (bf16[1,64,1536]{2,1,0:T(8,128)(2,1)}, bf16[1,64,1536]{2,1,0:T(8,128)(2,1)S(1)}, u32[]{:S(2)}, u32[]{:S(2)}) collective-permute-start(bf16[1,64,1536]{2,1,0:T(8,128)(2,1)} %get-tuple-element.213), channel_id=1, source_target_pairs={{0,1},{1,0},{2,3},{3,2},{4,5},{5,4},{6,7},{7,6},{8,9},{9,8},{10,11... | collective-permute-start | bytes 589832 | tf_op jit(solution)/shard_map/ppermute | solution.py:785
  8.8 18.4 %collective-permute-start.3 = (bf16[1,64,1536]{2,1,0:T(8,128)(2,1)}, bf16[1,64,1536]{2,1,0:T(8,128)(2,1)S(1)}, u32[]{:S(2)}, u32[]{:S(2)}) collective-permute-start(bf16[1,64,1536]{2,1,0:T(8,128)(2,1)} %get-tuple-element.214), channel_id=1, source_target_pairs={{0,1},{1,0},{2,3},{3,2},{4,5},{5,4},{6,7},{7,6},{8,9},{9,8},{10,11... | collective-permute-start | bytes 589832 | tf_op jit(solution)/shard_map/ppermute | solution.py:785
  21.1 50.6 %collective-permute-start.14 = (bf16[1,64,4096]{2,1,0:T(8,128)(2,1)}, bf16[1,64,4096]{2,1,0:T(8,128)(2,1)S(1)}, u32[]{:S(2)}, u32[]{:S(2)}) collective-permute-start(bf16[1,64,4096]{2,1,0:T(8,128)(2,1)} %get-tuple-element.227), channel_id=1, source_target_pairs={{0,1},{1,0},{2,3},{3,2},{4,5},{5,4},{6,7},{7,6},{8,9},{9,8},{10,11... | collective-permute-start | bytes 1572872 | tf_op jit(solution)/shard_map/ppermute | solution.py:785
  21.1 50.6 %collective-permute-start.15 = (bf16[1,256,1024]{2,1,0:T(8,128)(2,1)}, bf16[1,256,1024]{2,1,0:T(8,128)(2,1)S(1)}, u32[]{:S(2)}, u32[]{:S(2)}) collective-permute-start(bf16[1,256,1024]{2,1,0:T(8,128)(2,1)} %get-tuple-element.228), channel_id=1, source_target_pairs={{0,1},{1,0},{2,3},{3,2},{4,5},{5,4},{6,7},{7,6},{8,9},{9,8},{10,11... | collective-permute-start | bytes 1572872 | tf_op jit(solution)/shard_map/ppermute | solution.py:785
  27.2 13.8 %collective-permute-start.4 = (bf16[1,64,1536]{2,1,0:T(8,128)(2,1)S(1)}, bf16[1,64,1536]{2,1,0:T(8,128)(2,1)S(1)}, u32[]{:S(2)}, u32[]{:S(2)}) collective-permute-start(bf16[1,64,1536]{2,1,0:T(8,128)(2,1)S(1)} %collective-permute-done.3), channel_id=1, source_target_pairs={{0,4},{2,6},{4,0},{6,2},{8,12},{10,14},{12,8},{14,10},{16,20},{18,... | collective-permute-start | bytes 589832 | tf_op jit(solution)/shard_map/ppermute | solution.py:786
  33.3 24.7 %collective-permute-start.2 = (bf16[1,128,1536]{2,1,0:T(8,128)(2,1)S(1)}, bf16[1,128,1536]{2,1,0:T(8,128)(2,1)S(1)}, u32[]{:S(2)}, u32[]{:S(2)}) collective-permute-start(bf16[1,128,1536]{2,1,0:T(8,128)(2,1)S(1)} %bitcast_select_fusion.12.refs_0_), channel_id=1, source_target_pairs={{0,4},{2,6},{4,0},{6,2},{8,12},{10,14},{12,8},{14,10},{16,20},{18,... | collective-permute-start | bytes 1179656 | tf_op jit(solution)/shard_map/ppermute | solution.py:786
  41.3 16.8 %collective-permute-start.5 = (bf16[1,128,1536]{2,1,0:T(8,128)(2,1)S(1)}, bf16[1,128,1536]{2,1,0:T(8,128)(2,1)S(1)}, u32[]{:S(2)}, u32[]{:S(2)}) collective-permute-start(bf16[1,128,1536]{2,1,0:T(8,128)(2,1)S(1)} %bitcast_select_fusion.11.refs_2_), channel_id=1, source_target_pairs={{0,8},{2,10},{4,12},{6,14},{8,0},{10,2},{12,4},{14,6},{16,24},{18,... | collective-permute-start | bytes 1179656 | tf_op jit(solution)/shard_map/ppermute | solution.py:786
  61.9 15.0 %collective-permute-start.11 = (bf16[1,256,1536]{2,1,0:T(8,128)(2,1)S(1)}, bf16[1,256,1536]{2,1,0:T(8,128)(2,1)}, u32[]{:S(2)}, u32[]{:S(2)}) collective-permute-start(bf16[1,256,1536]{2,1,0:T(8,128)(2,1)S(1)} %bitcast_select_fusion.6.refs_4_), channel_id=1, source_target_pairs={{0,2},{2,0},{4,6},{6,4},{8,10},{10,8},{12,14},{14,12},{16,18},{18,... | collective-permute-start | bytes 2359304 | tf_op jit(solution)/shard_map/ppermute | solution.py:786
  62.8 14.7 %collective-permute-start.10 = (bf16[1,256,1536]{2,1,0:T(8,128)(2,1)S(1)}, bf16[1,256,1536]{2,1,0:T(8,128)(2,1)}, u32[]{:S(2)}, u32[]{:S(2)}) collective-permute-start(bf16[1,256,1536]{2,1,0:T(8,128)(2,1)S(1)} %bitcast_select_fusion.7.refs_2_), channel_id=1, source_target_pairs={{0,2},{2,0},{4,6},{6,4},{8,10},{10,8},{12,14},{14,12},{16,18},{18,... | collective-permute-start | bytes 2359304 | tf_op jit(solution)/shard_map/ppermute | solution.py:786
  73.4 22.0 %collective-permute-start.18 = (bf16[1,64,4096]{2,1,0:T(8,128)(2,1)}, bf16[1,64,4096]{2,1,0:T(8,128)(2,1)S(1)}, u32[]{:S(2)}, u32[]{:S(2)}) collective-permute-start(bf16[1,64,4096]{2,1,0:T(8,128)(2,1)} %get-tuple-element.237.refs_4_), channel_id=1, source_target_pairs={{0,8},{2,10},{4,12},{6,14},{8,0},{10,2},{12,4},{14,6},{16,24},{18,... | collective-permute-start | bytes 1572872 | tf_op jit(solution)/shard_map/ppermute | solution.py:786
  73.9 21.5 %collective-permute-start.19 = (bf16[1,256,1024]{2,1,0:T(8,128)(2,1)}, bf16[1,256,1024]{2,1,0:T(8,128)(2,1)S(1)}, u32[]{:S(2)}, u32[]{:S(2)}) collective-permute-start(bf16[1,256,1024]{2,1,0:T(8,128)(2,1)} %get-tuple-element.238.refs_6_), channel_id=1, source_target_pairs={{0,4},{2,6},{4,0},{6,2},{8,12},{10,14},{12,8},{14,10},{16,20},{18,... | collective-permute-start | bytes 1572872 | tf_op jit(solution)/shard_map/ppermute | solution.py:786
  75.4 20.0 %collective-permute-start.16 = (bf16[2,64,1024]{2,1,0:T(8,128)(2,1)}, bf16[2,64,1024]{2,1,0:T(8,128)(2,1)S(1)}, u32[]{:S(2)}, u32[]{:S(2)}) collective-permute-start(bf16[2,64,1024]{2,1,0:T(8,128)(2,1)} %get-tuple-element.235.refs_0_), channel_id=1, source_target_pairs={{0,8},{2,10},{4,12},{6,14},{8,0},{10,2},{12,4},{14,6},{16,24},{18,... | collective-permute-start | bytes 786440 | tf_op jit(solution)/shard_map/ppermute | solution.py:786
  77.0 18.4 %collective-permute-start.17 = (bf16[2,64,1024]{2,1,0:T(8,128)(2,1)}, bf16[2,64,1024]{2,1,0:T(8,128)(2,1)S(1)}, u32[]{:S(2)}, u32[]{:S(2)}) collective-permute-start(bf16[2,64,1024]{2,1,0:T(8,128)(2,1)} %get-tuple-element.236.refs_2_), channel_id=1, source_target_pairs={{0,4},{2,6},{4,0},{6,2},{8,12},{10,14},{12,8},{14,10},{16,20},{18,... | collective-permute-start | bytes 786440 | tf_op jit(solution)/shard_map/ppermute | solution.py:786
  98.5 36.5 %collective-permute-start.21 = (bf16[2,128,1024]{2,1,0:T(8,128)(2,1)S(1)}, bf16[2,128,1024]{2,1,0:T(8,128)(2,1)S(1)}, u32[]{:S(2)}, u32[]{:S(2)}) collective-permute-start(bf16[2,128,1024]{2,1,0:T(8,128)(2,1)S(1)} %bitcast_select_fusion.8.refs_2_), channel_id=1, source_target_pairs={{0,8},{2,10},{4,12},{6,14},{8,0},{10,2},{12,4},{14,6},{16,24},{18,... | collective-permute-start | bytes 1572872 | tf_op jit(solution)/shard_map/ppermute | solution.py:786
  100.2 34.8 %collective-permute-start.20 = (bf16[2,128,1024]{2,1,0:T(8,128)(2,1)S(1)}, bf16[2,128,1024]{2,1,0:T(8,128)(2,1)S(1)}, u32[]{:S(2)}, u32[]{:S(2)}) collective-permute-start(bf16[2,128,1024]{2,1,0:T(8,128)(2,1)S(1)} %bitcast_select_fusion.9.refs_0_), channel_id=1, source_target_pairs={{0,4},{2,6},{4,0},{6,2},{8,12},{10,14},{12,8},{14,10},{16,20},{18,... | collective-permute-start | bytes 1572872 | tf_op jit(solution)/shard_map/ppermute | solution.py:786
  103.4 49.3 %collective-permute-start.25 = (bf16[1,512,1024]{2,1,0:T(8,128)(2,1)S(1)}, bf16[1,512,1024]{2,1,0:T(8,128)(2,1)}, u32[]{:S(2)}, u32[]{:S(2)}) collective-permute-start(bf16[1,512,1024]{2,1,0:T(8,128)(2,1)S(1)} %bitcast_select_fusion.2.refs_2_), channel_id=1, source_target_pairs={{0,8},{2,10},{4,12},{6,14},{8,0},{10,2},{12,4},{14,6},{16,24},{18,... | collective-permute-start | bytes 3145736 | tf_op jit(solution)/shard_map/ppermute | solution.py:786
  139.9 25.1 %collective-permute-start.24 = (bf16[1,128,4096]{2,1,0:T(8,128)(2,1)S(1)}, bf16[1,128,4096]{2,1,0:T(8,128)(2,1)}, u32[]{:S(2)}, u32[]{:S(2)}) collective-permute-start(bf16[1,128,4096]{2,1,0:T(8,128)(2,1)S(1)} %bitcast_select_fusion.3.refs_0_), channel_id=1, source_target_pairs={{0,4},{2,6},{4,0},{6,2},{8,12},{10,14},{12,8},{14,10},{16,20},{18,... | collective-permute-start | bytes 3145736 | tf_op jit(solution)/shard_map/ppermute | solution.py:786
  195.1 14.4 %collective-permute-start.27 = (bf16[1,1024,1024]{2,1,0:T(8,128)(2,1)}, bf16[1,1024,1024]{2,1,0:T(8,128)(2,1)}, u32[]{:S(2)}, u32[]{:S(2)}) collective-permute-start(bf16[1,1024,1024]{2,1,0:T(8,128)(2,1)} %bitcast_select_fusion.refs_7_), channel_id=1, source_target_pairs={{0,2},{2,0},{4,6},{6,4},{8,10},{10,8},{12,14},{14,12},{16,18},{18,... | collective-permute-start | bytes 6291464 | tf_op jit(solution)/shard_map/ppermute | solution.py:786
  209.1 42.9 %collective-permute-start.29 = (bf16[2,2,2,3,64,512]{5,4,3,2,1,0:T(8,128)(2,1)}, bf16[2,2,2,3,64,512]{5,4,3,2,1,0:T(8,128)(2,1)S(1)}, u32[]{:S(2)}, u32[]{:S(2)}) collective-permute-start(bf16[2,2,2,3,64,512]{5,4,3,2,1,0:T(8,128)(2,1)} %bitcast.370), channel_id=1, source_target_pairs={{0,8},{2,10},{4,12},{6,14},{8,0},{10,2},{12,4},{14,6},{16,24},{18,... | collective-permute-start | bytes 4718600 | tf_op jit(solution)/shard_map/ppermute | solution.py:786
  257.2 16.8 %collective-permute-start.30 = (bf16[2,8,256,512]{3,2,1,0:T(8,128)(2,1)}, bf16[2,8,256,512]{3,2,1,0:T(8,128)(2,1)}, u32[]{:S(2)}, u32[]{:S(2)}) collective-permute-start(bf16[2,8,256,512]{3,2,1,0:T(8,128)(2,1)} %get-tuple-element.298), channel_id=1, source_target_pairs={{0,2},{2,0},{4,6},{6,4},{8,10},{10,8},{12,14},{14,12},{16,18},{18,... | collective-permute-start | bytes 12582920 | tf_op jit(solution)/shard_map/ppermute | solution.py:786
  257.2 16.7 %collective-permute-start.31 = (bf16[2,8,256,512]{3,2,1,0:T(8,128)(2,1)}, bf16[2,8,256,512]{3,2,1,0:T(8,128)(2,1)}, u32[]{:S(2)}, u32[]{:S(2)}) collective-permute-start(bf16[2,8,256,512]{3,2,1,0:T(8,128)(2,1)} %get-tuple-element.299), channel_id=1, source_target_pairs={{0,2},{2,0},{4,6},{6,4},{8,10},{10,8},{12,14},{14,12},{16,18},{18,... | collective-permute-start | bytes 12582920 | tf_op jit(solution)/shard_map/ppermute | solution.py:786
  284.4 50.6 %collective-permute-start.32 = (bf16[2,2,2,1,176,512]{5,4,3,2,1,0:T(8,128)(2,1)}, bf16[2,2,2,1,176,512]{5,4,3,2,1,0:T(8,128)(2,1)S(1)}, u32[]{:S(2)}, u32[]{:S(2)}) collective-permute-start(bf16[2,2,2,1,176,512]{5,4,3,2,1,0:T(8,128)(2,1)} %get-tuple-element.307), channel_id=1, source_target_pairs={{0,4},{2,6},{4,0},{6,2},{8,12},{10,14},{12,8},{14,10},{16,20},{18,... | collective-permute-start | bytes 4325384 | tf_op jit(solution)/shard_map/ppermute | solution.py:786
  285.0 50.1 %collective-permute-start.33 = (bf16[2,2,2,1,176,512]{5,4,2,1,0,3:T(8,128)(2,1)}, bf16[2,2,2,1,176,512]{5,4,2,1,0,3:T(8,128)(2,1)S(1)}, u32[]{:S(2)}, u32[]{:S(2)}) collective-permute-start(bf16[2,2,2,1,176,512]{5,4,2,1,0,3:T(8,128)(2,1)} %bitcast.371), channel_id=1, source_target_pairs={{0,1},{1,0},{2,3},{3,2},{4,5},{5,4},{6,7},{7,6},{8,9},{9,8},{10,11... | collective-permute-start | bytes 4325384 | tf_op jit(solution)/shard_map/ppermute | solution.py:785
  286.2 48.8 %collective-permute-start.34 = (bf16[2,2,2,1,160,512]{5,4,3,2,1,0:T(8,128)(2,1)}, bf16[2,2,2,1,160,512]{5,4,3,2,1,0:T(8,128)(2,1)}, u32[]{:S(2)}, u32[]{:S(2)}) collective-permute-start(bf16[2,2,2,1,160,512]{5,4,3,2,1,0:T(8,128)(2,1)} %get-tuple-element.311), channel_id=1, source_target_pairs={{0,8},{2,10},{4,12},{6,14},{8,0},{10,2},{12,4},{14,6},{16,24},{18,... | collective-permute-start | bytes 3932168 | tf_op jit(solution)/shard_map/ppermute | solution.py:786
  287.8 47.2 %collective-permute-start.35 = (bf16[2,2,3,64,512]{4,3,2,1,0:T(8,128)(2,1)}, bf16[2,2,3,64,512]{4,3,2,1,0:T(8,128)(2,1)S(1)}, u32[]{:S(2)}, u32[]{:S(2)}) collective-permute-start(bf16[2,2,3,64,512]{4,3,2,1,0:T(8,128)(2,1)} %bitcast.375), channel_id=1, source_target_pairs={{0,4},{2,6},{4,0},{6,2},{8,12},{10,14},{12,8},{14,10},{16,20},{18,... | collective-permute-start | bytes 2359304 | tf_op jit(solution)/shard_map/ppermute | solution.py:786
  344.2 28.6 %collective-permute-start.41 = (bf16[2,2,2,3,64,512]{5,4,3,2,1,0:T(8,128)(2,1)}, bf16[2,2,2,3,64,512]{5,4,3,2,1,0:T(8,128)(2,1)S(1)}, u32[]{:S(2)}, u32[]{:S(2)}) collective-permute-start(bf16[2,2,2,3,64,512]{5,4,3,2,1,0:T(8,128)(2,1)} %bitcast.300), channel_id=1, source_target_pairs={{0,2},{2,0},{4,6},{6,4},{8,10},{10,8},{12,14},{14,12},{16,18},{18,... | collective-permute-start | bytes 4718600 | tf_op jit(solution)/shard_map/ppermute | solution.py:786
  345.6 27.1 %collective-permute-start.40 = (bf16[2,2,2,2,64,512]{5,4,3,2,1,0:T(8,128)(2,1)}, bf16[2,2,2,2,64,512]{5,4,3,2,1,0:T(8,128)(2,1)S(1)}, u32[]{:S(2)}, u32[]{:S(2)}) collective-permute-start(bf16[2,2,2,2,64,512]{5,4,3,2,1,0:T(8,128)(2,1)} %bitcast.312), channel_id=1, source_target_pairs={{0,2},{2,0},{4,6},{6,4},{8,10},{10,8},{12,14},{14,12},{16,18},{18,... | collective-permute-start | bytes 3145736 | tf_op jit(solution)/shard_map/ppermute | solution.py:786
  345.8 26.9 %collective-permute-start.36 = (bf16[2,2,1,176,512]{4,3,2,1,0:T(8,128)(2,1)}, bf16[2,2,1,176,512]{4,3,2,1,0:T(8,128)(2,1)S(1)}, u32[]{:S(2)}, u32[]{:S(2)}) collective-permute-start(bf16[2,2,1,176,512]{4,3,2,1,0:T(8,128)(2,1)} %bitcast.378), channel_id=1, source_target_pairs={{0,1},{1,0},{2,3},{3,2},{4,5},{5,4},{6,7},{7,6},{8,9},{9,8},{10,11... | collective-permute-start | bytes 2162696 | tf_op jit(solution)/shard_map/ppermute | solution.py:785
  346.5 26.2 %collective-permute-start.37 = (bf16[2,2,1,176,512]{4,3,2,1,0:T(8,128)(2,1)}, bf16[2,2,1,176,512]{4,3,2,1,0:T(8,128)(2,1)S(1)}, u32[]{:S(2)}, u32[]{:S(2)}) collective-permute-start(bf16[2,2,1,176,512]{4,3,2,1,0:T(8,128)(2,1)} %bitcast.377), channel_id=1, source_target_pairs={{0,8},{2,10},{4,12},{6,14},{8,0},{10,2},{12,4},{14,6},{16,24},{18,... | collective-permute-start | bytes 2162696 | tf_op jit(solution)/shard_map/ppermute | solution.py:786
  356.5 16.2 %collective-permute-start.38 = (bf16[2,2,1,160,512]{4,3,1,0,2:T(8,128)(2,1)}, bf16[2,2,1,160,512]{4,3,1,0,2:T(8,128)(2,1)}, u32[]{:S(2)}, u32[]{:S(2)}) collective-permute-start(bf16[2,2,1,160,512]{4,3,1,0,2:T(8,128)(2,1)} %bitcast.379), channel_id=1, source_target_pairs={{0,4},{2,6},{4,0},{6,2},{8,12},{10,14},{12,8},{14,10},{16,20},{18,... | collective-permute-start | bytes 1966088 | tf_op jit(solution)/shard_map/ppermute | solution.py:786
  381.6 29.5 %collective-permute-start.48 = (bf16[2,2,2,3,64,512]{5,4,3,2,1,0:T(8,128)(2,1)}, bf16[2,2,2,3,64,512]{5,4,3,2,1,0:T(8,128)(2,1)S(1)}, u32[]{:S(2)}, u32[]{:S(2)}) collective-permute-start(bf16[2,2,2,3,64,512]{5,4,3,2,1,0:T(8,128)(2,1)} %bitcast.293), channel_id=1, source_target_pairs={{0,2},{2,0},{4,6},{6,4},{8,10},{10,8},{12,14},{14,12},{16,18},{18,... | collective-permute-start | bytes 4718600 | tf_op jit(solution)/shard_map/ppermute | solution.py:786
  382.9 28.2 %collective-permute-start.47 = (bf16[2,2,2,2,64,512]{5,4,3,2,1,0:T(8,128)(2,1)}, bf16[2,2,2,2,64,512]{5,4,3,2,1,0:T(8,128)(2,1)S(1)}, u32[]{:S(2)}, u32[]{:S(2)}) collective-permute-start(bf16[2,2,2,2,64,512]{5,4,3,2,1,0:T(8,128)(2,1)} %bitcast.313), channel_id=1, source_target_pairs={{0,2},{2,0},{4,6},{6,4},{8,10},{10,8},{12,14},{14,12},{16,18},{18,... | collective-permute-start | bytes 3145736 | tf_op jit(solution)/shard_map/ppermute | solution.py:786
  383.5 27.6 %collective-permute-start.46 = (bf16[2,2,3,64,512]{4,3,2,1,0:T(8,128)(2,1)}, bf16[2,2,3,64,512]{4,3,2,1,0:T(8,128)(2,1)S(1)}, u32[]{:S(2)}, u32[]{:S(2)}) collective-permute-start(bf16[2,2,3,64,512]{4,3,2,1,0:T(8,128)(2,1)} %bitcast.374), channel_id=1, source_target_pairs={{0,4},{2,6},{4,0},{6,2},{8,12},{10,14},{12,8},{14,10},{16,20},{18,... | collective-permute-start | bytes 2359304 | tf_op jit(solution)/shard_map/ppermute | solution.py:786
  393.8 17.3 %collective-permute-start.45 = (bf16[2,2,2,64,512]{4,3,2,1,0:T(8,128)(2,1)}, bf16[2,2,2,64,512]{4,3,2,1,0:T(8,128)(2,1)S(1)}, u32[]{:S(2)}, u32[]{:S(2)}) collective-permute-start(bf16[2,2,2,64,512]{4,3,2,1,0:T(8,128)(2,1)} %bitcast.380), channel_id=1, source_target_pairs={{0,8},{2,10},{4,12},{6,14},{8,0},{10,2},{12,4},{14,6},{16,24},{18,... | collective-permute-start | bytes 1572872 | tf_op jit(solution)/shard_map/ppermute | solution.py:786
  419.9 19.9 %collective-permute-start.53 = (bf16[2,2,3,64,512]{4,3,2,1,0:T(8,128)(2,1)}, bf16[2,2,3,64,512]{4,3,2,1,0:T(8,128)(2,1)S(1)}, u32[]{:S(2)}, u32[]{:S(2)}) collective-permute-start(bf16[2,2,3,64,512]{4,3,2,1,0:T(8,128)(2,1)} %bitcast.376), channel_id=1, source_target_pairs={{0,4},{2,6},{4,0},{6,2},{8,12},{10,14},{12,8},{14,10},{16,20},{18,... | collective-permute-start | bytes 2359304 | tf_op jit(solution)/shard_map/ppermute | solution.py:786
  420.5 19.3 %collective-permute-start.52 = (bf16[2,2,2,64,512]{4,3,2,1,0:T(8,128)(2,1)}, bf16[2,2,2,64,512]{4,3,2,1,0:T(8,128)(2,1)S(1)}, u32[]{:S(2)}, u32[]{:S(2)}) collective-permute-start(bf16[2,2,2,64,512]{4,3,2,1,0:T(8,128)(2,1)} %bitcast.381), channel_id=1, source_target_pairs={{0,1},{1,0},{2,3},{3,2},{4,5},{5,4},{6,7},{7,6},{8,9},{9,8},{10,11... | collective-permute-start | bytes 1572872 | tf_op jit(solution)/shard_map/ppermute | solution.py:785
  421.8 18.0 %collective-permute-start.51 = (bf16[2,3,64,512]{3,2,1,0:T(8,128)(2,1)}, bf16[2,3,64,512]{3,2,1,0:T(8,128)(2,1)S(1)}, u32[]{:S(2)}, u32[]{:S(2)}) collective-permute-start(bf16[2,3,64,512]{3,2,1,0:T(8,128)(2,1)} %get-tuple-element.363), channel_id=1, source_target_pairs={{0,8},{2,10},{4,12},{6,14},{8,0},{10,2},{12,4},{14,6},{16,24},{18,... | collective-permute-start | bytes 1179656 | tf_op jit(solution)/shard_map/ppermute | solution.py:786
  423.4 16.4 %collective-permute-start.50 = (bf16[2,2,64,512]{3,2,1,0:T(8,128)(2,1)}, bf16[2,2,64,512]{3,2,1,0:T(8,128)(2,1)S(1)}, u32[]{:S(2)}, u32[]{:S(2)}) collective-permute-start(bf16[2,2,64,512]{3,2,1,0:T(8,128)(2,1)} %bitcast.387), channel_id=1, source_target_pairs={{0,1},{1,0},{2,3},{3,2},{4,5},{5,4},{6,7},{7,6},{8,9},{9,8},{10,11... | collective-permute-start | bytes 786440 | tf_op jit(solution)/shard_map/ppermute | solution.py:785
  424.1 15.7 %collective-permute-start.54 = (f32[8,1024]{1,0:T(8,128)}, f32[8,1024]{1,0:T(8,128)S(1)}, u32[]{:S(2)}, u32[]{:S(2)}) collective-permute-start(f32[8,1024]{1,0:T(8,128)} %get-tuple-element.368.refs_8_), channel_id=1, source_target_pairs={{0,1},{1,0},{2,3},{3,2},{4,5},{5,4},{6,7},{7,6},{8,9},{9,8},{10,11... | collective-permute-start | bytes 98312 | tf_op jit(solution)/shard_map/ppermute | solution.py:785
  448.3 22.0 %collective-permute-start.63 = (bf16[3,64,512]{2,1,0:T(8,128)(2,1)}, bf16[3,64,512]{2,1,0:T(8,128)(2,1)}, u32[]{:S(2)}, u32[]{:S(2)}) collective-permute-start(bf16[3,64,512]{2,1,0:T(8,128)(2,1)} %bitcast.162), channel_id=1, source_target_pairs={{0,16},{2,18},{4,20},{6,22},{8,24},{10,26},{12,28},{14,30},{16,0},... | collective-permute-start | bytes 589832 | tf_op jit(solution)/shard_map/ppermute | solution.py:786
  452.4 28.2 %collective-permute-start.64 = (bf16[1,176,512]{2,1,0:T(8,128)(2,1)}, bf16[1,176,512]{2,1,0:T(8,128)(2,1)}, u32[]{:S(2)}, u32[]{:S(2)}) collective-permute-start(bf16[1,176,512]{2,1,0:T(8,128)(2,1)} %bitcast.164), channel_id=1, source_target_pairs={{0,16},{2,18},{4,20},{6,22},{8,24},{10,26},{12,28},{14,30},{16,0},... | collective-permute-start | bytes 540680 | tf_op jit(solution)/shard_map/ppermute | solution.py:786
  455.0 24.3 %collective-permute-start.66 = (bf16[1,160,512]{2,1,0:T(8,128)(2,1)}, bf16[1,160,512]{2,1,0:T(8,128)(2,1)}, u32[]{:S(2)}, u32[]{:S(2)}) collective-permute-start(bf16[1,160,512]{2,1,0:T(8,128)(2,1)} %bitcast.168), channel_id=1, source_target_pairs={{0,16},{2,18},{4,20},{6,22},{8,24},{10,26},{12,28},{14,30},{16,0},... | collective-permute-start | bytes 491528 | tf_op jit(solution)/shard_map/ppermute | solution.py:786
  457.0 24.3 %collective-permute-start.65 = (bf16[1,176,512]{2,1,0:T(8,128)(2,1)}, bf16[1,176,512]{2,1,0:T(8,128)(2,1)}, u32[]{:S(2)}, u32[]{:S(2)}) collective-permute-start(bf16[1,176,512]{2,1,0:T(8,128)(2,1)} %bitcast.166), channel_id=1, source_target_pairs={{0,16},{2,18},{4,20},{6,22},{8,24},{10,26},{12,28},{14,30},{16,0},... | collective-permute-start | bytes 540680 | tf_op jit(solution)/shard_map/ppermute | solution.py:786
  459.0 25.6 %collective-permute-start.60 = (bf16[3,64,512]{2,1,0:T(8,128)(2,1)}, bf16[3,64,512]{2,1,0:T(8,128)(2,1)}, u32[]{:S(2)}, u32[]{:S(2)}) collective-permute-start(bf16[3,64,512]{2,1,0:T(8,128)(2,1)} %bitcast.389), channel_id=1, source_target_pairs={{0,1},{1,0},{2,3},{3,2},{4,5},{5,4},{6,7},{7,6},{8,9},{9,8},{10,11... | collective-permute-start | bytes 589832 | tf_op jit(solution)/shard_map/ppermute | solution.py:785
  470.3 15.7 %collective-permute-start.61 = (bf16[3,64,512]{2,1,0:T(8,128)(2,1)}, bf16[3,64,512]{2,1,0:T(8,128)(2,1)S(1)}, u32[]{:S(2)}, u32[]{:S(2)}) collective-permute-start(bf16[3,64,512]{2,1,0:T(8,128)(2,1)} %bitcast.390), channel_id=1, source_target_pairs={{0,8},{2,10},{4,12},{6,14},{8,0},{10,2},{12,4},{14,6},{16,24},{18,... | collective-permute-start | bytes 589832 | tf_op jit(solution)/shard_map/ppermute | solution.py:786
  491.5 15.5 %collective-permute-start.68 = (bf16[3,64,512]{2,1,0:T(8,128)(2,1)}, bf16[3,64,512]{2,1,0:T(8,128)(2,1)}, u32[]{:S(2)}, u32[]{:S(2)}) collective-permute-start(bf16[3,64,512]{2,1,0:T(8,128)(2,1)} %get-tuple-element.397), channel_id=1, source_target_pairs={{0,16},{2,18},{4,20},{6,22},{8,24},{10,26},{12,28},{14,30},{16,0},... | collective-permute-start | bytes 589832 | tf_op jit(solution)/shard_map/ppermute | solution.py:786
  491.7 15.3 %collective-permute-start.67 = (bf16[2,64,512]{2,1,0:T(8,128)(2,1)}, bf16[2,64,512]{2,1,0:T(8,128)(2,1)S(1)}, u32[]{:S(2)}, u32[]{:S(2)}) collective-permute-start(bf16[2,64,512]{2,1,0:T(8,128)(2,1)} %get-tuple-element.395), channel_id=1, source_target_pairs={{0,16},{2,18},{4,20},{6,22},{8,24},{10,26},{12,28},{14,30},{16,0},... | collective-permute-start | bytes 393224 | tf_op jit(solution)/shard_map/ppermute | solution.py:786
  (106 other events, 656.4 us)
